TPU v7x, 32 devices: a whole 2x2x4 slice. The times are simulated.
32 devices in a mesh: row: 4 (over x, core), col: 4 (over z), tau: 2 (over y).
Axes of the slice: x: 2, y: 2, z: 4, core: 2. Of those that a mesh axis runs over, the one named last changes fastest.
Arguments:
- occ_states: bfloat16 [512, 512], P(('col', 'row')), may hold values from -0.25 to 0.25
- empty_states: bfloat16 [512, 4096], P(('col', 'row')), may hold values from -0.09375 to 0.09375
- mix_weights: float32 [4096, 16], replicated, may hold values from -4 to 4
- slice_of_block: int32 [128], replicated, may hold values from 0 to 23
- occ_energy: float32 [512], replicated, may hold values from -1.2 to -0.1
- pb_energy: float32 [384], replicated, may hold values from 0.1 to 2
- tau_points: float32 [6], P('tau'), may hold values from 0.05 to 2.5
- tau_weights: float32 [6], P('tau'), may hold values from 0.05 to 0.5
- trial: bfloat16 [512, 128], P(('col', 'row')), may hold values from -6 to 6
Outputs:
- trial_response: float32 [512, 128], P(('col', 'row'))
All inputs are finite; a program needn't handle non-finite values.
Results may differ from a plain program's by a relative error of at most 0.0018.
Values may be sent and summed in bfloat16 or wider, within the bound.
No kernel may reach another device: no remote copies, remote signals or barrier semaphores. Data moves between devices by JAX's collectives and lax.ppermute only.
A program may use at most 64 MiB of HBM per device.

v0:
```python
import jax
import jax.numpy as jnp
from jax import lax
from jax.sharding import PartitionSpec as P


def mixing_matrix(mix_weights, slice_of_block, nbands):
    per_slice = mix_weights.shape[1]
    state_slice = jnp.repeat(slice_of_block, mix_weights.shape[0] // slice_of_block.shape[0])
    band_slice = jnp.arange(nbands, dtype=jnp.int32) // per_slice
    picked = state_slice[:, None] == band_slice[None, :]
    spread_weights = jnp.tile(mix_weights, (1, nbands // per_slice))
    return jnp.where(picked, spread_weights, jnp.zeros_like(spread_weights)).astype(jnp.bfloat16)


def contract(left, right):
    return lax.dot_general(
        left, right, (((1,), (1,)), ((), ())), preferred_element_type=jnp.float32
    )


def scale_columns(cols_occ, cols_pb, occ_energy, pb_energy, tau_points):
    scaled = []
    for k in range(tau_points.shape[0]):
        time_point = tau_points[k]
        occ_scaled = (
            cols_occ.astype(jnp.float32) * jnp.exp(occ_energy * time_point)[None, :]
        ).astype(jnp.bfloat16)
        pb_scaled = (
            cols_pb.astype(jnp.float32) * jnp.exp(-pb_energy * time_point)[None, :]
        ).astype(jnp.bfloat16)
        scaled.append((occ_scaled, pb_scaled))
    return scaled


def apply_response(rows_occ, rows_pb, scaled, cols_trial, tau_weights):
    summed = None
    for k in range(len(scaled)):
        g_occ = contract(rows_occ, scaled[k][0])
        g_un = contract(rows_pb, scaled[k][1])
        chi_tile = (tau_weights[k] * g_occ * g_un).astype(jnp.bfloat16)
        product_term = jnp.dot(chi_tile, cols_trial, preferred_element_type=jnp.float32)
        summed = product_term if summed is None else summed + product_term
    return summed


def local(
    occ_states,
    empty_states,
    mix_weights,
    slice_of_block,
    occ_energy,
    pb_energy,
    tau_points,
    tau_weights,
    trial,
):
    band_mix = mixing_matrix(mix_weights, slice_of_block, pb_energy.shape[0])
    pseudo = jnp.dot(empty_states, band_mix, preferred_element_type=jnp.float32).astype(
        jnp.bfloat16
    )
    cols_occ, cols_pb, cols_trial = (
        lax.all_gather(occ_states, "row", axis=0, tiled=True),
        lax.all_gather(pseudo, "row", axis=0, tiled=True),
        lax.all_gather(trial, "row", axis=0, tiled=True),
    )
    column_scaled = scale_columns(cols_occ, cols_pb, occ_energy, pb_energy, tau_points)
    pieces = lax.all_gather((occ_states, pseudo), "col", axis=0, tiled=True)
    partial_value = apply_response(pieces[0], pieces[1], column_scaled, cols_trial, tau_weights)
    partial_value = lax.psum(partial_value, "tau")
    owned = lax.psum_scatter(partial_value, "col", scatter_dimension=0, tiled=True)
    return owned


def solution(mesh):
    in_specs = (
        P(("col", "row"), None),
        P(("col", "row"), None),
        P(),
        P(),
        P(),
        P(),
        P("tau"),
        P("tau"),
        P(("col", "row"), None),
    )
    out_specs = P(("col", "row"), None)
    return jax.shard_map(local, mesh=mesh, in_specs=in_specs, out_specs=out_specs, check_vma=False)
```

profile of v0, /device:TPU:0, one launch (start us, length us, event | category | flops | bytes accessed | tf_op | source)
XLA Modules:
  0.0 101.0 jit_solution(12969515031540765583)
XLA Ops:
  6.5 0.0 copy-start
  6.5 0.0 reduce-scatter.2.cloned.1.call-start
  6.5 15.4 %all_gather.16 = bf16[128,512]{1,0:T(8,128)(2,1)S(1)} all-gather(bf16[32,512]{1,0:T(8,128)(2,1)} %param.9), channel_id=1, replica_groups=mesh['row'=4,'col'=4,'tau'=2] {'col'}, dimensions={0}, use_global_device_ids=true | all-gather | bytes 163840 | tf_op jit(solution)/shard_map/all_gather | solution.py:68
  21.9 5.6 %all_gather.15 = bf16[128,512]{1,0:T(8,128)(2,1)S(1)} all-gather(bf16[32,512]{1,0:T(8,128)(2,1)} %param.9), channel_id=1, replica_groups=mesh['row'=4,'col'=4,'tau'=2] {'row'}, dimensions={0}, use_global_device_ids=true | all-gather | bytes 163840 | tf_op jit(solution)/shard_map/all_gather | solution.py:63
  27.6 0.7 broadcast_in_dim.4
  28.3 0.1 eq.15
  28.4 1.7 %fusion = bf16[4096,384]{0,1:T(8,128)(2,1)S(1)} fusion(f32[4096,16]{0,1:T(8,128)} %param.11, s32[4096]{0:T(1024)S(1)} %eq.15, s32[384]{0:T(512)S(1)} %add_select_fusion), kind=kLoop, calls=%fused_computation.1 | loop fusion | flops 3145728 | bytes 3425792 | tf_op jit(solution)/shard_map/convert_element_type | solution.py:13
  30.0 0.0 copy-done
  30.1 0.0 copy-start.2
  30.1 0.0 copy-start.3
  30.1 0.0 copy-start.4
  30.1 0.0 copy-start.5
  30.1 0.0 copy-start.1
  30.1 1.0 %fusion.8 = bf16[32,384]{1,0:T(8,128)(2,1)S(1)} fusion(bf16[4096,384]{0,1:T(8,128)(2,1)S(1)} %fusion, bf16[32,4096]{1,0:T(8,128)(2,1)S(1)} %copy-done), kind=kOutput, calls=%fused_computation.18 | convolution fusion | flops 100675584 | bytes 3432448 | tf_op jit(solution)/shard_map/dot_general | solution.py:59
  31.1 5.3 %all_gather.18 = bf16[128,384]{1,0:T(8,128)(2,1)S(1)} all-gather(bf16[32,384]{1,0:T(8,128)(2,1)S(1)} %fusion.8), channel_id=1, replica_groups=mesh['row'=4,'col'=4,'tau'=2] {'row'}, dimensions={0}, use_global_device_ids=true | all-gather | bytes 122880 | tf_op jit(solution)/shard_map/all_gather | solution.py:64
  36.5 13.3 %all_gather.17 = bf16[128,384]{1,0:T(8,128)(2,1)S(1)} all-gather(bf16[32,384]{1,0:T(8,128)(2,1)S(1)} %fusion.8), channel_id=1, replica_groups=mesh['row'=4,'col'=4,'tau'=2] {'col'}, dimensions={0}, use_global_device_ids=true | all-gather | bytes 122880 | tf_op jit(solution)/shard_map/all_gather | solution.py:68
  49.8 0.7 fusion.37
  50.5 0.6 fusion.36
  51.1 0.0 copy-done.4
  51.1 1.9 %multiply_exponential_fusion = (f32[384]{0:T(512)S(1)}, f32[384]{0:T(512)S(1)}, f32[384]{0:T(512)S(1)}) fusion(f32[384]{0:T(512)S(1)} %copy-done.4, f32[]{:T(128)} %bitcast.9, f32[]{:T(128)} %bitcast.6, f32[]{:T(128)} %bitcast.1), kind=kLoop, calls=%fused_computation.43 | loop fusion | flops 1536 | bytes 6156 | tf_op jit(solution)/shard_map/exp | solution.py:30
  53.0 1.9 %multiply_exponential_fusion.1 = (f32[512]{0:T(512)S(1)}, f32[512]{0:T(512)S(1)}, f32[512]{0:T(512)S(1)}) fusion(f32[512]{0:T(512)S(1)} %copy-done.5, f32[]{:T(128)} %bitcast.9, f32[]{:T(128)} %bitcast.1, f32[]{:T(128)} %bitcast.6), kind=kLoop, calls=%fused_computation.44 | loop fusion | flops 1536 | bytes 8204 | tf_op jit(solution)/shard_map/exp | solution.py:27
  54.9 0.0 copy-done.1
  54.9 5.2 %all_gather.19 = bf16[128,128]{1,0:T(8,128)(2,1)S(1)} all-gather(bf16[32,128]{1,0:T(8,128)(2,1)S(1)} %copy-done.1), channel_id=1, replica_groups=mesh['row'=4,'col'=4,'tau'=2] {'row'}, dimensions={0}, use_global_device_ids=true | all-gather | bytes 40960 | tf_op jit(solution)/shard_map/all_gather | solution.py:65
  60.1 0.8 fusion.2
  60.9 0.8 fusion.1
  61.8 0.8 fusion.3
  62.6 0.4 fusion.7
  62.9 0.4 convolution_add_fusion.1
  63.3 1.0 convolution_add_fusion
  64.3 0.0 reduce-scatter.2.cloned.1.call-update
  64.3 20.5 %reduce-scatter.2.cloned.1.call-done = f32[32,128]{1,0:T(8,128)} async-done(((f32[128,128]{1,0:T(8,128)}), f32[32,128]{1,0:T(8,128)}) %reduce-scatter.2.cloned.1.call-update) | async-done | bytes 16400 | tf_op jit(solution)/shard_map/reduce_scatter | solution.py:71
  84.8 9.3 %psum.8 = f32[32,128]{1,0:T(8,128)} all-reduce(f32[32,128]{1,0:T(8,128)} %reduce-scatter.2.cloned.1.call-done), channel_id=1, replica_groups=mesh['row'=4,'col'=4,'tau'=2] {'tau'}, use_global_device_ids=true, to_apply=%region_0.1 | all-reduce | flops 4096 | bytes 32768 | tf_op jit(solution)/shard_map/psum | solution.py:70
  (4 shorter events, 0.0 us)
Async XLA Ops:
  6.5 23.5 %copy-start = (bf16[32,4096]{1,0:T(8,128)(2,1)S(1)}, bf16[32,4096]{1,0:T(8,128)(2,1)}, u32[]{:S(2)}) copy-start(bf16[32,4096]{1,0:T(8,128)(2,1)} %param.10) | copy-start | bytes 786436
  6.5 78.3 %reduce-scatter.2.cloned.1.call-start = ((), (), s32[]{:S(2)}) async-start(), calls=%async_computation.1 | async-start | bytes 81920 | tf_op jit(solution)/shard_map/reduce_scatter | solution.py:71
  30.1 19.7 %copy-start.2 = (f32[3]{0:T(128)S(1)}, f32[3]{0:T(128)}, u32[]{:S(2)}) copy-start(f32[3]{0:T(128)} %param.15) | copy-start | bytes 40
  30.1 20.4 %copy-start.3 = (f32[3]{0:T(128)S(1)}, f32[3]{0:T(128)}, u32[]{:S(2)}) copy-start(f32[3]{0:T(128)} %param.16) | copy-start | bytes 40
  30.1 21.0 %copy-start.4 = (f32[384]{0:T(512)S(1)}, f32[384]{0:T(512)}, u32[]{:S(2)}) copy-start(f32[384]{0:T(512)} %param.14) | copy-start | bytes 4612
  30.1 22.9 %copy-start.5 = (f32[512]{0:T(512)S(1)}, f32[512]{0:T(512)}, u32[]{:S(2)}) copy-start(f32[512]{0:T(512)} %param.13) | copy-start | bytes 6148
  30.1 24.8 %copy-start.1 = (bf16[32,128]{1,0:T(8,128)(2,1)S(1)}, bf16[32,128]{1,0:T(8,128)(2,1)}, u32[]{:S(2)}) copy-start(bf16[32,128]{1,0:T(8,128)(2,1)} %param.17) | copy-start | bytes 24580
Sparse Core Ops, SparseCore 0:
  64.4 20.3 reduce-scatter.1
where the time goes:
time: 101 us
  blocking collectives  54.2 us (54%)
  waiting for transfers between devices  20.5 us (20%)
  between operations  13.5 us (13%)
  other arithmetic  5.45 us (5%)
  matrix products  5.16 us (5%)
  local copies, waits for them, and re-layouts  2.15 us (2%)
    all_gather x2, blocking collectives, local(): pieces = lax.all_gather((occ_states, pseudo), 'col', axis=0, tiled=True)  28.7 us
    reduce_scatter x1, waiting for transfers between devices, local(): lax.psum_scatter(partial_value, 'col', scatter_dimension=0, tiled=True)  20.5 us
    psum x1, blocking collectives, local(): partial_value = lax.psum(partial_value, 'tau')  9.33 us
    all_gather x1, blocking collectives, local(): lax.all_gather(occ_states, 'row', axis=0, tiled=True)  5.62 us
    all_gather x1, blocking collectives, local(): lax.all_gather(pseudo, 'row', axis=0, tiled=True)  5.34 us
    all_gather x1, blocking collectives, local(): lax.all_gather(trial, 'row', axis=0, tiled=True)  5.19 us
    dot_general x3, matrix products, contract(): lax.dot_general(left, right, (((1,), (1,)), ((), ())), preferred_element_...  2.43 us
  transfers between devices with their start and end apart: 1, of which 1 were waited for; matrix products, arithmetic and copies ran while one was open for 0% of the time, Pallas kernels for 0%

commit v1 on v0

v1 whole, which is shorter than its diff:
```python
import functools

import jax
import jax.numpy as jnp
from jax import lax
from jax.experimental import pallas as pl
from jax.experimental.pallas import tpu as pltpu
from jax.sharding import PartitionSpec as P

LANES = 128
VMEM = pl.BlockSpec(memory_space=pltpu.VMEM)
SMEM = pl.BlockSpec(memory_space=pltpu.SMEM)
PARAMS = pltpu.CompilerParams(vmem_limit_bytes=48 * 1024 * 1024)
NT = (((1,), (1,)), ((), ()))


def swap(block, axis, size, bit):
    return lax.ppermute(block, axis, [(i, i ^ bit) for i in range(size)])


def bits_of(size):
    return [1 << b for b in range(size.bit_length() - 1)]


def pack_kernel(slice_ref, tau_ref, weight_ref, mix_ref, empty_ref, occ_ref, trial_ref, packed_ref, times_ref, band_ref):
    nocc = occ_ref.shape[1]
    nbands, nempty = band_ref.shape
    per_slice = mix_ref.shape[0]
    width = nempty // slice_ref.shape[0]
    packed_ref[:, :nocc] = occ_ref[...]
    packed_ref[:, nocc + nbands :] = trial_ref[...]
    ntau = tau_ref.shape[0]
    for k in range(ntau):
        times_ref[k : k + 1, :] = jnp.full((1, LANES), tau_ref[k], jnp.float32)
        times_ref[ntau + k : ntau + k + 1, :] = jnp.full((1, LANES), weight_ref[k], jnp.float32)
    lane = lax.broadcasted_iota(jnp.int32, (per_slice, LANES), 1) // width
    per_chunk = LANES // width
    for chunk in range(nempty // LANES):
        at = slice(chunk * LANES, (chunk + 1) * LANES)
        state_slice = jnp.full((per_slice, LANES), slice_ref[chunk * per_chunk], jnp.int32)
        for b in range(1, per_chunk):
            state_slice = jnp.where(lane == b, slice_ref[chunk * per_chunk + b], state_slice)
        state_slice = state_slice.astype(jnp.float32).astype(jnp.bfloat16)
        mix = mix_ref[:, at].astype(jnp.bfloat16)
        for s in range(nbands // per_slice):
            band_ref[s * per_slice : (s + 1) * per_slice, at] = jnp.where(
                state_slice == jnp.bfloat16(s), mix, jnp.zeros_like(mix)
            )
    pseudo = lax.dot_general(empty_ref[...], band_ref[...], NT, preferred_element_type=jnp.float32)
    packed_ref[:, nocc : nocc + nbands] = pseudo.astype(jnp.bfloat16)


def respond(scaled_ref, weight_of, nocc, npb, cols_ref, ntau, rows):
    cols = cols_ref[...]
    g_occ = lax.dot_general(scaled_ref[:, :nocc], cols[:, :nocc], NT, preferred_element_type=jnp.float32)
    g_un = lax.dot_general(scaled_ref[:, nocc:], cols[:, nocc : nocc + npb], NT, preferred_element_type=jnp.float32)
    trial = cols[:, nocc + npb :]
    total = None
    for k in range(ntau):
        at = slice(k * rows, (k + 1) * rows)
        chi = (weight_of(k) * g_occ[at] * g_un[at]).astype(jnp.bfloat16)
        term = jnp.dot(chi, trial, preferred_element_type=jnp.float32)
        total = term if total is None else total + term
    return total


def first_kernel(nocc, npb, nplanes, ntau, *refs):
    own_ref, far_ref, times_ref, occ_energy_ref, pb_energy_ref = refs[:5]
    cols_refs = refs[5:-3]
    scaled_ref, weights_ref, total_ref = refs[-3:]
    rows = own_ref.shape[0]
    plane_rows = times_ref.shape[0] // nplanes
    for plane in range(nplanes):
        for k in range(ntau):
            point = times_ref[plane * plane_rows + k : plane * plane_rows + k + 1, 0:1]
            gain_occ = jnp.exp(occ_energy_ref[...] * point)
            gain_pb = jnp.exp(-pb_energy_ref[...] * point)
            at = plane * ntau + k
            weights_ref[at : at + 1, :] = times_ref[plane * plane_rows + ntau + k : plane * plane_rows + ntau + k + 1, :]
            for j, ref in enumerate((own_ref, far_ref)):
                to = slice((2 * at + j) * rows, (2 * at + j + 1) * rows)
                scaled_ref[to, :nocc] = (ref[:, :nocc].astype(jnp.float32) * gain_occ).astype(jnp.bfloat16)
                scaled_ref[to, nocc:] = (ref[:, nocc : nocc + npb].astype(jnp.float32) * gain_pb).astype(jnp.bfloat16)
    weight_of = lambda k: weights_ref[k : k + 1, 0:1]
    total = None
    for ref in cols_refs:
        term = respond(scaled_ref, weight_of, nocc, npb, ref, nplanes * ntau, 2 * rows)
        total = term if total is None else total + term
    total_ref[...] = total


def next_kernel(nocc, npb, ntau, scaled_ref, weights_ref, before_ref, cols_ref, total_ref):
    weight_of = lambda k: weights_ref[k : k + 1, 0:1]
    total_ref[...] = before_ref[...] + respond(
        scaled_ref, weight_of, nocc, npb, cols_ref, ntau, before_ref.shape[0]
    )


def local(sizes, occ_states, empty_states, mix_weights, slice_of_block, occ_energy, pb_energy, tau_points, tau_weights, trial):
    nrow, ncol, nplanes = sizes
    rows, nocc = occ_states.shape
    npb, nv = pb_energy.shape[0], trial.shape[1]
    ntau = tau_points.shape[0]
    plane_rows = -(-2 * ntau // 8) * 8
    width = nocc + npb + nv

    own, times = pl.pallas_call(
        pack_kernel,
        out_shape=(
            jax.ShapeDtypeStruct((rows, width), jnp.bfloat16),
            jax.ShapeDtypeStruct((plane_rows, LANES), jnp.float32),
        ),
        in_specs=[SMEM, SMEM, SMEM, VMEM, VMEM, VMEM, VMEM],
        out_specs=(VMEM, VMEM),
        scratch_shapes=[pltpu.VMEM((npb, empty_states.shape[1]), jnp.bfloat16)],
        compiler_params=PARAMS,
        name="pack",
    )(slice_of_block, tau_points, tau_weights, mix_weights.T, empty_states, occ_states, trial)

    col_bits, row_bits = bits_of(ncol), bits_of(nrow)
    near_bits, far_bit = col_bits[:-1], col_bits[-1]
    held = own
    for bit in near_bits:
        held = jnp.concatenate([held, swap(held, "col", ncol, bit)])
    far = swap(own, "col", ncol, far_bit)
    pieces = [held]
    for bit in row_bits[1:]:
        sent = pieces[0] if len(pieces) == 1 else jnp.concatenate(pieces)
        pieces.append(swap(sent, "row", nrow, bit))
    for bit in bits_of(nplanes):
        times = jnp.concatenate([times, swap(times, "tau", nplanes, bit)])
    paired = [swap(piece, "row", nrow, row_bits[0]) for piece in pieces]

    all_tau = nplanes * ntau
    scaled, weights, total = pl.pallas_call(
        functools.partial(first_kernel, nocc, npb, nplanes, ntau),
        out_shape=(
            jax.ShapeDtypeStruct((all_tau * 2 * rows, nocc + npb), jnp.bfloat16),
            jax.ShapeDtypeStruct((-(-all_tau // 8) * 8, LANES), jnp.float32),
            jax.ShapeDtypeStruct((2 * rows, nv), jnp.float32),
        ),
        in_specs=[VMEM] * 7,
        out_specs=(VMEM, VMEM, VMEM),
        compiler_params=PARAMS,
        name="first",
    )(own, far, times, occ_energy[None, :], pb_energy[None, :], pieces[0], paired[0])
    for piece in [p for pair in zip(pieces[1:], paired[1:]) for p in pair]:
        total = pl.pallas_call(
            functools.partial(next_kernel, nocc, npb, all_tau),
            out_shape=jax.ShapeDtypeStruct((2 * rows, nv), jnp.float32),
            in_specs=[VMEM] * 4,
            out_specs=VMEM,
            compiler_params=PARAMS,
            name="next",
        )(scaled, weights, total, piece)
    return total[:rows] + swap(total[rows:], "col", ncol, far_bit)


def solution(mesh):
    points = P(("col", "row"), None)
    in_specs = (points, points, P(), P(), P(), P(), P("tau"), P("tau"), points)
    sizes = tuple(mesh.shape[axis] for axis in ("row", "col", "tau"))
    return jax.shard_map(
        functools.partial(local, sizes), mesh=mesh, in_specs=in_specs, out_specs=points, check_vma=False
    )
```

time: 101 us -> 32.1 us (0.32)
  blocking collectives: 54.2 us -> 0 us
  between operations: 13.5 us -> 0.05 us
  starting transfers between devices: 0.01 us -> 10.9 us
  waiting for transfers between devices: 20.5 us -> 12.7 us
  matrix products: 5.16 us -> 0 us
  other arithmetic: 5.45 us -> 0.61 us
  Pallas kernels: 0 us -> 3.43 us
  local copies, waits for them, and re-layouts: 2.15 us -> 4.07 us
    all_gather x5 -> x0, blocking collectives: 44.9 us -> none  [the longest x2 28.7 us: local(): pieces = lax.all_gather((occ_states, pseudo), 'col', axis=0, tiled=True)]
    reduce_scatter x1 -> x0, waiting for transfers between devices: 20.5 us -> none  [local(): lax.psum_scatter(partial_value, 'col', scatter_dimension=0, tiled=True)]
    ppermute x0 -> x7, waiting for transfers between devices: none -> 12.7 us  [swap(): return lax.ppermute(block, axis, [(i, i ^ bit) for i in range(size)])]
    ppermute x0 -> x7, starting transfers between devices: none -> 10.9 us  [swap(): return lax.ppermute(block, axis, [(i, i ^ bit) for i in range(size)])]
    psum x1 -> x0, blocking collectives: 9.33 us -> none  [local(): partial_value = lax.psum(partial_value, 'tau')]
    dot_general x7 -> x0, matrix products: 5.16 us -> none  [the longest x3 2.43 us: contract(): lax.dot_general(left, right, (((1,), (1,)), ((), ())), preferred_element_...]
    unnamed x12 -> x19, local copies, waits for them, and re-layouts: 0.04 us -> 4.05 us
    exp x2 -> x0, other arithmetic: 3.78 us -> none  [the longest x1 1.89 us: scale_columns(): jnp.exp(occ_energy * time_point)[None, :]]
  transfers between devices with their start and end apart: 1 -> 7, of which waited for: 1 -> 4; matrix products, arithmetic and copies ran while one was open for 0% -> 0% of each run, Pallas kernels for 0% -> 4%
where the time goes in v1:
time: 32.1 us; the launch traced here: 31.8 us
  waiting for transfers between devices  12.7 us (40%)
  starting transfers between devices  10.9 us (34%)
  local copies, waits for them, and re-layouts  4.07 us (13%)
  Pallas kernels  3.43 us (11%)
  other arithmetic  0.61 us (2%)
    ppermute x7, waiting for transfers between devices, swap(): return lax.ppermute(block, axis, [(i, i ^ bit) for i in range(size)])  12.7 us
    ppermute x7, starting transfers between devices, swap(): return lax.ppermute(block, axis, [(i, i ^ bit) for i in range(size)])  10.9 us
    unnamed x19, local copies, waits for them, and re-layouts  4.05 us
    pallas_call x1, Pallas kernels, local(): pl.pallas_call(pack_kernel, out_shape=(jax.ShapeDtypeStruct((rows, width)...  1.61 us
    pallas_call x2, Pallas kernels, local(): pl.pallas_call(functools.partial(next_kernel, nocc, npb, all_tau), out_sh...  0.97 us
    pallas_call x1, Pallas kernels, local(): pl.pallas_call(functools.partial(first_kernel, nocc, npb, nplanes, ntau),...  0.85 us
  transfers between devices with their start and end apart: 7, of which 4 were waited for; matrix products, arithmetic and copies ran while one was open for 0% of the time, Pallas kernels for 4%

profile of v1, /device:TPU:0, one launch (start us, length us, event | category | flops | bytes accessed | tf_op | source)
XLA Modules:
  0.0 31.8 jit_solution(17217781724052535070)
XLA Ops:
  0.0 0.0 copy-start.5
  0.0 0.0 copy-start.6
  0.0 0.0 copy-start.7
  0.0 0.6 %copy-done.5 = s32[128]{0:T(128)S(1)} copy-done((s32[128]{0:T(128)S(1)}, s32[128]{0:T(128)}, u32[]{:S(2)}) %copy-start.5) | copy-done | bytes 536
  0.7 0.0 copy-done.6
  0.7 0.0 copy-done.7
  0.7 0.9 %copy-done = f32[4096,16]{0,1:T(8,128)S(1)} copy-done((f32[4096,16]{0,1:T(8,128)S(1)}, f32[4096,16]{0,1:T(8,128)}, u32[]{:S(2)}) %copy-start) | copy-done | bytes 262168
  1.6 0.9 %copy-done.1 = bf16[32,4096]{1,0:T(8,128)(2,1)S(1)} copy-done((bf16[32,4096]{1,0:T(8,128)(2,1)S(1)}, bf16[32,4096]{1,0:T(8,128)(2,1)}, u32[]{:S(2)}) %copy-start.1) | copy-done | bytes 262168
  2.6 0.8 %copy-done.2 = bf16[32,512]{1,0:T(8,128)(2,1)S(1)} copy-done((bf16[32,512]{1,0:T(8,128)(2,1)S(1)}, bf16[32,512]{1,0:T(8,128)(2,1)}, u32[]{:S(2)}) %copy-start.2) | copy-done | bytes 32792
  3.3 0.7 %copy-done.3 = bf16[32,128]{1,0:T(8,128)(2,1)S(1)} copy-done((bf16[32,128]{1,0:T(8,128)(2,1)S(1)}, bf16[32,128]{1,0:T(8,128)(2,1)}, u32[]{:S(2)}) %copy-start.3) | copy-done | bytes 8216
  4.0 1.6 %pack.1 = (bf16[32,1024]{1,0:T(8,128)(2,1)S(1)}, f32[8,128]{1,0:T(8,128)S(1)}) custom-call(s32[128]{0:T(128)S(1)} %copy-done.5, f32[3]{0:T(128)S(1)} %copy-done.6, f32[3]{0:T(128)S(1)} %copy-done.7, f32[16,4096]{1,0:T(8,128)S(1)} %bitcast.2, bf16[32,4096]{1,0:T(8,128)(2,1)S(1)} %copy-done.1, bf16[32,512]{1,0:T(8,128)(2,1)S(1)} %copy-done.2, ...), custom_call_target="tpu_custom_call" | custom-call | tf_op jit(solution)/shard_map/pack/pallas_call | solution.py:107
  5.7 3.1 %collective-permute-start.2 = (bf16[32,1024]{1,0:T(8,128)(2,1)S(1)}, bf16[32,1024]{1,0:T(8,128)(2,1)S(1)}, u32[]{:S(2)}, u32[]{:S(2)}) collective-permute-start(bf16[32,1024]{1,0:T(8,128)(2,1)S(1)} %get-tuple-element.10.refs_0_), channel_id=1, source_target_pairs={{0,2},{2,0},{4,6},{6,4},{1,3},{3,1},{5,7},{7,5},{8,10},{10,8},{12,... | collective-permute-start | bytes 196616 | tf_op jit(solution)/shard_map/ppermute | solution.py:18
  8.8 2.2 %collective-permute-done.2 = bf16[32,1024]{1,0:T(8,128)(2,1)S(1)} collective-permute-done((bf16[32,1024]{1,0:T(8,128)(2,1)S(1)}, bf16[32,1024]{1,0:T(8,128)(2,1)S(1)}, u32[]{:S(2)}, u32[]{:S(2)}) %collective-permute-start.2) | collective-permute-done | bytes 65568 | tf_op jit(solution)/shard_map/ppermute | solution.py:18
  11.0 2.0 %collective-permute-start.4 = (bf16[64,1024]{1,0:T(8,128)(2,1)S(1)}, bf16[64,1024]{1,0:T(8,128)(2,1)S(1)}, u32[]{:S(2)}, u32[]{:S(2)}) collective-permute-start(bf16[64,1024]{1,0:T(8,128)(2,1)S(1)} %constant_dynamic-update-slice_fusion.refs_5_), channel_id=1, source_target_pairs={{0,16},{8,24},{16,0},{24,8},{1,17},{9,25},{17,1},{25,9},{2,18},{10... | collective-permute-start | bytes 393224 | tf_op jit(solution)/shard_map/ppermute | solution.py:18
  13.0 0.0 collective-permute-start.3
  13.0 3.0 %collective-permute-done.4.cols_ref = bf16[64,1024]{1,0:T(8,128)(2,1)S(1)} collective-permute-done((bf16[64,1024]{1,0:T(8,128)(2,1)S(1)}, bf16[64,1024]{1,0:T(8,128)(2,1)S(1)}, u32[]{:S(2)}, u32[]{:S(2)}) %collective-permute-start.4) | collective-permute-done | bytes 131104 | tf_op jit(solution)/shard_map/ppermute | solution.py:18
  16.0 0.0 collective-permute-start.5
  16.0 2.0 %collective-permute-start.1 = (f32[8,128]{1,0:T(8,128)S(1)}, f32[8,128]{1,0:T(8,128)S(1)}, u32[]{:S(2)}, u32[]{:S(2)}) collective-permute-start(f32[8,128]{1,0:T(8,128)S(1)} %get-tuple-element.11), channel_id=1, source_target_pairs={{0,1},{1,0},{2,3},{3,2},{4,5},{5,4},{6,7},{7,6},{8,9},{9,8},{10,11... | collective-permute-start | bytes 12296 | tf_op jit(solution)/shard_map/ppermute | solution.py:18
  18.0 2.6 %collective-permute-start = (bf16[32,1024]{1,0:T(8,128)(2,1)S(1)}, bf16[32,1024]{1,0:T(8,128)(2,1)S(1)}, u32[]{:S(2)}, u32[]{:S(2)}) collective-permute-start(bf16[32,1024]{1,0:T(8,128)(2,1)S(1)} %get-tuple-element.10.refs_0_), channel_id=1, source_target_pairs={{0,4},{2,6},{4,0},{6,2},{1,5},{3,7},{5,1},{7,3},{8,12},{10,14},{12... | collective-permute-start | bytes 196616 | tf_op jit(solution)/shard_map/ppermute | solution.py:18
  20.6 0.0 copy-done.8
  20.6 0.0 collective-permute-done.1
  20.6 0.0 copy-start.4
  20.6 3.9 %collective-permute-done.refs_1_ = bf16[32,1024]{1,0:T(8,128)(2,1)S(1)} collective-permute-done((bf16[32,1024]{1,0:T(8,128)(2,1)S(1)}, bf16[32,1024]{1,0:T(8,128)(2,1)S(1)}, u32[]{:S(2)}, u32[]{:S(2)}) %collective-permute-start) | collective-permute-done | bytes 65568 | tf_op jit(solution)/shard_map/ppermute | solution.py:18
  24.6 0.0 collective-permute-done.3.refs_6_
  24.6 0.0 copy-done.4
  24.6 0.9 %first.1 = (bf16[384,896]{1,0:T(8,128)(2,1)S(1)}, f32[8,128]{1,0:T(8,128)S(1)}, f32[64,128]{1,0:T(8,128)S(1)}) custom-call(bf16[32,1024]{1,0:T(8,128)(2,1)S(1)} %get-tuple-element.10.refs_0_, bf16[32,1024]{1,0:T(8,128)(2,1)S(1)} %collective-permute-done.refs_1_, f32[16,128]{1,0:T(8,128)S(1)} %pad_maximum_fusion.refs_2_, f32[1,512]{1,0:T(1,128)S(1)} %bitcast.3, ...), custom_call_target="tpu_custom_call" | custom-call | tf_op jit(solution)/shard_map/first/pallas_call | solution.py:135
  25.4 0.5 %next.2.before_ref = f32[64,128]{1,0:T(8,128)S(1)} custom-call(bf16[384,896]{1,0:T(8,128)(2,1)S(1)} %get-tuple-element.12.scaled_ref, f32[8,128]{1,0:T(8,128)S(1)} %get-tuple-element.13.weights_ref, f32[64,128]{1,0:T(8,128)S(1)} %get-tuple-element.14.before_ref, bf16[64,1024]{1,0:T(8,128)(2,1)S(1)} %collective-permute-done.4.cols_ref), custom_call_target="tpu_custom_call" | custom-call | tf_op jit(solution)/shard_map/next/pallas_call | solution.py:148
  25.9 0.0 collective-permute-done.5.cols_ref
  25.9 0.5 %next.3 = f32[64,128]{1,0:T(8,128)S(1)} custom-call(bf16[384,896]{1,0:T(8,128)(2,1)S(1)} %get-tuple-element.12.scaled_ref, f32[8,128]{1,0:T(8,128)S(1)} %get-tuple-element.13.weights_ref, f32[64,128]{1,0:T(8,128)S(1)} %next.2.before_ref, bf16[64,1024]{1,0:T(8,128)(2,1)S(1)} %collective-permute-done.5.cols_ref), custom_call_target="tpu_custom_call" | custom-call | tf_op jit(solution)/shard_map/next/pallas_call | solution.py:148
  26.4 1.3 %collective-permute-start.6 = (f32[32,128]{1,0:T(8,128)S(1)}, f32[32,128]{1,0:T(8,128)S(1)}, u32[]{:S(2)}, u32[]{:S(2)}) collective-permute-start(f32[32,128]{1,0:T(8,128)S(1)} %slice.9), channel_id=1, source_target_pairs={{0,4},{2,6},{4,0},{6,2},{1,5},{3,7},{5,1},{7,3},{8,12},{10,14},{12... | collective-permute-start | bytes 49160 | tf_op jit(solution)/shard_map/ppermute | solution.py:18
  27.7 3.5 %collective-permute-done.6 = f32[32,128]{1,0:T(8,128)S(1)} collective-permute-done((f32[32,128]{1,0:T(8,128)S(1)}, f32[32,128]{1,0:T(8,128)S(1)}, u32[]{:S(2)}, u32[]{:S(2)}) %collective-permute-start.6) | collective-permute-done | bytes 16416 | tf_op jit(solution)/shard_map/ppermute | solution.py:18
  31.2 0.6 %slice_add_fusion = f32[32,128]{1,0:T(8,128)} fusion(f32[32,128]{1,0:T(8,128)S(1)} %collective-permute-done.6, f32[64,128]{1,0:T(8,128)S(1)} %next.3), kind=kLoop, calls=%fused_computation | loop fusion | flops 4096 | bytes 49152 | tf_op jit(solution)/shard_map/add | solution.py:156
  (10 shorter events, 0.0 us)
Async XLA Ops:
  0.0 0.7 %copy-start.5 = (s32[128]{0:T(128)S(1)}, s32[128]{0:T(128)}, u32[]{:S(2)}) copy-start(s32[128]{0:T(128)} %slice_ref.1) | copy-start | bytes 1540
  0.0 0.7 %copy-start.6 = (f32[3]{0:T(128)S(1)}, f32[3]{0:T(128)}, u32[]{:S(2)}) copy-start(f32[3]{0:T(128)} %tau_ref.1) | copy-start | bytes 40
  0.0 0.7 %copy-start.7 = (f32[3]{0:T(128)S(1)}, f32[3]{0:T(128)}, u32[]{:S(2)}) copy-start(f32[3]{0:T(128)} %weight_ref.1) | copy-start | bytes 40
  0.7 0.9 %copy-start = (f32[4096,16]{0,1:T(8,128)S(1)}, f32[4096,16]{0,1:T(8,128)}, u32[]{:S(2)}) copy-start(f32[4096,16]{0,1:T(8,128)} %param.11) | copy-start | bytes 786436
  1.6 0.9 %copy-start.1 = (bf16[32,4096]{1,0:T(8,128)(2,1)S(1)}, bf16[32,4096]{1,0:T(8,128)(2,1)}, u32[]{:S(2)}) copy-start(bf16[32,4096]{1,0:T(8,128)(2,1)} %empty_ref.1) | copy-start | bytes 786436
  2.6 0.8 %copy-start.2 = (bf16[32,512]{1,0:T(8,128)(2,1)S(1)}, bf16[32,512]{1,0:T(8,128)(2,1)}, u32[]{:S(2)}) copy-start(bf16[32,512]{1,0:T(8,128)(2,1)} %occ_ref.1) | copy-start | bytes 98308
  3.3 0.7 %copy-start.3 = (bf16[32,128]{1,0:T(8,128)(2,1)S(1)}, bf16[32,128]{1,0:T(8,128)(2,1)}, u32[]{:S(2)}) copy-start(bf16[32,128]{1,0:T(8,128)(2,1)} %trial_ref.1) | copy-start | bytes 24580
  5.7 5.3 %collective-permute-start.2 = (bf16[32,1024]{1,0:T(8,128)(2,1)S(1)}, bf16[32,1024]{1,0:T(8,128)(2,1)S(1)}, u32[]{:S(2)}, u32[]{:S(2)}) collective-permute-start(bf16[32,1024]{1,0:T(8,128)(2,1)S(1)} %get-tuple-element.10.refs_0_), channel_id=1, source_target_pairs={{0,2},{2,0},{4,6},{6,4},{1,3},{3,1},{5,7},{7,5},{8,10},{10,8},{12,... | collective-permute-start | bytes 196616 | tf_op jit(solution)/shard_map/ppermute | solution.py:18
  11.0 9.6 %copy-start.8 = (f32[384]{0:T(512)S(1)}, f32[384]{0:T(512)}, u32[]{:S(2)}) copy-start(f32[384]{0:T(512)} %param.14) | copy-start | bytes 4612
  11.0 5.0 %collective-permute-start.4 = (bf16[64,1024]{1,0:T(8,128)(2,1)S(1)}, bf16[64,1024]{1,0:T(8,128)(2,1)S(1)}, u32[]{:S(2)}, u32[]{:S(2)}) collective-permute-start(bf16[64,1024]{1,0:T(8,128)(2,1)S(1)} %constant_dynamic-update-slice_fusion.refs_5_), channel_id=1, source_target_pairs={{0,16},{8,24},{16,0},{24,8},{1,17},{9,25},{17,1},{25,9},{2,18},{10... | collective-permute-start | bytes 393224 | tf_op jit(solution)/shard_map/ppermute | solution.py:18
  13.0 11.6 %collective-permute-start.3 = (bf16[64,1024]{1,0:T(8,128)(2,1)S(1)}, bf16[64,1024]{1,0:T(8,128)(2,1)S(1)}, u32[]{:S(2)}, u32[]{:S(2)}) collective-permute-start(bf16[64,1024]{1,0:T(8,128)(2,1)S(1)} %constant_dynamic-update-slice_fusion.refs_5_), channel_id=1, source_target_pairs={{0,8},{8,0},{16,24},{24,16},{1,9},{9,1},{17,25},{25,17},{2,10},{10... | collective-permute-start | bytes 393224 | tf_op jit(solution)/shard_map/ppermute | solution.py:18
  16.0 9.9 %collective-permute-start.5 = (bf16[64,1024]{1,0:T(8,128)(2,1)S(1)}, bf16[64,1024]{1,0:T(8,128)(2,1)S(1)}, u32[]{:S(2)}, u32[]{:S(2)}) collective-permute-start(bf16[64,1024]{1,0:T(8,128)(2,1)S(1)} %collective-permute-done.4.cols_ref), channel_id=1, source_target_pairs={{0,8},{8,0},{16,24},{24,16},{1,9},{9,1},{17,25},{25,17},{2,10},{10... | collective-permute-start | bytes 393224 | tf_op jit(solution)/shard_map/ppermute | solution.py:18
  16.0 4.6 %collective-permute-start.1 = (f32[8,128]{1,0:T(8,128)S(1)}, f32[8,128]{1,0:T(8,128)S(1)}, u32[]{:S(2)}, u32[]{:S(2)}) collective-permute-start(f32[8,128]{1,0:T(8,128)S(1)} %get-tuple-element.11), channel_id=1, source_target_pairs={{0,1},{1,0},{2,3},{3,2},{4,5},{5,4},{6,7},{7,6},{8,9},{9,8},{10,11... | collective-permute-start | bytes 12296 | tf_op jit(solution)/shard_map/ppermute | solution.py:18
  18.0 6.6 %collective-permute-start = (bf16[32,1024]{1,0:T(8,128)(2,1)S(1)}, bf16[32,1024]{1,0:T(8,128)(2,1)S(1)}, u32[]{:S(2)}, u32[]{:S(2)}) collective-permute-start(bf16[32,1024]{1,0:T(8,128)(2,1)S(1)} %get-tuple-element.10.refs_0_), channel_id=1, source_target_pairs={{0,4},{2,6},{4,0},{6,2},{1,5},{3,7},{5,1},{7,3},{8,12},{10,14},{12... | collective-permute-start | bytes 196616 | tf_op jit(solution)/shard_map/ppermute | solution.py:18
  20.6 4.0 %copy-start.4 = (f32[512]{0:T(512)S(1)}, f32[512]{0:T(512)}, u32[]{:S(2)}) copy-start(f32[512]{0:T(512)} %param.13) | copy-start | bytes 6148
  26.4 4.8 %collective-permute-start.6 = (f32[32,128]{1,0:T(8,128)S(1)}, f32[32,128]{1,0:T(8,128)S(1)}, u32[]{:S(2)}, u32[]{:S(2)}) collective-permute-start(f32[32,128]{1,0:T(8,128)S(1)} %slice.9), channel_id=1, source_target_pairs={{0,4},{2,6},{4,0},{6,2},{1,5},{3,7},{5,1},{7,3},{8,12},{10,14},{12... | collective-permute-start | bytes 49160 | tf_op jit(solution)/shard_map/ppermute | solution.py:18

commit v2 on v1

v2 whole, which is shorter than its diff:
```python
import functools

import jax
import jax.numpy as jnp
from jax import lax
from jax.experimental import pallas as pl
from jax.experimental.pallas import tpu as pltpu
from jax.sharding import PartitionSpec as P

LANES = 128
FIRST_COST = 10**9
VMEM = pl.BlockSpec(memory_space=pltpu.VMEM)
PARAMS = pltpu.CompilerParams(vmem_limit_bytes=48 * 1024 * 1024)
NT = (((1,), (1,)), ((), ()))


def plane_rows_of(ntau):
    return -(-2 * ntau // 8) * 8


def swap(block, axis, size, bit):
    return lax.ppermute(block, axis, [(i, i ^ bit) for i in range(size)])


def bits_of(size):
    return [1 << b for b in range(size.bit_length() - 1)]


def pack_kernel(
    slice_hbm, tau_hbm, weight_hbm, mix_hbm, empty_hbm, occ_hbm, trial_hbm,
    packed_ref, times_ref,
    partial_ref, slice_ref, tau_ref, weight_ref, mix_ref, empty_ref, sems,
):
    nocc = occ_hbm.shape[1]
    per_slice, nempty = mix_ref.shape
    nbands = partial_ref.shape[1]
    width = nempty // slice_ref.shape[0]
    per_chunk = LANES // width
    copies = [
        pltpu.make_async_copy(source, target, sems.at[i])
        for i, (source, target) in enumerate((
            (slice_hbm, slice_ref),
            (mix_hbm, mix_ref),
            (empty_hbm, empty_ref),
            (tau_hbm, tau_ref),
            (weight_hbm, weight_ref),
            (occ_hbm, packed_ref.at[:, :nocc]),
            (trial_hbm, packed_ref.at[:, nocc + nbands :]),
        ))
    ]
    for copy in copies:
        copy.start()
    partial_ref[...] = jnp.zeros_like(partial_ref)
    lane = lax.broadcasted_iota(jnp.int32, (per_slice, LANES), 1) // width
    inside = [lane == b for b in range(per_chunk)]
    for copy in copies[:3]:
        copy.wait()
    for chunk in range(nempty // LANES):
        at = slice(chunk * LANES, (chunk + 1) * LANES)
        mix = mix_ref[:, at]
        diagonal = jnp.concatenate(
            [jnp.where(inside[b], mix, jnp.zeros_like(mix)).astype(jnp.bfloat16) for b in range(per_chunk)], axis=0
        )
        share = lax.dot_general(diagonal, empty_ref[:, at], NT, preferred_element_type=jnp.float32)
        for b in range(per_chunk):
            first = pl.multiple_of(slice_ref[chunk * per_chunk + b] * per_slice, per_slice)
            to = pl.ds(first, per_slice)
            partial_ref[b, to, :] = partial_ref[b, to, :] + share[b * per_slice : (b + 1) * per_slice]
    pseudo = partial_ref[0]
    for b in range(1, per_chunk):
        pseudo = pseudo + partial_ref[b]
    packed_ref[:, nocc : nocc + nbands] = pseudo.T.astype(jnp.bfloat16)
    for copy in copies[3:]:
        copy.wait()
    ntau = tau_ref.shape[0]
    for k in range(ntau):
        times_ref[k : k + 1, :] = jnp.full((1, LANES), tau_ref[k], jnp.float32)
        times_ref[ntau + k : ntau + k + 1, :] = jnp.full((1, LANES), weight_ref[k], jnp.float32)


def scale(block_refs, times_ref, energy_refs, ntau, scaled_ref):
    rows = block_refs[0].shape[0]
    nocc = energy_refs[0].shape[1]
    at = 0
    for plane in range(0, times_ref.shape[0], plane_rows_of(ntau)):
        for k in range(plane, plane + ntau):
            point = times_ref[k : k + 1, 0:1]
            gain = jnp.concatenate(
                [jnp.exp(energy_refs[0][...] * point), jnp.exp(-energy_refs[1][...] * point)], axis=1
            )
            for ref in block_refs:
                states = ref[:, : scaled_ref.shape[1]].astype(jnp.float32)
                scaled_ref[at : at + rows, :] = (states * gain).astype(jnp.bfloat16)
                at += rows


def respond(scaled_ref, times_ref, nocc, ntau, cols_refs):
    nstates = scaled_ref.shape[1]
    planes = range(0, times_ref.shape[0], plane_rows_of(ntau))
    rows = scaled_ref.shape[0] // (len(planes) * ntau)
    total = None
    for cols_ref in cols_refs:
        cols = cols_ref[...]
        g_occ = lax.dot_general(scaled_ref[:, :nocc], cols[:, :nocc], NT, preferred_element_type=jnp.float32)
        g_un = lax.dot_general(scaled_ref[:, nocc:], cols[:, nocc:nstates], NT, preferred_element_type=jnp.float32)
        trial = cols[:, nstates:]
        at = 0
        for plane in planes:
            for k in range(plane + ntau, plane + 2 * ntau):
                weight = times_ref[k : k + 1, 0:1]
                chi = (weight * g_occ[at : at + rows] * g_un[at : at + rows]).astype(jnp.bfloat16)
                term = jnp.dot(chi, trial, preferred_element_type=jnp.float32)
                total = term if total is None else total + term
                at += rows
    return total


def first_kernel(ntau, own_ref, far_ref, times_ref, occ_energy_ref, pb_energy_ref, *refs):
    cols_refs, (scaled_ref, total_ref) = refs[:-2], refs[-2:]
    scale((own_ref, far_ref), times_ref, (occ_energy_ref, pb_energy_ref), ntau, scaled_ref)
    total_ref[...] = respond(scaled_ref, times_ref, occ_energy_ref.shape[1], ntau, cols_refs)


def second_kernel(
    ntau, nseen, own_ref, far_ref, times_ref, more_times_ref, occ_energy_ref, pb_energy_ref, scaled_ref, before_ref, *refs
):
    cols_refs, (more_scaled_ref, total_ref) = refs[:-2], refs[-2:]
    nocc = occ_energy_ref.shape[1]
    scale((own_ref, far_ref), more_times_ref, (occ_energy_ref, pb_energy_ref), ntau, more_scaled_ref)
    total = before_ref[...] + respond(more_scaled_ref, more_times_ref, nocc, ntau, cols_refs)
    if len(cols_refs) > nseen:
        total = total + respond(scaled_ref, times_ref, nocc, ntau, cols_refs[nseen:])
    total_ref[...] = total


def last_kernel(ntau, nocc, times_ref, more_times_ref, scaled_ref, more_scaled_ref, before_ref, cols_ref, total_ref):
    total_ref[...] = (
        before_ref[...]
        + respond(scaled_ref, times_ref, nocc, ntau, [cols_ref])
        + respond(more_scaled_ref, more_times_ref, nocc, ntau, [cols_ref])
    )


def call(kernel, outs, args, name, cost=None):
    return pl.pallas_call(
        kernel,
        out_shape=outs,
        in_specs=[VMEM] * len(args),
        out_specs=jax.tree.map(lambda _: VMEM, outs),
        compiler_params=PARAMS,
        cost_estimate=cost,
        name=name,
    )(*args)


def local(sizes, occ_states, empty_states, mix_weights, slice_of_block, occ_energy, pb_energy, tau_points, tau_weights, trial):
    nrow, ncol, nplanes = sizes
    rows, nocc = occ_states.shape
    npb, nv = pb_energy.shape[0], trial.shape[1]
    ntau = tau_points.shape[0]
    plane_rows = plane_rows_of(ntau)
    width = nocc + npb + nv

    nblocks, (nempty, per_slice) = slice_of_block.shape[0], mix_weights.shape
    operands = (slice_of_block, tau_points, tau_weights, mix_weights.T, empty_states, occ_states, trial)
    own, times = pl.pallas_call(
        pack_kernel,
        out_shape=(
            jax.ShapeDtypeStruct((rows, width), jnp.bfloat16),
            jax.ShapeDtypeStruct((plane_rows, LANES), jnp.float32),
        ),
        in_specs=[pl.BlockSpec(memory_space=pl.ANY)] * len(operands),
        out_specs=(VMEM, VMEM),
        scratch_shapes=[
            pltpu.VMEM((LANES * nblocks // nempty, npb, rows), jnp.float32),
            pltpu.SMEM((nblocks,), jnp.int32),
            pltpu.SMEM((ntau,), jnp.float32),
            pltpu.SMEM((ntau,), jnp.float32),
            pltpu.VMEM((per_slice, nempty), jnp.float32),
            pltpu.VMEM((rows, nempty), jnp.bfloat16),
            pltpu.SemaphoreType.DMA((len(operands),)),
        ],
        compiler_params=PARAMS,
        name="pack",
    )(*[pltpu.with_memory_space_constraint(operand, pltpu.HBM) for operand in operands])

    col_bits, row_bits = bits_of(ncol), bits_of(nrow)
    near_bits, far_bit = col_bits[:-1], col_bits[-1]
    received = []
    for bit in near_bits:
        received.append(swap(jnp.concatenate([own, *received]), "col", ncol, bit))
    near = jnp.concatenate([own, *received])
    far = swap(own, "col", ncol, far_bit)
    beside = swap(own, "row", nrow, row_bits[0])
    later = []
    for bit in row_bits[1:]:
        later.append(swap(jnp.concatenate([near, *later]), "row", nrow, bit))
    others = []
    for bit in bits_of(nplanes):
        others.append(swap(jnp.concatenate([times, *others]), "tau", nplanes, bit))
    more_times = jnp.concatenate(others)

    energies = (occ_energy[None, :], pb_energy[None, :])
    scaled_of = lambda times: jax.ShapeDtypeStruct(
        (times.shape[0] // plane_rows * ntau * 2 * rows, nocc + npb), jnp.bfloat16
    )
    total_of = jax.ShapeDtypeStruct((2 * rows, nv), jnp.float32)
    scaled, total = call(
        functools.partial(first_kernel, ntau),
        (scaled_of(times), total_of),
        (own, far, times, *energies, near, beside),
        "first",
        pl.CostEstimate(flops=FIRST_COST, bytes_accessed=10**6, transcendentals=0),
    )
    total, more_times, *later = lax.optimization_barrier((total, more_times, *later))
    last = swap(jnp.concatenate([*received, *later]), "row", nrow, row_bits[0])
    more_scaled, total = call(
        functools.partial(second_kernel, ntau, 2),
        (scaled_of(more_times), total_of),
        (own, far, times, more_times, *energies, scaled, total, near, beside, *later),
        "second",
    )
    total = call(
        functools.partial(last_kernel, ntau, nocc),
        total_of,
        (times, more_times, scaled, more_scaled, total, last),
        "last",
    )
    return total[:rows] + swap(total[rows:], "col", ncol, far_bit)


def solution(mesh):
    points = P(("col", "row"), None)
    in_specs = (points, points, P(), P(), P(), P(), P("tau"), P("tau"), points)
    sizes = tuple(mesh.shape[axis] for axis in ("row", "col", "tau"))
    return jax.shard_map(
        functools.partial(local, sizes), mesh=mesh, in_specs=in_specs, out_specs=points, check_vma=False
    )
```

time: 32.1 us -> 20.9 us (0.65)
  waiting for transfers between devices: 12.7 us -> 3.58 us
  local copies, waits for them, and re-layouts: 4.07 us -> 0.03 us
  starting transfers between devices: 10.9 us -> 12.2 us
  Pallas kernels: 3.43 us -> 4.28 us
    ppermute x7, waiting for transfers between devices: 12.7 us -> 3.58 us  [swap(): return lax.ppermute(block, axis, [(i, i ^ bit) for i in range(size)])]
    unnamed x19 -> x5, local copies, waits for them, and re-layouts: 4.05 us -> 0.01 us
    ppermute x7, starting transfers between devices: 10.9 us -> 12.2 us  [swap(): return lax.ppermute(block, axis, [(i, i ^ bit) for i in range(size)])]
    pallas_call x3, Pallas kernels: 1.82 us -> 2.33 us  [call(): pl.pallas_call(kernel, out_shape=outs, in_specs=[VMEM] * len(args), out_s...]
    pallas_call x1, Pallas kernels: 1.61 us -> 1.96 us  [local(): pl.pallas_call(pack_kernel, out_shape=(jax.ShapeDtypeStruct((rows, width)...]
  transfers between devices with their start and end apart: 7 -> 7, of which waited for: 4 -> 5; matrix products, arithmetic and copies ran while one was open for 0% -> 0% of each run, Pallas kernels for 4% -> 8%
where the time goes in v2:
time: 20.9 us; the launch traced here: 20.8 us
  starting transfers between devices  12.2 us (58%)
  Pallas kernels  4.28 us (20%)
  waiting for transfers between devices  3.58 us (17%)
  other arithmetic  0.62 us (3%)
    ppermute x7, starting transfers between devices, swap(): return lax.ppermute(block, axis, [(i, i ^ bit) for i in range(size)])  12.2 us
    ppermute x7, waiting for transfers between devices, swap(): return lax.ppermute(block, axis, [(i, i ^ bit) for i in range(size)])  3.58 us
    pallas_call x3, Pallas kernels, call(): pl.pallas_call(kernel, out_shape=outs, in_specs=[VMEM] * len(args), out_s...  2.33 us
    pallas_call x1, Pallas kernels, local(): pl.pallas_call(pack_kernel, out_shape=(jax.ShapeDtypeStruct((rows, width)...  1.96 us
    add x1, other arithmetic, local(): return total[:rows] + swap(total[rows:], 'col', ncol, far_bit)  0.61 us
  transfers between devices with their start and end apart: 7, of which 5 were waited for; matrix products, arithmetic and copies ran while one was open for 0% of the time, Pallas kernels for 8%

profile of v2, /device:TPU:0, one launch (start us, length us, event | category | flops | bytes accessed | tf_op | source)
XLA Modules:
  0.0 20.8 jit_solution(11589936129146052198)
XLA Ops:
  0.0 2.0 %pack.1 = (bf16[32,1024]{1,0:T(8,128)(2,1)S(1)}, f32[8,128]{1,0:T(8,128)S(1)}) custom-call(s32[128]{0:T(128)} %slice_hbm.1, f32[3]{0:T(128)} %tau_hbm.1, f32[3]{0:T(128)} %weight_hbm.1, f32[16,4096]{1,0:T(8,128)} %bitcast.4, bf16[32,4096]{1,0:T(8,128)(2,1)} %empty_hbm.1, bf16[32,512]{1,0:T(8,128)(2,1)} %occ_hbm.1, bf16[32,128]{1,0:T(8,128)(2,1)} %trial_hbm.1), custom_call_target="tpu_custom_call" | custom-call | tf_op jit(solution)/shard_map/pack/pallas_call | solution.py:166
  2.0 0.5 %collective-permute-start.2 = (bf16[32,1024]{1,0:T(8,128)(2,1)S(1)}, bf16[32,1024]{1,0:T(8,128)(2,1)S(1)}, u32[]{:S(2)}, u32[]{:S(2)}) collective-permute-start(bf16[32,1024]{1,0:T(8,128)(2,1)S(1)} %get-tuple-element.15.own_ref), channel_id=1, source_target_pairs={{0,8},{8,0},{16,24},{24,16},{1,9},{9,1},{17,25},{25,17},{2,10},{10... | collective-permute-start | bytes 196616 | tf_op jit(solution)/shard_map/ppermute | solution.py:22
  2.5 2.6 %collective-permute-start.1 = (bf16[32,1024]{1,0:T(8,128)(2,1)S(1)}, bf16[32,1024]{1,0:T(8,128)(2,1)S(1)}, u32[]{:S(2)}, u32[]{:S(2)}) collective-permute-start(bf16[32,1024]{1,0:T(8,128)(2,1)S(1)} %get-tuple-element.15.own_ref), channel_id=1, source_target_pairs={{0,2},{2,0},{4,6},{6,4},{1,3},{3,1},{5,7},{7,5},{8,10},{10,8},{12,... | collective-permute-start | bytes 196616 | tf_op jit(solution)/shard_map/ppermute | solution.py:22
  5.1 2.6 %collective-permute-start = (bf16[32,1024]{1,0:T(8,128)(2,1)S(1)}, bf16[32,1024]{1,0:T(8,128)(2,1)S(1)}, u32[]{:S(2)}, u32[]{:S(2)}) collective-permute-start(bf16[32,1024]{1,0:T(8,128)(2,1)S(1)} %get-tuple-element.15.own_ref), channel_id=1, source_target_pairs={{0,4},{2,6},{4,0},{6,2},{1,5},{3,7},{5,1},{7,3},{8,12},{10,14},{12... | collective-permute-start | bytes 196616 | tf_op jit(solution)/shard_map/ppermute | solution.py:22
  7.7 0.1 collective-permute-done.1
  7.8 0.0 copy-start.1
  7.8 1.7 %collective-permute-start.4 = (bf16[64,1024]{1,0:T(8,128)(2,1)S(1)}, bf16[64,1024]{1,0:T(8,128)(2,1)S(1)}, u32[]{:S(2)}, u32[]{:S(2)}) collective-permute-start(bf16[64,1024]{1,0:T(8,128)(2,1)S(1)} %constant_dynamic-update-slice_fusion.refs_0_), channel_id=1, source_target_pairs={{0,16},{8,24},{16,0},{24,8},{1,17},{9,25},{17,1},{25,9},{2,18},{10... | collective-permute-start | bytes 393224 | tf_op jit(solution)/shard_map/ppermute | solution.py:22
  9.6 0.0 copy-start
  9.6 1.5 %collective-permute-start.3 = (f32[8,128]{1,0:T(8,128)S(1)}, f32[8,128]{1,0:T(8,128)S(1)}, u32[]{:S(2)}, u32[]{:S(2)}) collective-permute-start(f32[8,128]{1,0:T(8,128)S(1)} %get-tuple-element.14.times_ref), channel_id=1, source_target_pairs={{0,1},{1,0},{2,3},{3,2},{4,5},{5,4},{6,7},{7,6},{8,9},{9,8},{10,11... | collective-permute-start | bytes 12296 | tf_op jit(solution)/shard_map/ppermute | solution.py:22
  11.1 0.0 copy-done.1
  11.1 0.0 collective-permute-done.2.refs_1_
  11.1 0.6 %collective-permute-done.far_ref = bf16[32,1024]{1,0:T(8,128)(2,1)S(1)} collective-permute-done((bf16[32,1024]{1,0:T(8,128)(2,1)S(1)}, bf16[32,1024]{1,0:T(8,128)(2,1)S(1)}, u32[]{:S(2)}, u32[]{:S(2)}) %collective-permute-start) | collective-permute-done | bytes 65568 | tf_op jit(solution)/shard_map/ppermute | solution.py:22
  11.7 0.0 copy-done
  11.7 0.6 %first.1 = (bf16[192,896]{1,0:T(8,128)(2,1)S(1)}, f32[64,128]{1,0:T(8,128)S(1)}) custom-call(bf16[32,1024]{1,0:T(8,128)(2,1)S(1)} %get-tuple-element.15.own_ref, bf16[32,1024]{1,0:T(8,128)(2,1)S(1)} %collective-permute-done.far_ref, f32[8,128]{1,0:T(8,128)S(1)} %get-tuple-element.14.times_ref, f32[1,512]{1,0:T(1,128)S(1)} %bitcast.2, ...), custom_call_target="tpu_custom_call" | custom-call | flops 1000000000 | bytes 1000000 | tf_op jit(solution)/shard_map/first/pallas_call | solution.py:145
  12.3 0.8 %collective-permute-done.3.more_times_ref = f32[8,128]{1,0:T(8,128)S(1)} collective-permute-done((f32[8,128]{1,0:T(8,128)S(1)}, f32[8,128]{1,0:T(8,128)S(1)}, u32[]{:S(2)}, u32[]{:S(2)}) %collective-permute-start.3) | collective-permute-done | bytes 4128 | tf_op jit(solution)/shard_map/ppermute | solution.py:22
  13.2 0.0 collective-permute-done.4.refs_2_
  13.2 0.1 collective-permute-start.5
  13.3 1.1 %second.1 = (bf16[192,896]{1,0:T(8,128)(2,1)S(1)}, f32[64,128]{1,0:T(8,128)S(1)}) custom-call(bf16[32,1024]{1,0:T(8,128)(2,1)S(1)} %get-tuple-element.15.own_ref, bf16[32,1024]{1,0:T(8,128)(2,1)S(1)} %collective-permute-done.far_ref, f32[8,128]{1,0:T(8,128)S(1)} %get-tuple-element.14.times_ref, f32[8,128]{1,0:T(8,128)S(1)} %collective-permute-done.3.more_times_ref, ...), custom_call_target="tpu_custom_call" | custom-call | tf_op jit(solution)/shard_map/second/pallas_call | solution.py:145
  14.4 0.3 %collective-permute-done.5.cols_ref = bf16[96,1024]{1,0:T(8,128)(2,1)S(1)} collective-permute-done((bf16[96,1024]{1,0:T(8,128)(2,1)S(1)}, bf16[96,1024]{1,0:T(8,128)(2,1)S(1)}, u32[]{:S(2)}, u32[]{:S(2)}) %collective-permute-start.5) | collective-permute-done | bytes 196640 | tf_op jit(solution)/shard_map/ppermute | solution.py:22
  14.7 0.6 %last.1 = f32[64,128]{1,0:T(8,128)S(1)} custom-call(f32[8,128]{1,0:T(8,128)S(1)} %get-tuple-element.14.times_ref, f32[8,128]{1,0:T(8,128)S(1)} %collective-permute-done.3.more_times_ref, bf16[192,896]{1,0:T(8,128)(2,1)S(1)} %get-tuple-element.18.scaled_ref, bf16[192,896]{1,0:T(8,128)(2,1)S(1)} %get-tuple-element.21.more_scaled_ref, ...), custom_call_target="tpu_custom_call" | custom-call | tf_op jit(solution)/shard_map/last/pallas_call | solution.py:145
  15.3 3.1 %collective-permute-start.6 = (f32[32,128]{1,0:T(8,128)S(1)}, f32[32,128]{1,0:T(8,128)S(1)}, u32[]{:S(2)}, u32[]{:S(2)}) collective-permute-start(f32[32,128]{1,0:T(8,128)S(1)} %slice.9), channel_id=1, source_target_pairs={{0,4},{2,6},{4,0},{6,2},{1,5},{3,7},{5,1},{7,3},{8,12},{10,14},{12... | collective-permute-start | bytes 49160 | tf_op jit(solution)/shard_map/ppermute | solution.py:22
  18.4 1.7 %collective-permute-done.6 = f32[32,128]{1,0:T(8,128)S(1)} collective-permute-done((f32[32,128]{1,0:T(8,128)S(1)}, f32[32,128]{1,0:T(8,128)S(1)}, u32[]{:S(2)}, u32[]{:S(2)}) %collective-permute-start.6) | collective-permute-done | bytes 16416 | tf_op jit(solution)/shard_map/ppermute | solution.py:22
  20.1 0.6 %slice_add_fusion = f32[32,128]{1,0:T(8,128)} fusion(f32[32,128]{1,0:T(8,128)S(1)} %collective-permute-done.6, f32[64,128]{1,0:T(8,128)S(1)} %last.1), kind=kLoop, calls=%fused_computation.1 | loop fusion | flops 4096 | bytes 49152 | tf_op jit(solution)/shard_map/add | solution.py:229
  (5 shorter events, 0.0 us)
Async XLA Ops:
  2.0 9.1 %collective-permute-start.2 = (bf16[32,1024]{1,0:T(8,128)(2,1)S(1)}, bf16[32,1024]{1,0:T(8,128)(2,1)S(1)}, u32[]{:S(2)}, u32[]{:S(2)}) collective-permute-start(bf16[32,1024]{1,0:T(8,128)(2,1)S(1)} %get-tuple-element.15.own_ref), channel_id=1, source_target_pairs={{0,8},{8,0},{16,24},{24,16},{1,9},{9,1},{17,25},{25,17},{2,10},{10... | collective-permute-start | bytes 196616 | tf_op jit(solution)/shard_map/ppermute | solution.py:22
  2.5 5.3 %collective-permute-start.1 = (bf16[32,1024]{1,0:T(8,128)(2,1)S(1)}, bf16[32,1024]{1,0:T(8,128)(2,1)S(1)}, u32[]{:S(2)}, u32[]{:S(2)}) collective-permute-start(bf16[32,1024]{1,0:T(8,128)(2,1)S(1)} %get-tuple-element.15.own_ref), channel_id=1, source_target_pairs={{0,2},{2,0},{4,6},{6,4},{1,3},{3,1},{5,7},{7,5},{8,10},{10,8},{12,... | collective-permute-start | bytes 196616 | tf_op jit(solution)/shard_map/ppermute | solution.py:22
  5.1 6.6 %collective-permute-start = (bf16[32,1024]{1,0:T(8,128)(2,1)S(1)}, bf16[32,1024]{1,0:T(8,128)(2,1)S(1)}, u32[]{:S(2)}, u32[]{:S(2)}) collective-permute-start(bf16[32,1024]{1,0:T(8,128)(2,1)S(1)} %get-tuple-element.15.own_ref), channel_id=1, source_target_pairs={{0,4},{2,6},{4,0},{6,2},{1,5},{3,7},{5,1},{7,3},{8,12},{10,14},{12... | collective-permute-start | bytes 196616 | tf_op jit(solution)/shard_map/ppermute | solution.py:22
  7.8 3.3 %copy-start.1 = (f32[384]{0:T(512)S(1)}, f32[384]{0:T(512)}, u32[]{:S(2)}) copy-start(f32[384]{0:T(512)} %param.14) | copy-start | bytes 4612
  7.8 5.3 %collective-permute-start.4 = (bf16[64,1024]{1,0:T(8,128)(2,1)S(1)}, bf16[64,1024]{1,0:T(8,128)(2,1)S(1)}, u32[]{:S(2)}, u32[]{:S(2)}) collective-permute-start(bf16[64,1024]{1,0:T(8,128)(2,1)S(1)} %constant_dynamic-update-slice_fusion.refs_0_), channel_id=1, source_target_pairs={{0,16},{8,24},{16,0},{24,8},{1,17},{9,25},{17,1},{25,9},{2,18},{10... | collective-permute-start | bytes 393224 | tf_op jit(solution)/shard_map/ppermute | solution.py:22
  9.6 2.1 %copy-start = (f32[512]{0:T(512)S(1)}, f32[512]{0:T(512)}, u32[]{:S(2)}) copy-start(f32[512]{0:T(512)} %param.13) | copy-start | bytes 6148
  9.6 3.6 %collective-permute-start.3 = (f32[8,128]{1,0:T(8,128)S(1)}, f32[8,128]{1,0:T(8,128)S(1)}, u32[]{:S(2)}, u32[]{:S(2)}) collective-permute-start(f32[8,128]{1,0:T(8,128)S(1)} %get-tuple-element.14.times_ref), channel_id=1, source_target_pairs={{0,1},{1,0},{2,3},{3,2},{4,5},{5,4},{6,7},{7,6},{8,9},{9,8},{10,11... | collective-permute-start | bytes 12296 | tf_op jit(solution)/shard_map/ppermute | solution.py:22
  13.2 1.5 %collective-permute-start.5 = (bf16[96,1024]{1,0:T(8,128)(2,1)S(1)}, bf16[96,1024]{1,0:T(8,128)(2,1)S(1)}, u32[]{:S(2)}, u32[]{:S(2)}) collective-permute-start(bf16[96,1024]{1,0:T(8,128)(2,1)S(1)} %pad_maximum_fusion), channel_id=1, source_target_pairs={{0,8},{8,0},{16,24},{24,16},{1,9},{9,1},{17,25},{25,17},{2,10},{10... | collective-permute-start | bytes 589832 | tf_op jit(solution)/shard_map/ppermute | solution.py:22
  15.3 4.8 %collective-permute-start.6 = (f32[32,128]{1,0:T(8,128)S(1)}, f32[32,128]{1,0:T(8,128)S(1)}, u32[]{:S(2)}, u32[]{:S(2)}) collective-permute-start(f32[32,128]{1,0:T(8,128)S(1)} %slice.9), channel_id=1, source_target_pairs={{0,4},{2,6},{4,0},{6,2},{1,5},{3,7},{5,1},{7,3},{8,12},{10,14},{12... | collective-permute-start | bytes 49160 | tf_op jit(solution)/shard_map/ppermute | solution.py:22

commit v3 on v2

--- a/solution.py
+++ b/solution.py
@@ -97,22 +97,18 @@
 def respond(scaled_ref, times_ref, nocc, ntau, cols_refs):
     nstates = scaled_ref.shape[1]
     planes = range(0, times_ref.shape[0], plane_rows_of(ntau))
-    rows = scaled_ref.shape[0] // (len(planes) * ntau)
-    total = None
-    for cols_ref in cols_refs:
-        cols = cols_ref[...]
-        g_occ = lax.dot_general(scaled_ref[:, :nocc], cols[:, :nocc], NT, preferred_element_type=jnp.float32)
-        g_un = lax.dot_general(scaled_ref[:, nocc:], cols[:, nocc:nstates], NT, preferred_element_type=jnp.float32)
-        trial = cols[:, nstates:]
-        at = 0
-        for plane in planes:
-            for k in range(plane + ntau, plane + 2 * ntau):
-                weight = times_ref[k : k + 1, 0:1]
-                chi = (weight * g_occ[at : at + rows] * g_un[at : at + rows]).astype(jnp.bfloat16)
-                term = jnp.dot(chi, trial, preferred_element_type=jnp.float32)
-                total = term if total is None else total + term
-                at += rows
-    return total
+    weights = [times_ref[plane + ntau + k : plane + ntau + k + 1, 0:1] for plane in planes for k in range(ntau)]
+    rows = scaled_ref.shape[0] // len(weights)
+    occ, pb, trial = (
+        jnp.concatenate([ref[:, at] for ref in cols_refs], axis=0)
+        for at in (slice(nocc), slice(nocc, nstates), slice(nstates, None))
+    )
+    g_occ = lax.dot_general(scaled_ref[:, :nocc], occ, NT, preferred_element_type=jnp.float32)
+    g_un = lax.dot_general(scaled_ref[:, nocc:], pb, NT, preferred_element_type=jnp.float32)
+    each = [slice(k * rows, (k + 1) * rows) for k in range(len(weights))]
+    chi = jnp.concatenate([(w * g_occ[at] * g_un[at]).astype(jnp.bfloat16) for w, at in zip(weights, each)], axis=0)
+    terms = jnp.dot(chi, trial, preferred_element_type=jnp.float32)
+    return functools.reduce(jnp.add, [terms[at] for at in each])
 
 
 def first_kernel(ntau, own_ref, far_ref, times_ref, occ_energy_ref, pb_energy_ref, *refs):
@@ -191,7 +187,7 @@
         received.append(swap(jnp.concatenate([own, *received]), "col", ncol, bit))
     near = jnp.concatenate([own, *received])
     far = swap(own, "col", ncol, far_bit)
-    beside = swap(own, "row", nrow, row_bits[0])
+    beside = swap(near, "row", nrow, row_bits[0])
     later = []
     for bit in row_bits[1:]:
         later.append(swap(jnp.concatenate([near, *later]), "row", nrow, bit))
@@ -208,14 +204,14 @@
     scaled, total = call(
         functools.partial(first_kernel, ntau),
         (scaled_of(times), total_of),
-        (own, far, times, *energies, near, beside),
+        (own, far, times, *energies, near),
         "first",
         pl.CostEstimate(flops=FIRST_COST, bytes_accessed=10**6, transcendentals=0),
     )
     total, more_times, *later = lax.optimization_barrier((total, more_times, *later))
-    last = swap(jnp.concatenate([*received, *later]), "row", nrow, row_bits[0])
+    last = swap(jnp.concatenate(later), "row", nrow, row_bits[0])
     more_scaled, total = call(
-        functools.partial(second_kernel, ntau, 2),
+        functools.partial(second_kernel, ntau, 1),
         (scaled_of(more_times), total_of),
         (own, far, times, more_times, *energies, scaled, total, near, beside, *later),
         "second",

time: 20.9 us -> 20.3 us (0.971)
  Pallas kernels: 4.28 us -> 3.63 us
  waiting for transfers between devices: 3.58 us -> 4.09 us
  starting transfers between devices: 12.2 us -> 11.8 us
    pallas_call x3, Pallas kernels: 2.33 us -> 1.67 us  [call(): pl.pallas_call(kernel, out_shape=outs, in_specs=[VMEM] * len(args), out_s...]
    ppermute x7, waiting for transfers between devices: 3.58 us -> 4.09 us  [swap(): return lax.ppermute(block, axis, [(i, i ^ bit) for i in range(size)])]
    ppermute x7, starting transfers between devices: 12.2 us -> 11.8 us  [swap(): return lax.ppermute(block, axis, [(i, i ^ bit) for i in range(size)])]
  transfers between devices with their start and end apart: 7 -> 7, of which waited for: 5 -> 4; matrix products, arithmetic and copies ran while one was open for 0% -> 0% of each run, Pallas kernels for 8% -> 6%
where the time goes in v3:
time: 20.3 us; the launch traced here: 20.2 us
  starting transfers between devices  11.8 us (58%)
  waiting for transfers between devices  4.09 us (20%)
  Pallas kernels  3.63 us (18%)
  other arithmetic  0.61 us (3%)
    ppermute x7, starting transfers between devices, swap(): return lax.ppermute(block, axis, [(i, i ^ bit) for i in range(size)])  11.8 us
    ppermute x7, waiting for transfers between devices, swap(): return lax.ppermute(block, axis, [(i, i ^ bit) for i in range(size)])  4.09 us
    pallas_call x1, Pallas kernels, local(): pl.pallas_call(pack_kernel, out_shape=(jax.ShapeDtypeStruct((rows, width)...  1.95 us
    pallas_call x3, Pallas kernels, call(): pl.pallas_call(kernel, out_shape=outs, in_specs=[VMEM] * len(args), out_s...  1.67 us
    add x1, other arithmetic, local(): return total[:rows] + swap(total[rows:], 'col', ncol, far_bit)  0.61 us
  transfers between devices with their start and end apart: 7, of which 4 were waited for; matrix products, arithmetic and copies ran while one was open for 0% of the time, Pallas kernels for 6%

profile of v3, /device:TPU:0, one launch (start us, length us, event | category | flops | bytes accessed | tf_op | source)
XLA Modules:
  0.0 20.2 jit_solution(7566528194944850505)
XLA Ops:
  0.0 2.0 %pack.1 = (bf16[32,1024]{1,0:T(8,128)(2,1)S(1)}, f32[8,128]{1,0:T(8,128)S(1)}) custom-call(s32[128]{0:T(128)} %slice_hbm.1, f32[3]{0:T(128)} %tau_hbm.1, f32[3]{0:T(128)} %weight_hbm.1, f32[16,4096]{1,0:T(8,128)} %bitcast.4, bf16[32,4096]{1,0:T(8,128)(2,1)} %empty_hbm.1, bf16[32,512]{1,0:T(8,128)(2,1)} %occ_hbm.1, bf16[32,128]{1,0:T(8,128)(2,1)} %trial_hbm.1), custom_call_target="tpu_custom_call" | custom-call | tf_op jit(solution)/shard_map/pack/pallas_call | solution.py:162
  2.0 3.1 %collective-permute-start.1 = (bf16[32,1024]{1,0:T(8,128)(2,1)S(1)}, bf16[32,1024]{1,0:T(8,128)(2,1)S(1)}, u32[]{:S(2)}, u32[]{:S(2)}) collective-permute-start(bf16[32,1024]{1,0:T(8,128)(2,1)S(1)} %get-tuple-element.15.own_ref), channel_id=1, source_target_pairs={{0,2},{2,0},{4,6},{6,4},{1,3},{3,1},{5,7},{7,5},{8,10},{10,8},{12,... | collective-permute-start | bytes 196616 | tf_op jit(solution)/shard_map/ppermute | solution.py:22
  5.1 2.6 %collective-permute-start = (bf16[32,1024]{1,0:T(8,128)(2,1)S(1)}, bf16[32,1024]{1,0:T(8,128)(2,1)S(1)}, u32[]{:S(2)}, u32[]{:S(2)}) collective-permute-start(bf16[32,1024]{1,0:T(8,128)(2,1)S(1)} %get-tuple-element.15.own_ref), channel_id=1, source_target_pairs={{0,4},{2,6},{4,0},{6,2},{1,5},{3,7},{5,1},{7,3},{8,12},{10,14},{12... | collective-permute-start | bytes 196616 | tf_op jit(solution)/shard_map/ppermute | solution.py:22
  7.6 0.0 collective-permute-done.1
  7.7 0.0 copy-start.1
  7.7 1.6 %collective-permute-start.3 = (bf16[64,1024]{1,0:T(8,128)(2,1)S(1)}, bf16[64,1024]{1,0:T(8,128)(2,1)S(1)}, u32[]{:S(2)}, u32[]{:S(2)}) collective-permute-start(bf16[64,1024]{1,0:T(8,128)(2,1)S(1)} %constant_dynamic-update-slice_fusion.refs_0_), channel_id=1, source_target_pairs={{0,16},{8,24},{16,0},{24,8},{1,17},{9,25},{17,1},{25,9},{2,18},{10... | collective-permute-start | bytes 393224 | tf_op jit(solution)/shard_map/ppermute | solution.py:22
  9.3 0.0 copy-start
  9.3 1.5 %collective-permute-start.2 = (f32[8,128]{1,0:T(8,128)S(1)}, f32[8,128]{1,0:T(8,128)S(1)}, u32[]{:S(2)}, u32[]{:S(2)}) collective-permute-start(f32[8,128]{1,0:T(8,128)S(1)} %get-tuple-element.14.times_ref), channel_id=1, source_target_pairs={{0,1},{1,0},{2,3},{3,2},{4,5},{5,4},{6,7},{7,6},{8,9},{9,8},{10,11... | collective-permute-start | bytes 12296 | tf_op jit(solution)/shard_map/ppermute | solution.py:22
  10.8 0.0 copy-done.1
  10.8 0.0 collective-permute-start.4
  10.8 0.1 collective-permute-done.far_ref
  11.0 0.0 copy-done
  11.0 0.5 %first.1 = (bf16[192,896]{1,0:T(8,128)(2,1)S(1)}, f32[64,128]{1,0:T(8,128)S(1)}) custom-call(bf16[32,1024]{1,0:T(8,128)(2,1)S(1)} %get-tuple-element.15.own_ref, bf16[32,1024]{1,0:T(8,128)(2,1)S(1)} %collective-permute-done.far_ref, f32[8,128]{1,0:T(8,128)S(1)} %get-tuple-element.14.times_ref, f32[1,512]{1,0:T(1,128)S(1)} %bitcast.2, ...), custom_call_target="tpu_custom_call" | custom-call | flops 1000000000 | bytes 1000000 | tf_op jit(solution)/shard_map/first/pallas_call | solution.py:141
  11.4 1.5 %collective-permute-done.2.more_times_ref = f32[8,128]{1,0:T(8,128)S(1)} collective-permute-done((f32[8,128]{1,0:T(8,128)S(1)}, f32[8,128]{1,0:T(8,128)S(1)}, u32[]{:S(2)}, u32[]{:S(2)}) %collective-permute-start.2) | collective-permute-done | bytes 4128 | tf_op jit(solution)/shard_map/ppermute | solution.py:22
  12.9 0.0 collective-permute-done.3.refs_2_
  12.9 0.0 collective-permute-start.5
  12.9 0.0 collective-permute-done.4.refs_1_
  12.9 0.7 %second.1 = (bf16[192,896]{1,0:T(8,128)(2,1)S(1)}, f32[64,128]{1,0:T(8,128)S(1)}) custom-call(bf16[32,1024]{1,0:T(8,128)(2,1)S(1)} %get-tuple-element.15.own_ref, bf16[32,1024]{1,0:T(8,128)(2,1)S(1)} %collective-permute-done.far_ref, f32[8,128]{1,0:T(8,128)S(1)} %get-tuple-element.14.times_ref, f32[8,128]{1,0:T(8,128)S(1)} %collective-permute-done.2.more_times_ref, ...), custom_call_target="tpu_custom_call" | custom-call | tf_op jit(solution)/shard_map/second/pallas_call | solution.py:141
  13.6 0.7 %collective-permute-done.5.cols_ref = bf16[64,1024]{1,0:T(8,128)(2,1)S(1)} collective-permute-done((bf16[64,1024]{1,0:T(8,128)(2,1)S(1)}, bf16[64,1024]{1,0:T(8,128)(2,1)S(1)}, u32[]{:S(2)}, u32[]{:S(2)}) %collective-permute-start.5) | collective-permute-done | bytes 131104 | tf_op jit(solution)/shard_map/ppermute | solution.py:22
  14.3 0.6 %last.1 = f32[64,128]{1,0:T(8,128)S(1)} custom-call(f32[8,128]{1,0:T(8,128)S(1)} %get-tuple-element.14.times_ref, f32[8,128]{1,0:T(8,128)S(1)} %collective-permute-done.2.more_times_ref, bf16[192,896]{1,0:T(8,128)(2,1)S(1)} %get-tuple-element.18.scaled_ref, bf16[192,896]{1,0:T(8,128)(2,1)S(1)} %get-tuple-element.21.more_scaled_ref, ...), custom_call_target="tpu_custom_call" | custom-call | tf_op jit(solution)/shard_map/last/pallas_call | solution.py:141
  14.8 2.9 %collective-permute-start.6 = (f32[32,128]{1,0:T(8,128)S(1)}, f32[32,128]{1,0:T(8,128)S(1)}, u32[]{:S(2)}, u32[]{:S(2)}) collective-permute-start(f32[32,128]{1,0:T(8,128)S(1)} %slice.9), channel_id=1, source_target_pairs={{0,4},{2,6},{4,0},{6,2},{1,5},{3,7},{5,1},{7,3},{8,12},{10,14},{12... | collective-permute-start | bytes 49160 | tf_op jit(solution)/shard_map/ppermute | solution.py:22
  17.8 1.8 %collective-permute-done.6 = f32[32,128]{1,0:T(8,128)S(1)} collective-permute-done((f32[32,128]{1,0:T(8,128)S(1)}, f32[32,128]{1,0:T(8,128)S(1)}, u32[]{:S(2)}, u32[]{:S(2)}) %collective-permute-start.6) | collective-permute-done | bytes 16416 | tf_op jit(solution)/shard_map/ppermute | solution.py:22
  19.5 0.6 %slice_add_fusion = f32[32,128]{1,0:T(8,128)} fusion(f32[32,128]{1,0:T(8,128)S(1)} %collective-permute-done.6, f32[64,128]{1,0:T(8,128)S(1)} %last.1), kind=kLoop, calls=%fused_computation | loop fusion | flops 4096 | bytes 49152 | tf_op jit(solution)/shard_map/add | solution.py:225
  (4 shorter events, 0.0 us)
Async XLA Ops:
  2.0 5.7 %collective-permute-start.1 = (bf16[32,1024]{1,0:T(8,128)(2,1)S(1)}, bf16[32,1024]{1,0:T(8,128)(2,1)S(1)}, u32[]{:S(2)}, u32[]{:S(2)}) collective-permute-start(bf16[32,1024]{1,0:T(8,128)(2,1)S(1)} %get-tuple-element.15.own_ref), channel_id=1, source_target_pairs={{0,2},{2,0},{4,6},{6,4},{1,3},{3,1},{5,7},{7,5},{8,10},{10,8},{12,... | collective-permute-start | bytes 196616 | tf_op jit(solution)/shard_map/ppermute | solution.py:22
  5.1 5.9 %collective-permute-start = (bf16[32,1024]{1,0:T(8,128)(2,1)S(1)}, bf16[32,1024]{1,0:T(8,128)(2,1)S(1)}, u32[]{:S(2)}, u32[]{:S(2)}) collective-permute-start(bf16[32,1024]{1,0:T(8,128)(2,1)S(1)} %get-tuple-element.15.own_ref), channel_id=1, source_target_pairs={{0,4},{2,6},{4,0},{6,2},{1,5},{3,7},{5,1},{7,3},{8,12},{10,14},{12... | collective-permute-start | bytes 196616 | tf_op jit(solution)/shard_map/ppermute | solution.py:22
  7.7 3.2 %copy-start.1 = (f32[384]{0:T(512)S(1)}, f32[384]{0:T(512)}, u32[]{:S(2)}) copy-start(f32[384]{0:T(512)} %param.14) | copy-start | bytes 4612
  7.7 5.2 %collective-permute-start.3 = (bf16[64,1024]{1,0:T(8,128)(2,1)S(1)}, bf16[64,1024]{1,0:T(8,128)(2,1)S(1)}, u32[]{:S(2)}, u32[]{:S(2)}) collective-permute-start(bf16[64,1024]{1,0:T(8,128)(2,1)S(1)} %constant_dynamic-update-slice_fusion.refs_0_), channel_id=1, source_target_pairs={{0,16},{8,24},{16,0},{24,8},{1,17},{9,25},{17,1},{25,9},{2,18},{10... | collective-permute-start | bytes 393224 | tf_op jit(solution)/shard_map/ppermute | solution.py:22
  9.3 1.7 %copy-start = (f32[512]{0:T(512)S(1)}, f32[512]{0:T(512)}, u32[]{:S(2)}) copy-start(f32[512]{0:T(512)} %param.13) | copy-start | bytes 6148
  9.3 3.6 %collective-permute-start.2 = (f32[8,128]{1,0:T(8,128)S(1)}, f32[8,128]{1,0:T(8,128)S(1)}, u32[]{:S(2)}, u32[]{:S(2)}) collective-permute-start(f32[8,128]{1,0:T(8,128)S(1)} %get-tuple-element.14.times_ref), channel_id=1, source_target_pairs={{0,1},{1,0},{2,3},{3,2},{4,5},{5,4},{6,7},{7,6},{8,9},{9,8},{10,11... | collective-permute-start | bytes 12296 | tf_op jit(solution)/shard_map/ppermute | solution.py:22
  10.8 2.1 %collective-permute-start.4 = (bf16[64,1024]{1,0:T(8,128)(2,1)S(1)}, bf16[64,1024]{1,0:T(8,128)(2,1)S(1)}, u32[]{:S(2)}, u32[]{:S(2)}) collective-permute-start(bf16[64,1024]{1,0:T(8,128)(2,1)S(1)} %constant_dynamic-update-slice_fusion.refs_0_), channel_id=1, source_target_pairs={{0,8},{8,0},{16,24},{24,16},{1,9},{9,1},{17,25},{25,17},{2,10},{10... | collective-permute-start | bytes 393224 | tf_op jit(solution)/shard_map/ppermute | solution.py:22
  12.9 1.3 %collective-permute-start.5 = (bf16[64,1024]{1,0:T(8,128)(2,1)S(1)}, bf16[64,1024]{1,0:T(8,128)(2,1)S(1)}, u32[]{:S(2)}, u32[]{:S(2)}) collective-permute-start(bf16[64,1024]{1,0:T(8,128)(2,1)S(1)} %collective-permute-done.3.refs_2_), channel_id=1, source_target_pairs={{0,8},{8,0},{16,24},{24,16},{1,9},{9,1},{17,25},{25,17},{2,10},{10... | collective-permute-start | bytes 393224 | tf_op jit(solution)/shard_map/ppermute | solution.py:22
  14.8 4.7 %collective-permute-start.6 = (f32[32,128]{1,0:T(8,128)S(1)}, f32[32,128]{1,0:T(8,128)S(1)}, u32[]{:S(2)}, u32[]{:S(2)}) collective-permute-start(f32[32,128]{1,0:T(8,128)S(1)} %slice.9), channel_id=1, source_target_pairs={{0,4},{2,6},{4,0},{6,2},{1,5},{3,7},{5,1},{7,3},{8,12},{10,14},{12... | collective-permute-start | bytes 49160 | tf_op jit(solution)/shard_map/ppermute | solution.py:22

commit v4 on v3

v4 whole, which is shorter than its diff:
```python
import functools

import jax
import jax.numpy as jnp
from jax import lax
from jax.experimental import pallas as pl
from jax.experimental.pallas import tpu as pltpu
from jax.sharding import PartitionSpec as P

LANES = 128
KERNEL_COST = 10**9
SECOND_COST = 3 * 10**9
VMEM = pl.BlockSpec(memory_space=pltpu.VMEM)
PARAMS = pltpu.CompilerParams(vmem_limit_bytes=48 * 1024 * 1024)
NT = (((1,), (1,)), ((), ()))


def plane_rows_of(ntau):
    return -(-2 * ntau // 8) * 8


def swap(block, axis, size, bit):
    return lax.ppermute(block, axis, [(i, i ^ bit) for i in range(size)])


def bits_of(size):
    return [1 << b for b in range(size.bit_length() - 1)]


def pack_kernel(
    slice_hbm, tau_hbm, weight_hbm, mix_hbm, empty_hbm, occ_hbm, trial_hbm,
    packed_ref, times_ref,
    slice_ref, tau_ref, weight_ref, mix_ref, empty_ref, sems, *partial_refs,
):
    nocc = occ_hbm.shape[1]
    per_slice, nempty = mix_ref.shape
    nbands = partial_refs[0].shape[0]
    width = nempty // slice_ref.shape[0]
    per_chunk = LANES // width
    copies = [
        pltpu.make_async_copy(source, target, sems.at[i])
        for i, (source, target) in enumerate((
            (slice_hbm, slice_ref),
            (mix_hbm, mix_ref),
            (empty_hbm, empty_ref),
            (tau_hbm, tau_ref),
            (weight_hbm, weight_ref),
            (occ_hbm, packed_ref.at[:, :nocc]),
            (trial_hbm, packed_ref.at[:, nocc + nbands :]),
        ))
    ]
    for copy in copies:
        copy.start()
    for ref in partial_refs:
        ref[...] = jnp.zeros_like(ref)
    lane = lax.broadcasted_iota(jnp.int32, (per_slice, LANES), 1) // width
    inside = [lane == b for b in range(per_chunk)]
    for copy in copies[:3]:
        copy.wait()
    for chunk in range(nempty // LANES):
        at = slice(chunk * LANES, (chunk + 1) * LANES)
        mix = mix_ref[:, at]
        diagonal = jnp.concatenate(
            [jnp.where(inside[b], mix, jnp.zeros_like(mix)).astype(jnp.bfloat16) for b in range(per_chunk)], axis=0
        )
        share = lax.dot_general(diagonal, empty_ref[:, at], NT, preferred_element_type=jnp.float32)
        for b, ref in enumerate(partial_refs):
            first = pl.multiple_of(slice_ref[chunk * per_chunk + b] * per_slice, per_slice)
            to = pl.ds(first, per_slice)
            ref[to, :] = ref[to, :] + share[b * per_slice : (b + 1) * per_slice]
    pseudo = functools.reduce(jnp.add, [ref[...] for ref in partial_refs])
    packed_ref[:, nocc : nocc + nbands] = pseudo.T.astype(jnp.bfloat16)
    for copy in copies[3:]:
        copy.wait()
    ntau = tau_ref.shape[0]
    for k in range(ntau):
        times_ref[k : k + 1, :] = jnp.full((1, LANES), tau_ref[k], jnp.float32)
        times_ref[ntau + k : ntau + k + 1, :] = jnp.full((1, LANES), weight_ref[k], jnp.float32)


def times_in(times_refs, ntau):
    rows = [(ref, plane + k) for ref in times_refs for plane in range(0, ref.shape[0], plane_rows_of(ntau)) for k in range(ntau)]
    return [ref[k : k + 1, 0:1] for ref, k in rows], [ref[k + ntau : k + ntau + 1, 0:1] for ref, k in rows]


def scale(block_ref, points, energy_refs, scaled_ref, at=0):
    rows, nstates = block_ref.shape[0], scaled_ref.shape[1]
    states = block_ref[:, :nstates].astype(jnp.float32)
    for point in points:
        gain = jnp.concatenate([jnp.exp(energy_refs[0][...] * point), jnp.exp(-energy_refs[1][...] * point)], axis=1)
        scaled_ref[at : at + rows, :] = (states * gain).astype(jnp.bfloat16)
        at += rows


def respond(scaled_ref, weights, nocc, cols_refs):
    nstates = scaled_ref.shape[1]
    rows = scaled_ref.shape[0] // len(weights)
    occ, pb, trial = (
        jnp.concatenate([ref[:, at] for ref in cols_refs], axis=0)
        for at in (slice(nocc), slice(nocc, nstates), slice(nstates, None))
    )
    g_occ = lax.dot_general(scaled_ref[:, :nocc], occ, NT, preferred_element_type=jnp.float32)
    g_un = lax.dot_general(scaled_ref[:, nocc:], pb, NT, preferred_element_type=jnp.float32)
    each = [slice(k * rows, (k + 1) * rows) for k in range(len(weights))]
    chi = jnp.concatenate([(w * g_occ[at] * g_un[at]).astype(jnp.bfloat16) for w, at in zip(weights, each)], axis=0)
    terms = jnp.dot(chi, trial, preferred_element_type=jnp.float32)
    return functools.reduce(jnp.add, [terms[at] for at in each])


def first_kernel(
    ntau, cols_ref, own_ref, far_ref, times_ref, occ_energy_ref, pb_energy_ref, own_scaled_ref, scaled_ref, total_ref
):
    points, weights = times_in([times_ref], ntau)
    scale(far_ref, points, (occ_energy_ref, pb_energy_ref), scaled_ref)
    scale(own_ref, points, (occ_energy_ref, pb_energy_ref), own_scaled_ref)
    total_ref[...] = respond(scaled_ref, weights, occ_energy_ref.shape[1], [cols_ref])


def second_kernel(
    ntau, block_ref, times_ref, more_times_ref, occ_energy_ref, pb_energy_ref, seen_ref, before_ref, near_ref, *refs
):
    cols_refs, (scaled_ref, total_ref) = refs[:-2], refs[-2:]
    nocc, nseen = occ_energy_ref.shape[1], seen_ref.shape[0]
    more_points, more_weights = times_in([more_times_ref], ntau)
    weights = times_in([times_ref], ntau)[1] + more_weights
    scaled_ref[:nseen, :] = seen_ref[...]
    scale(block_ref, more_points, (occ_energy_ref, pb_energy_ref), scaled_ref, nseen)
    total_ref[...] = (
        before_ref[...]
        + respond(scaled_ref.at[nseen:], more_weights, nocc, [near_ref])
        + respond(scaled_ref, weights, nocc, cols_refs)
    )


def last_kernel(ntau, nocc, times_ref, more_times_ref, scaled_ref, before_ref, cols_ref, total_ref):
    weights = times_in([times_ref, more_times_ref], ntau)[1]
    total_ref[...] = before_ref[...] + respond(scaled_ref, weights, nocc, [cols_ref])


def whole_kernel(ntau, block_ref, times_ref, more_times_ref, occ_energy_ref, pb_energy_ref, seen_ref, *refs):
    cols_refs, (total_ref, scaled_ref) = refs[:-2], refs[-2:]
    nseen = seen_ref.shape[0]
    scaled_ref[:nseen, :] = seen_ref[...]
    scale(block_ref, times_in([more_times_ref], ntau)[0], (occ_energy_ref, pb_energy_ref), scaled_ref, nseen)
    weights = times_in([times_ref, more_times_ref], ntau)[1]
    total_ref[...] = respond(scaled_ref, weights, occ_energy_ref.shape[1], cols_refs)


def call(kernel, outs, args, name, cost, scratch=()):
    return pl.pallas_call(
        kernel,
        out_shape=outs,
        in_specs=[VMEM] * len(args),
        out_specs=jax.tree.map(lambda _: VMEM, outs),
        scratch_shapes=scratch,
        compiler_params=PARAMS,
        cost_estimate=pl.CostEstimate(flops=cost, bytes_accessed=10**6, transcendentals=0),
        name=name,
    )(*args)


def local(sizes, occ_states, empty_states, mix_weights, slice_of_block, occ_energy, pb_energy, tau_points, tau_weights, trial):
    nrow, ncol, nplanes = sizes
    rows, nocc = occ_states.shape
    npb, nv = pb_energy.shape[0], trial.shape[1]
    ntau = tau_points.shape[0]
    plane_rows = plane_rows_of(ntau)
    width = nocc + npb + nv

    nblocks, (nempty, per_slice) = slice_of_block.shape[0], mix_weights.shape
    operands = (slice_of_block, tau_points, tau_weights, mix_weights.T, empty_states, occ_states, trial)
    own, times = pl.pallas_call(
        pack_kernel,
        out_shape=(
            jax.ShapeDtypeStruct((rows, width), jnp.bfloat16),
            jax.ShapeDtypeStruct((plane_rows, LANES), jnp.float32),
        ),
        in_specs=[pl.BlockSpec(memory_space=pl.ANY)] * len(operands),
        out_specs=(VMEM, VMEM),
        scratch_shapes=[
            pltpu.SMEM((nblocks,), jnp.int32),
            pltpu.SMEM((ntau,), jnp.float32),
            pltpu.SMEM((ntau,), jnp.float32),
            pltpu.VMEM((per_slice, nempty), jnp.float32),
            pltpu.VMEM((rows, nempty), jnp.bfloat16),
            pltpu.SemaphoreType.DMA((len(operands),)),
            *[pltpu.VMEM((npb, rows), jnp.float32)] * (LANES * nblocks // nempty),
        ],
        compiler_params=PARAMS,
        name="pack",
    )(*[pltpu.with_memory_space_constraint(operand, pltpu.HBM) for operand in operands])

    col_bits, row_bits = bits_of(ncol), bits_of(nrow)
    near_bits, far_bit = col_bits[:-1], col_bits[-1]
    received = []
    for bit in near_bits:
        received.append(swap(jnp.concatenate([own, *received]), "col", ncol, bit))
    near = jnp.concatenate([own, *received])
    far = swap(own, "col", ncol, far_bit)
    beside = swap(near, "row", nrow, row_bits[0])
    later = []
    for bit in row_bits[1:]:
        later.append(swap(jnp.concatenate([near, *later]), "row", nrow, bit))
    others = []
    for bit in bits_of(nplanes):
        others.append(swap(jnp.concatenate([times, *others]), "tau", nplanes, bit))
    more_times = jnp.concatenate(others)

    energies = (occ_energy[None, :], pb_energy[None, :])
    scaled_of = lambda planes: jax.ShapeDtypeStruct((planes * ntau * rows, nocc + npb), jnp.bfloat16)
    total_of = jax.ShapeDtypeStruct((rows, nv), jnp.float32)
    own_scaled, scaled, far_total = call(
        functools.partial(first_kernel, ntau),
        (scaled_of(1), scaled_of(1), total_of),
        (near, own, far, times, *energies),
        "first",
        KERNEL_COST,
    )
    far_total, *later = lax.optimization_barrier((far_total, *later))
    last = swap(jnp.concatenate(later), "row", nrow, row_bits[0])
    scaled, far_total = call(
        functools.partial(second_kernel, ntau),
        (scaled_of(nplanes), total_of),
        (far, times, more_times, *energies, scaled, far_total, near, beside, *later),
        "second",
        SECOND_COST,
    )
    far_total = call(
        functools.partial(last_kernel, ntau, nocc),
        total_of,
        (times, more_times, scaled, far_total, last),
        "last",
        KERNEL_COST,
    )
    total = call(
        functools.partial(whole_kernel, ntau),
        total_of,
        (own, times, more_times, *energies, own_scaled, near, beside, *later, last),
        "whole",
        KERNEL_COST,
        [pltpu.VMEM(scaled_of(nplanes).shape, jnp.bfloat16)],
    )
    return total + swap(far_total, "col", ncol, far_bit)


def solution(mesh):
    points = P(("col", "row"), None)
    in_specs = (points, points, P(), P(), P(), P(), P("tau"), P("tau"), points)
    sizes = tuple(mesh.shape[axis] for axis in ("row", "col", "tau"))
    return jax.shard_map(
        functools.partial(local, sizes), mesh=mesh, in_specs=in_specs, out_specs=points, check_vma=False
    )
```

time: 20.3 us -> 19.4 us (0.956)
  waiting for transfers between devices: 4.09 us -> 3.41 us
  Pallas kernels: 3.63 us -> 3.4 us
    ppermute x7, waiting for transfers between devices: 4.09 us -> 3.41 us  [swap(): return lax.ppermute(block, axis, [(i, i ^ bit) for i in range(size)])]
    pallas_call x1, Pallas kernels: 1.95 us -> 1.52 us  [local(): pl.pallas_call(pack_kernel, out_shape=(jax.ShapeDtypeStruct((rows, width)...]
    pallas_call x3 -> x4, Pallas kernels: 1.67 us -> 1.88 us  [call(): pl.pallas_call(kernel, out_shape=outs, in_specs=[VMEM] * len(args), out_s...]
  transfers between devices with their start and end apart: 7 -> 7, of which waited for: 4 -> 5; matrix products, arithmetic and copies ran while one was open for 0% -> 0% of each run, Pallas kernels for 6% -> 8%
where the time goes in v4:
time: 19.4 us; the launch traced here: 19.3 us
  starting transfers between devices  11.8 us (61%)
  waiting for transfers between devices  3.41 us (18%)
  Pallas kernels  3.4 us (18%)
  other arithmetic  0.61 us (3%)
    ppermute x7, starting transfers between devices, swap(): return lax.ppermute(block, axis, [(i, i ^ bit) for i in range(size)])  11.8 us
    ppermute x7, waiting for transfers between devices, swap(): return lax.ppermute(block, axis, [(i, i ^ bit) for i in range(size)])  3.41 us
    pallas_call x4, Pallas kernels, call(): pl.pallas_call(kernel, out_shape=outs, in_specs=[VMEM] * len(args), out_s...  1.88 us
    pallas_call x1, Pallas kernels, local(): pl.pallas_call(pack_kernel, out_shape=(jax.ShapeDtypeStruct((rows, width)...  1.52 us
    add x1, other arithmetic, local(): return total + swap(far_total, 'col', ncol, far_bit)  0.61 us
  transfers between devices with their start and end apart: 7, of which 5 were waited for; matrix products, arithmetic and copies ran while one was open for 0% of the time, Pallas kernels for 8%

profile of v4, /device:TPU:0, one launch (start us, length us, event | category | flops | bytes accessed | tf_op | source)
XLA Modules:
  0.0 19.3 jit_solution(14697567376765773319)
XLA Ops:
  0.0 1.5 %pack.1 = (bf16[32,1024]{1,0:T(8,128)(2,1)S(1)}, f32[8,128]{1,0:T(8,128)S(1)}) custom-call(s32[128]{0:T(128)} %slice_hbm.1, f32[3]{0:T(128)} %tau_hbm.1, f32[3]{0:T(128)} %weight_hbm.1, f32[16,4096]{1,0:T(8,128)} %bitcast.5, bf16[32,4096]{1,0:T(8,128)(2,1)} %empty_hbm.1, bf16[32,512]{1,0:T(8,128)(2,1)} %occ_hbm.1, bf16[32,128]{1,0:T(8,128)(2,1)} %trial_hbm.1), custom_call_target="tpu_custom_call" | custom-call | tf_op jit(solution)/shard_map/pack/pallas_call | solution.py:172
  1.5 3.1 %collective-permute-start.1 = (bf16[32,1024]{1,0:T(8,128)(2,1)S(1)}, bf16[32,1024]{1,0:T(8,128)(2,1)S(1)}, u32[]{:S(2)}, u32[]{:S(2)}) collective-permute-start(bf16[32,1024]{1,0:T(8,128)(2,1)S(1)} %get-tuple-element.14.own_ref.block_ref), channel_id=1, source_target_pairs={{0,2},{2,0},{4,6},{6,4},{1,3},{3,1},{5,7},{7,5},{8,10},{10,8},{12,... | collective-permute-start | bytes 196616 | tf_op jit(solution)/shard_map/ppermute | solution.py:23
  4.6 2.6 %collective-permute-start.2 = (bf16[32,1024]{1,0:T(8,128)(2,1)S(1)}, bf16[32,1024]{1,0:T(8,128)(2,1)S(1)}, u32[]{:S(2)}, u32[]{:S(2)}) collective-permute-start(bf16[32,1024]{1,0:T(8,128)(2,1)S(1)} %get-tuple-element.14.own_ref.block_ref), channel_id=1, source_target_pairs={{0,4},{2,6},{4,0},{6,2},{1,5},{3,7},{5,1},{7,3},{8,12},{10,14},{12... | collective-permute-start | bytes 196616 | tf_op jit(solution)/shard_map/ppermute | solution.py:23
  7.2 0.0 collective-permute-done.1
  7.2 0.0 copy-start.1
  7.2 1.6 %collective-permute-start.4 = (bf16[64,1024]{1,0:T(8,128)(2,1)S(1)}, bf16[64,1024]{1,0:T(8,128)(2,1)S(1)}, u32[]{:S(2)}, u32[]{:S(2)}) collective-permute-start(bf16[64,1024]{1,0:T(8,128)(2,1)S(1)} %constant_dynamic-update-slice_fusion.cols_ref.refs_0_.near_ref), channel_id=1, source_target_pairs={{0,16},{8,24},{16,0},{24,8},{1,17},{9,25},{17,1},{25,9},{2,18},{10... | collective-permute-start | bytes 393224 | tf_op jit(solution)/shard_map/ppermute | solution.py:23
  8.9 0.0 collective-permute-start.3
  8.9 0.0 copy-start
  8.9 1.5 %collective-permute-start = (f32[8,128]{1,0:T(8,128)S(1)}, f32[8,128]{1,0:T(8,128)S(1)}, u32[]{:S(2)}, u32[]{:S(2)}) collective-permute-start(f32[8,128]{1,0:T(8,128)S(1)} %get-tuple-element.15.times_ref), channel_id=1, source_target_pairs={{0,1},{1,0},{2,3},{3,2},{4,5},{5,4},{6,7},{7,6},{8,9},{9,8},{10,11... | collective-permute-start | bytes 12296 | tf_op jit(solution)/shard_map/ppermute | solution.py:23
  10.4 0.0 copy-done.1
  10.4 0.1 collective-permute-done.2.far_ref.block_ref
  10.5 0.0 copy-done
  10.5 0.4 %first.1 = (bf16[96,896]{1,0:T(8,128)(2,1)S(1)}, bf16[96,896]{1,0:T(8,128)(2,1)S(1)}, f32[32,128]{1,0:T(8,128)S(1)}) custom-call(bf16[64,1024]{1,0:T(8,128)(2,1)S(1)} %constant_dynamic-update-slice_fusion.cols_ref.refs_0_.near_ref, bf16[32,1024]{1,0:T(8,128)(2,1)S(1)} %get-tuple-element.14.own_ref.block_ref, ...), custom_call_target="tpu_custom_call" | custom-call | flops 1000000000 | bytes 1000000 | tf_op jit(solution)/shard_map/first/pallas_call | solution.py:150
  10.9 1.4 %collective-permute-done.4.refs_2_.refs_1_ = bf16[64,1024]{1,0:T(8,128)(2,1)S(1)} collective-permute-done((bf16[64,1024]{1,0:T(8,128)(2,1)S(1)}, bf16[64,1024]{1,0:T(8,128)(2,1)S(1)}, u32[]{:S(2)}, u32[]{:S(2)}) %collective-permute-start.4) | collective-permute-done | bytes 131104 | tf_op jit(solution)/shard_map/ppermute | solution.py:23
  12.3 0.0 collective-permute-start.5
  12.3 0.2 %collective-permute-done.more_times_ref = f32[8,128]{1,0:T(8,128)S(1)} collective-permute-done((f32[8,128]{1,0:T(8,128)S(1)}, f32[8,128]{1,0:T(8,128)S(1)}, u32[]{:S(2)}, u32[]{:S(2)}) %collective-permute-start) | collective-permute-done | bytes 4128 | tf_op jit(solution)/shard_map/ppermute | solution.py:23
  12.5 0.0 collective-permute-done.3.refs_1_.refs_0_
  12.5 0.6 %second.1 = (bf16[192,896]{1,0:T(8,128)(2,1)S(1)}, f32[32,128]{1,0:T(8,128)S(1)}) custom-call(bf16[32,1024]{1,0:T(8,128)(2,1)S(1)} %collective-permute-done.2.far_ref.block_ref, f32[8,128]{1,0:T(8,128)S(1)} %get-tuple-element.15.times_ref, f32[8,128]{1,0:T(8,128)S(1)} %collective-permute-done.more_times_ref, f32[1,512]{1,0:T(1,128)S(1)} %bitcast.3, ...), custom_call_target="tpu_custom_call" | custom-call | flops 3000000000 | bytes 1000000 | tf_op jit(solution)/shard_map/second/pallas_call | solution.py:150
  13.1 0.5 %collective-permute-done.5.refs_3_.cols_ref = bf16[64,1024]{1,0:T(8,128)(2,1)S(1)} collective-permute-done((bf16[64,1024]{1,0:T(8,128)(2,1)S(1)}, bf16[64,1024]{1,0:T(8,128)(2,1)S(1)}, u32[]{:S(2)}, u32[]{:S(2)}) %collective-permute-start.5) | collective-permute-done | bytes 131104 | tf_op jit(solution)/shard_map/ppermute | solution.py:23
  13.6 0.4 %last.1 = f32[32,128]{1,0:T(8,128)S(1)} custom-call(f32[8,128]{1,0:T(8,128)S(1)} %get-tuple-element.15.times_ref, f32[8,128]{1,0:T(8,128)S(1)} %collective-permute-done.more_times_ref, bf16[192,896]{1,0:T(8,128)(2,1)S(1)} %get-tuple-element.21.scaled_ref, f32[32,128]{1,0:T(8,128)S(1)} %get-tuple-element.22.before_ref, ...), custom_call_target="tpu_custom_call" | custom-call | flops 1000000000 | bytes 1000000 | tf_op jit(solution)/shard_map/last/pallas_call | solution.py:150
  14.0 2.9 %collective-permute-start.6 = (f32[32,128]{1,0:T(8,128)S(1)}, f32[32,128]{1,0:T(8,128)S(1)}, u32[]{:S(2)}, u32[]{:S(2)}) collective-permute-start(f32[32,128]{1,0:T(8,128)S(1)} %last.1), channel_id=1, source_target_pairs={{0,4},{2,6},{4,0},{6,2},{1,5},{3,7},{5,1},{7,3},{8,12},{10,14},{12... | collective-permute-start | bytes 49160 | tf_op jit(solution)/shard_map/ppermute | solution.py:23
  16.9 0.5 %whole.1 = f32[32,128]{1,0:T(8,128)S(1)} custom-call(bf16[32,1024]{1,0:T(8,128)(2,1)S(1)} %get-tuple-element.14.own_ref.block_ref, f32[8,128]{1,0:T(8,128)S(1)} %get-tuple-element.15.times_ref, f32[8,128]{1,0:T(8,128)S(1)} %collective-permute-done.more_times_ref, f32[1,512]{1,0:T(1,128)S(1)} %bitcast.4, f32[1,384]{1,0:T(1,128)S(1)} %broadcast_in_dim.7.pb_energy_ref, ...), custom_call_target="tpu_custom_call" | custom-call | flops 1000000000 | bytes 1000000 | tf_op jit(solution)/shard_map/whole/pallas_call | solution.py:150
  17.4 1.2 %collective-permute-done.6 = f32[32,128]{1,0:T(8,128)S(1)} collective-permute-done((f32[32,128]{1,0:T(8,128)S(1)}, f32[32,128]{1,0:T(8,128)S(1)}, u32[]{:S(2)}, u32[]{:S(2)}) %collective-permute-start.6) | collective-permute-done | bytes 16416 | tf_op jit(solution)/shard_map/ppermute | solution.py:23
  18.6 0.6 %add.3 = f32[32,128]{1,0:T(8,128)} add(f32[32,128]{1,0:T(8,128)S(1)} %whole.1, f32[32,128]{1,0:T(8,128)S(1)} %collective-permute-done.6) | non-fusion elementwise | flops 4096 | bytes 49152 | tf_op jit(solution)/shard_map/add | solution.py:243
  (3 shorter events, 0.0 us)
Async XLA Ops:
  1.5 5.7 %collective-permute-start.1 = (bf16[32,1024]{1,0:T(8,128)(2,1)S(1)}, bf16[32,1024]{1,0:T(8,128)(2,1)S(1)}, u32[]{:S(2)}, u32[]{:S(2)}) collective-permute-start(bf16[32,1024]{1,0:T(8,128)(2,1)S(1)} %get-tuple-element.14.own_ref.block_ref), channel_id=1, source_target_pairs={{0,2},{2,0},{4,6},{6,4},{1,3},{3,1},{5,7},{7,5},{8,10},{10,8},{12,... | collective-permute-start | bytes 196616 | tf_op jit(solution)/shard_map/ppermute | solution.py:23
  4.6 5.9 %collective-permute-start.2 = (bf16[32,1024]{1,0:T(8,128)(2,1)S(1)}, bf16[32,1024]{1,0:T(8,128)(2,1)S(1)}, u32[]{:S(2)}, u32[]{:S(2)}) collective-permute-start(bf16[32,1024]{1,0:T(8,128)(2,1)S(1)} %get-tuple-element.14.own_ref.block_ref), channel_id=1, source_target_pairs={{0,4},{2,6},{4,0},{6,2},{1,5},{3,7},{5,1},{7,3},{8,12},{10,14},{12... | collective-permute-start | bytes 196616 | tf_op jit(solution)/shard_map/ppermute | solution.py:23
  7.2 3.2 %copy-start.1 = (f32[384]{0:T(512)S(1)}, f32[384]{0:T(512)}, u32[]{:S(2)}) copy-start(f32[384]{0:T(512)} %param.14) | copy-start | bytes 4612
  7.2 5.0 %collective-permute-start.4 = (bf16[64,1024]{1,0:T(8,128)(2,1)S(1)}, bf16[64,1024]{1,0:T(8,128)(2,1)S(1)}, u32[]{:S(2)}, u32[]{:S(2)}) collective-permute-start(bf16[64,1024]{1,0:T(8,128)(2,1)S(1)} %constant_dynamic-update-slice_fusion.cols_ref.refs_0_.near_ref), channel_id=1, source_target_pairs={{0,16},{8,24},{16,0},{24,8},{1,17},{9,25},{17,1},{25,9},{2,18},{10... | collective-permute-start | bytes 393224 | tf_op jit(solution)/shard_map/ppermute | solution.py:23
  8.9 3.6 %collective-permute-start.3 = (bf16[64,1024]{1,0:T(8,128)(2,1)S(1)}, bf16[64,1024]{1,0:T(8,128)(2,1)S(1)}, u32[]{:S(2)}, u32[]{:S(2)}) collective-permute-start(bf16[64,1024]{1,0:T(8,128)(2,1)S(1)} %constant_dynamic-update-slice_fusion.cols_ref.refs_0_.near_ref), channel_id=1, source_target_pairs={{0,8},{8,0},{16,24},{24,16},{1,9},{9,1},{17,25},{25,17},{2,10},{10... | collective-permute-start | bytes 393224 | tf_op jit(solution)/shard_map/ppermute | solution.py:23
  8.9 1.6 %copy-start = (f32[512]{0:T(512)S(1)}, f32[512]{0:T(512)}, u32[]{:S(2)}) copy-start(f32[512]{0:T(512)} %param.13) | copy-start | bytes 6148
  8.9 3.6 %collective-permute-start = (f32[8,128]{1,0:T(8,128)S(1)}, f32[8,128]{1,0:T(8,128)S(1)}, u32[]{:S(2)}, u32[]{:S(2)}) collective-permute-start(f32[8,128]{1,0:T(8,128)S(1)} %get-tuple-element.15.times_ref), channel_id=1, source_target_pairs={{0,1},{1,0},{2,3},{3,2},{4,5},{5,4},{6,7},{7,6},{8,9},{9,8},{10,11... | collective-permute-start | bytes 12296 | tf_op jit(solution)/shard_map/ppermute | solution.py:23
  12.3 1.3 %collective-permute-start.5 = (bf16[64,1024]{1,0:T(8,128)(2,1)S(1)}, bf16[64,1024]{1,0:T(8,128)(2,1)S(1)}, u32[]{:S(2)}, u32[]{:S(2)}) collective-permute-start(bf16[64,1024]{1,0:T(8,128)(2,1)S(1)} %collective-permute-done.4.refs_2_.refs_1_), channel_id=1, source_target_pairs={{0,8},{8,0},{16,24},{24,16},{1,9},{9,1},{17,25},{25,17},{2,10},{10... | collective-permute-start | bytes 393224 | tf_op jit(solution)/shard_map/ppermute | solution.py:23
  14.0 4.6 %collective-permute-start.6 = (f32[32,128]{1,0:T(8,128)S(1)}, f32[32,128]{1,0:T(8,128)S(1)}, u32[]{:S(2)}, u32[]{:S(2)}) collective-permute-start(f32[32,128]{1,0:T(8,128)S(1)} %last.1), channel_id=1, source_target_pairs={{0,4},{2,6},{4,0},{6,2},{1,5},{3,7},{5,1},{7,3},{8,12},{10,14},{12... | collective-permute-start | bytes 49160 | tf_op jit(solution)/shard_map/ppermute | solution.py:23

commit v5 on v4

v5 whole, which is shorter than its diff:
```python
import functools

import jax
import jax.numpy as jnp
from jax import lax
from jax.experimental import pallas as pl
from jax.experimental.pallas import tpu as pltpu
from jax.sharding import PartitionSpec as P

LANES = 128
KERNEL_COST = 10**9
SCALE_COST = 10**9
JOIN_COST = 10**9
VMEM = pl.BlockSpec(memory_space=pltpu.VMEM)
PARAMS = pltpu.CompilerParams(vmem_limit_bytes=48 * 1024 * 1024)
NT = (((1,), (1,)), ((), ()))


def plane_rows_of(ntau):
    return -(-2 * ntau // 8) * 8


def swap(block, axis, size, bit):
    return lax.ppermute(block, axis, [(i, i ^ bit) for i in range(size)])


def bits_of(size):
    return [1 << b for b in range(size.bit_length() - 1)]


def pack_kernel(
    slice_hbm, tau_hbm, weight_hbm, mix_hbm, empty_hbm, occ_hbm, trial_hbm, occ_energy_hbm, pb_energy_hbm,
    packed_ref, times_ref, code_ref, energy_ref,
    slice_ref, tau_ref, weight_ref, mix_ref, empty_ref, occ_energy_ref, pb_energy_ref, sems, *partial_refs,
):
    nocc = occ_hbm.shape[1]
    per_slice, nempty = mix_ref.shape
    nbands = partial_refs[0].shape[0]
    width = nempty // slice_ref.shape[0]
    per_chunk = LANES // width
    copies = [
        pltpu.make_async_copy(source, target, sems.at[i])
        for i, (source, target) in enumerate((
            (slice_hbm, slice_ref),
            (mix_hbm, mix_ref),
            (empty_hbm, empty_ref),
            (tau_hbm, tau_ref),
            (weight_hbm, weight_ref),
            (occ_hbm, packed_ref.at[:, :nocc]),
            (trial_hbm, packed_ref.at[:, nocc + nbands :]),
            (occ_energy_hbm, occ_energy_ref),
            (pb_energy_hbm, pb_energy_ref),
        ))
    ]
    for copy in copies:
        copy.start()
    for ref in partial_refs:
        ref[...] = jnp.zeros_like(ref)
    lane = lax.broadcasted_iota(jnp.int32, (per_slice, LANES), 1) // width
    inside = [lane == b for b in range(per_chunk)]
    for copy in copies[:3]:
        copy.wait()
    for chunk in range(nempty // LANES):
        at = slice(chunk * LANES, (chunk + 1) * LANES)
        mix = mix_ref[:, at]
        diagonal = jnp.concatenate(
            [jnp.where(inside[b], mix, jnp.zeros_like(mix)).astype(jnp.bfloat16) for b in range(per_chunk)], axis=0
        )
        share = lax.dot_general(diagonal, empty_ref[:, at], NT, preferred_element_type=jnp.float32)
        for b, ref in enumerate(partial_refs):
            first = pl.multiple_of(slice_ref[chunk * per_chunk + b] * per_slice, per_slice)
            to = pl.ds(first, per_slice)
            ref[to, :] = ref[to, :] + share[b * per_slice : (b + 1) * per_slice]
    pseudo = functools.reduce(jnp.add, [ref[...] for ref in partial_refs])
    packed_ref[:, nocc : nocc + nbands] = pseudo.T.astype(jnp.bfloat16)
    for copy in copies[3:]:
        copy.wait()
    energy_ref[:, :nocc] = occ_energy_ref[...][None, :]
    energy_ref[:, nocc:] = -pb_energy_ref[...][None, :]
    ntau = tau_ref.shape[0]
    code_ref[...] = jnp.zeros_like(code_ref)
    for k in range(ntau):
        for i, ref in enumerate((tau_ref, weight_ref)):
            rest = jnp.full((1, LANES), ref[k], jnp.float32)
            times_ref[i * ntau + k : i * ntau + k + 1, :] = rest
            for j in range(3):
                part = rest.astype(jnp.bfloat16)
                row = (3 * i + j) * ntau + k
                code_ref[row : row + 1, :] = part
                rest = rest - part.astype(jnp.float32)


def times_in(times_refs, ntau):
    rows = [(ref, plane + k) for ref in times_refs for plane in range(0, ref.shape[0], plane_rows_of(ntau)) for k in range(ntau)]
    return [ref[k : k + 1, 0:1] for ref, k in rows], [ref[k + ntau : k + ntau + 1, 0:1] for ref, k in rows]


def scale(block_ref, points, energy_ref, scaled_ref):
    rows, nstates = block_ref.shape[0], scaled_ref.shape[1]
    states = block_ref[:, :nstates].astype(jnp.float32)
    energy = energy_ref[...]
    for k, point in enumerate(points):
        scaled_ref[k * rows : (k + 1) * rows, :] = (states * jnp.exp(energy * point)).astype(jnp.bfloat16)


def respond(scaled_ref, weights, nocc, nv, cols_refs):
    nstates = scaled_ref.shape[1]
    rows = scaled_ref.shape[0] // len(weights)
    occ, pb, trial = (
        jnp.concatenate([ref[:, at] for ref in cols_refs], axis=0)
        for at in (slice(nocc), slice(nocc, nstates), slice(nstates, nstates + nv))
    )
    g_occ = lax.dot_general(scaled_ref[:, :nocc], occ, NT, preferred_element_type=jnp.float32)
    g_un = lax.dot_general(scaled_ref[:, nocc:], pb, NT, preferred_element_type=jnp.float32)
    each = [slice(k * rows, (k + 1) * rows) for k in range(len(weights))]
    chi = jnp.concatenate([(w * g_occ[at] * g_un[at]).astype(jnp.bfloat16) for w, at in zip(weights, each)], axis=0)
    terms = jnp.dot(chi, trial, preferred_element_type=jnp.float32)
    return functools.reduce(jnp.add, [terms[at] for at in each])


def join_kernel(*refs):
    *part_refs, joined_ref = refs
    at = 0
    for ref in part_refs:
        joined_ref[at : at + ref.shape[0], :] = ref[...]
        at += ref.shape[0]


def scale_kernel(ntau, block_ref, times_ref, energy_ref, scaled_ref):
    scale(block_ref, times_in([times_ref], ntau)[0], energy_ref, scaled_ref)


def far_kernel(ntau, nocc, nv, block_ref, times_ref, more_times_ref, energy_ref, seen_ref, *refs):
    cols_refs, (total_ref, scaled_ref) = refs[:-2], refs[-2:]
    nseen = seen_ref.shape[0]
    scaled_ref[:nseen, :] = seen_ref[...]
    scale(block_ref, times_in([more_times_ref], ntau)[0], energy_ref, scaled_ref.at[nseen:])
    total_ref[...] = respond(scaled_ref, times_in([times_ref, more_times_ref], ntau)[1], nocc, nv, cols_refs)


def own_kernel(ntau, nocc, nv, block_ref, times_ref, more_times_ref, energy_ref, *refs):
    cols_refs, (total_ref, scaled_ref) = refs[:-2], refs[-2:]
    points, weights = times_in([times_ref, more_times_ref], ntau)
    scale(block_ref, points, energy_ref, scaled_ref)
    total_ref[...] = respond(scaled_ref, weights, nocc, nv, cols_refs)


def call(kernel, outs, args, name, cost, scratch=()):
    return pl.pallas_call(
        kernel,
        out_shape=outs,
        in_specs=[VMEM] * len(args),
        out_specs=jax.tree.map(lambda _: VMEM, outs),
        scratch_shapes=scratch,
        compiler_params=PARAMS,
        cost_estimate=pl.CostEstimate(flops=cost, bytes_accessed=10**6, transcendentals=0),
        name=name,
    )(*args)


def local(sizes, occ_states, empty_states, mix_weights, slice_of_block, occ_energy, pb_energy, tau_points, tau_weights, trial):
    nrow, ncol, nplanes = sizes
    rows, nocc = occ_states.shape
    npb, nv = pb_energy.shape[0], trial.shape[1]
    ntau = tau_points.shape[0]
    plane_rows = plane_rows_of(ntau)
    width = nocc + npb + nv
    assert 6 * ntau <= rows

    nblocks, (nempty, per_slice) = slice_of_block.shape[0], mix_weights.shape
    operands = (slice_of_block, tau_points, tau_weights, mix_weights.T, empty_states, occ_states, trial)
    operands += (occ_energy, pb_energy)
    own, times, code, energy = pl.pallas_call(
        pack_kernel,
        out_shape=(
            jax.ShapeDtypeStruct((rows, width), jnp.bfloat16),
            jax.ShapeDtypeStruct((plane_rows, LANES), jnp.float32),
            jax.ShapeDtypeStruct((rows, LANES), jnp.bfloat16),
            jax.ShapeDtypeStruct((1, nocc + npb), jnp.float32),
        ),
        in_specs=[pl.BlockSpec(memory_space=pl.ANY)] * len(operands),
        out_specs=(VMEM,) * 4,
        scratch_shapes=[
            pltpu.SMEM((nblocks,), jnp.int32),
            pltpu.SMEM((ntau,), jnp.float32),
            pltpu.SMEM((ntau,), jnp.float32),
            pltpu.VMEM((per_slice, nempty), jnp.float32),
            pltpu.VMEM((rows, nempty), jnp.bfloat16),
            pltpu.VMEM((nocc,), jnp.float32),
            pltpu.VMEM((npb,), jnp.float32),
            pltpu.SemaphoreType.DMA((len(operands),)),
            *[pltpu.VMEM((npb, rows), jnp.float32)] * (LANES * nblocks // nempty),
        ],
        compiler_params=PARAMS,
        name="pack",
    )(*[pltpu.with_memory_space_constraint(operand, pltpu.HBM) for operand in operands])

    col_bits, row_bits = bits_of(ncol), bits_of(nrow)
    (core_bit, x_bit), col_bit, far_bit = row_bits[:2], col_bits[0], col_bits[-1]
    base = own
    for bit in col_bits[1:-1]:
        base = jnp.concatenate([base, swap(base, "col", ncol, bit)])
    for bit in row_bits[2:]:
        base = jnp.concatenate([base, swap(base, "row", nrow, bit)])
    nbase = base.shape[0]

    far = swap(own[:, : nocc + npb], "col", ncol, far_bit)
    beside = swap(base, "row", nrow, core_bit)
    index = lambda r, c, t: (r * ncol + c) * nplanes + t
    places = [(r, c, t) for r in range(nrow) for c in range(ncol) for t in range(nplanes)]
    across = lax.ppermute(
        base, ("row", "col", "tau"), [(index(r, c, t), index(r ^ x_bit, c ^ col_bit, t)) for r, c, t in places]
    )
    across_beside = swap(across, "row", nrow, core_bit)
    mixed = lax.ppermute(
        jnp.concatenate([jnp.concatenate([base, beside]), jnp.tile(code, (2 * base.shape[0] // rows, 1))], axis=1),
        ("row", "col", "tau"),
        [
            (index(r, c, t), index(r ^ x_bit, c, t ^ 1) if r & core_bit else index(r, c ^ col_bit, t))
            for r, c, t in places
        ],
    )
    early = (base, beside, across)
    joined = jax.ShapeDtypeStruct((sum(part.shape[0] for part in early), width), jnp.bfloat16)
    early = call(join_kernel, joined, early, "join", JOIN_COST)
    early, mixed = lax.optimization_barrier((early, mixed))
    far, across_beside = lax.optimization_barrier((far, across_beside))
    traded = swap(mixed, "row", nrow, core_bit)
    cols = (early, across_beside, mixed, traded)

    parts = jnp.where(
        lax.axis_index("row") & core_bit == 0, traded[: 6 * ntau, width:], mixed[: 6 * ntau, width:]
    ).astype(jnp.float32)
    parts = [parts[j * ntau : (j + 1) * ntau] for j in range(6)]
    padding = jnp.zeros((plane_rows - 2 * ntau, LANES), jnp.float32)
    more_times = jnp.concatenate([parts[0] + parts[1] + parts[2], parts[3] + parts[4] + parts[5], padding])
    for bit in bits_of(nplanes)[1:]:
        more_times = jnp.concatenate([more_times, swap(jnp.concatenate([times, more_times]), "tau", nplanes, bit)])

    scaled_of = lambda planes: jax.ShapeDtypeStruct((planes * ntau * rows, nocc + npb), jnp.bfloat16)
    total_of = jax.ShapeDtypeStruct((rows, nv), jnp.float32)
    scratch = [pltpu.VMEM(scaled_of(nplanes).shape, jnp.bfloat16)]
    scaled = call(functools.partial(scale_kernel, ntau), scaled_of(1), (far, times, energy), "scale", SCALE_COST)
    far_total = call(
        functools.partial(far_kernel, ntau, nocc, nv),
        total_of,
        (far, times, more_times, energy, scaled, *cols),
        "far",
        KERNEL_COST,
        scratch,
    )
    total = call(
        functools.partial(own_kernel, ntau, nocc, nv),
        total_of,
        (own, times, more_times, energy, *cols),
        "own",
        KERNEL_COST,
        scratch,
    )
    return swap(far_total, "col", ncol, far_bit) + total


def solution(mesh):
    points = P(("col", "row"), None)
    in_specs = (points, points, P(), P(), P(), P(), P("tau"), P("tau"), points)
    sizes = tuple(mesh.shape[axis] for axis in ("row", "col", "tau"))
    return jax.shard_map(
        functools.partial(local, sizes), mesh=mesh, in_specs=in_specs, out_specs=points, check_vma=False
    )
```

time: 19.4 us -> 19.1 us (0.985)
  waiting for transfers between devices: 3.41 us -> 5.24 us
  starting transfers between devices: 11.8 us -> 10.2 us
  Pallas kernels: 3.4 us -> 2.67 us
    ppermute x7 -> x5, starting transfers between devices: 11.8 us -> 6.13 us  [swap(): return lax.ppermute(block, axis, [(i, i ^ bit) for i in range(size)])]
    ppermute x0 -> x2, starting transfers between devices: none -> 4.09 us  [the longest x1 3.58 us: local(): lax.ppermute(base, ('row', 'col', 'tau'), [(index(r, c, t), index(r ^ x_b...]
    ppermute x0 -> x2, waiting for transfers between devices: none -> 2.24 us  [the longest x1 2.23 us: local(): lax.ppermute(jnp.concatenate([jnp.concatenate([base, beside]), jnp.tile(c...]
    pallas_call x4, Pallas kernels: 1.88 us -> 1.11 us  [call(): pl.pallas_call(kernel, out_shape=outs, in_specs=[VMEM] * len(args), out_s...]
    ppermute x7 -> x5, waiting for transfers between devices: 3.41 us -> 3 us  [swap(): return lax.ppermute(block, axis, [(i, i ^ bit) for i in range(size)])]
    add x1 -> x2, other arithmetic: 0.61 us -> 0.62 us  [the longest x1 0.61 us: local(): return swap(far_total, 'col', ncol, far_bit) + total]
  transfers between devices with their start and end apart: 7 -> 7, of which waited for: 5 -> 4; matrix products, arithmetic and copies ran while one was open for 0% -> 1% of each run, Pallas kernels for 8% -> 3%
where the time goes in v5:
time: 19.1 us; the launch traced here: 19 us
  starting transfers between devices  10.2 us (53%)
  waiting for transfers between devices  5.24 us (27%)
  Pallas kernels  2.67 us (14%)
  other arithmetic  0.71 us (4%)
    ppermute x5, starting transfers between devices, swap(): return lax.ppermute(block, axis, [(i, i ^ bit) for i in range(size)])  6.13 us
    ppermute x1, starting transfers between devices, local(): lax.ppermute(base, ('row', 'col', 'tau'), [(index(r, c, t), index(r ^ x_b...  3.58 us
    ppermute x5, waiting for transfers between devices, swap(): return lax.ppermute(block, axis, [(i, i ^ bit) for i in range(size)])  3 us
    ppermute x1, waiting for transfers between devices, local(): lax.ppermute(jnp.concatenate([jnp.concatenate([base, beside]), jnp.tile(c...  2.23 us
    pallas_call x1, Pallas kernels, local(): pl.pallas_call(pack_kernel, out_shape=(jax.ShapeDtypeStruct((rows, width)...  1.56 us
    pallas_call x4, Pallas kernels, call(): pl.pallas_call(kernel, out_shape=outs, in_specs=[VMEM] * len(args), out_s...  1.11 us
    add x1, other arithmetic, local(): return swap(far_total, 'col', ncol, far_bit) + total  0.61 us
    ppermute x1, starting transfers between devices, local(): lax.ppermute(jnp.concatenate([jnp.concatenate([base, beside]), jnp.tile(c...  0.51 us
  transfers between devices with their start and end apart: 7, of which 4 were waited for; matrix products, arithmetic and copies ran while one was open for 1% of the time, Pallas kernels for 3%

profile of v5, /device:TPU:0, one launch (start us, length us, event | category | flops | bytes accessed | tf_op | source)
XLA Modules:
  0.0 19.0 jit_solution(14338969470059272877)
XLA Ops:
  0.0 1.6 %pack.1 = (bf16[32,1024]{1,0:T(8,128)(2,1)S(1)}, f32[8,128]{1,0:T(8,128)S(1)}, bf16[32,128]{1,0:T(8,128)(2,1)S(1)}, f32[1,896]{1,0:T(1,128)S(1)}) custom-call(s32[128]{0:T(128)} %slice_hbm.1, f32[3]{0:T(128)} %tau_hbm.1, f32[3]{0:T(128)} %weight_hbm.1, f32[16,4096]{1,0:T(8,128)} %bitcast.2, bf16[32,4096]{1,0:T(8,128)(2,1)} %empty_hbm.1, ...), custom_call_target="tpu_custom_call" | custom-call | tf_op jit(solution)/shard_map/pack/pallas_call | solution.py:173
  1.6 0.5 %collective-permute-start.3 = (bf16[32,1024]{1,0:T(8,128)(2,1)S(1)}, bf16[32,1024]{1,0:T(8,128)(2,1)S(1)}, u32[]{:S(2)}, u32[]{:S(2)}) collective-permute-start(bf16[32,1024]{1,0:T(8,128)(2,1)S(1)} %get-tuple-element.13.refs_0_.block_ref), channel_id=1, source_target_pairs={{0,8},{8,0},{16,24},{24,16},{1,9},{9,1},{17,25},{25,17},{2,10},{10... | collective-permute-start | bytes 196616 | tf_op jit(solution)/shard_map/ppermute | solution.py:24
  2.1 3.6 %collective-permute-start.1 = (bf16[32,1024]{1,0:T(8,128)(2,1)S(1)}, bf16[32,1024]{1,0:T(8,128)(2,1)S(1)}, u32[]{:S(2)}, u32[]{:S(2)}) collective-permute-start(bf16[32,1024]{1,0:T(8,128)(2,1)S(1)} %get-tuple-element.13.refs_0_.block_ref), channel_id=1, source_target_pairs={{0,18},{1,19},{2,16},{3,17},{4,22},{5,23},{6,20},{7,21},{8,26},{9,... | collective-permute-start | bytes 196616 | tf_op jit(solution)/shard_map/ppermute | solution.py:211
  5.7 0.0 collective-permute-done.3.refs_1_
  5.7 0.5 %collective-permute-start.4 = (bf16[64,1152]{1,0:T(8,128)(2,1)S(1)}, bf16[64,1152]{1,0:T(8,128)(2,1)S(1)}, u32[]{:S(2)}, u32[]{:S(2)}) collective-permute-start(bf16[64,1152]{1,0:T(8,128)(2,1)S(1)} %pad_maximum_fusion), channel_id=1, source_target_pairs={{0,2},{1,3},{2,0},{3,1},{4,6},{5,7},{6,4},{7,5},{8,25},{9,24},{10,... | collective-permute-start | bytes 442376 | tf_op jit(solution)/shard_map/ppermute | solution.py:215
  6.2 2.6 %collective-permute-start = (bf16[32,896]{1,0:T(8,128)(2,1)S(1)}, bf16[32,896]{1,0:T(8,128)(2,1)S(1)}, u32[]{:S(2)}, u32[]{:S(2)}) collective-permute-start(bf16[32,896]{1,0:T(8,128)(2,1)S(1)} %slice.27), channel_id=1, source_target_pairs={{0,4},{2,6},{4,0},{6,2},{1,5},{3,7},{5,1},{7,3},{8,12},{10,14},{12... | collective-permute-start | bytes 172040 | tf_op jit(solution)/shard_map/ppermute | solution.py:24
  8.8 0.0 collective-permute-done.1.refs_2_
  8.8 0.7 %collective-permute-start.2 = (bf16[32,1024]{1,0:T(8,128)(2,1)S(1)}, bf16[32,1024]{1,0:T(8,128)(2,1)S(1)}, u32[]{:S(2)}, u32[]{:S(2)}) collective-permute-start(bf16[32,1024]{1,0:T(8,128)(2,1)S(1)} %collective-permute-done.1.refs_2_), channel_id=1, source_target_pairs={{0,8},{8,0},{16,24},{24,16},{1,9},{9,1},{17,25},{25,17},{2,10},{10... | collective-permute-start | bytes 196616 | tf_op jit(solution)/shard_map/ppermute | solution.py:24
  9.5 2.2 %collective-permute-done.4.refs_2_ = bf16[64,1152]{1,0:T(8,128)(2,1)S(1)} collective-permute-done((bf16[64,1152]{1,0:T(8,128)(2,1)S(1)}, bf16[64,1152]{1,0:T(8,128)(2,1)S(1)}, u32[]{:S(2)}, u32[]{:S(2)}) %collective-permute-start.4) | collective-permute-done | bytes 147488 | tf_op jit(solution)/shard_map/ppermute | solution.py:215
  11.7 0.0 collective-permute-start.5
  11.7 0.1 pad.2.clone
  11.8 0.7 %collective-permute-done.block_ref = bf16[32,896]{1,0:T(8,128)(2,1)S(1)} collective-permute-done((bf16[32,896]{1,0:T(8,128)(2,1)S(1)}, bf16[32,896]{1,0:T(8,128)(2,1)S(1)}, u32[]{:S(2)}, u32[]{:S(2)}) %collective-permute-start) | collective-permute-done | bytes 57376 | tf_op jit(solution)/shard_map/ppermute | solution.py:24
  12.5 0.0 collective-permute-done.2.refs_1_
  12.5 0.1 scale.1.seen_ref
  12.6 0.5 %collective-permute-done.5.refs_3_ = bf16[64,1152]{1,0:T(8,128)(2,1)S(1)} collective-permute-done((bf16[64,1152]{1,0:T(8,128)(2,1)S(1)}, bf16[64,1152]{1,0:T(8,128)(2,1)S(1)}, u32[]{:S(2)}, u32[]{:S(2)}) %collective-permute-start.5) | collective-permute-done | bytes 147488 | tf_op jit(solution)/shard_map/ppermute | solution.py:24
  13.1 0.1 maximum_maximum_fusion.more_times_ref
  13.2 0.5 %far.1 = f32[32,128]{1,0:T(8,128)S(1)} custom-call(bf16[32,896]{1,0:T(8,128)(2,1)S(1)} %collective-permute-done.block_ref, f32[8,128]{1,0:T(8,128)S(1)} %get-tuple-element.15.times_ref, f32[8,128]{1,0:T(8,128)S(1)} %maximum_maximum_fusion.more_times_ref, f32[1,896]{1,0:T(1,128)S(1)} %get-tuple-element.18.energy_ref, bf16[96,896]{1,0:T(8,128)(2,1)S(1)} %scale.1.seen_ref, ...), custom_call_target="tpu_custom_call" | custom-call | flops 1000000000 | bytes 1000000 | tf_op jit(solution)/shard_map/far/pallas_call | solution.py:149
  13.7 2.4 %collective-permute-start.6 = (f32[32,128]{1,0:T(8,128)S(1)}, f32[32,128]{1,0:T(8,128)S(1)}, u32[]{:S(2)}, u32[]{:S(2)}) collective-permute-start(f32[32,128]{1,0:T(8,128)S(1)} %far.1), channel_id=1, source_target_pairs={{0,4},{2,6},{4,0},{6,2},{1,5},{3,7},{5,1},{7,3},{8,12},{10,14},{12... | collective-permute-start | bytes 49160 | tf_op jit(solution)/shard_map/ppermute | solution.py:24
  16.0 0.5 %own.1 = f32[32,128]{1,0:T(8,128)S(1)} custom-call(bf16[32,1024]{1,0:T(8,128)(2,1)S(1)} %get-tuple-element.13.refs_0_.block_ref, f32[8,128]{1,0:T(8,128)S(1)} %get-tuple-element.15.times_ref, f32[8,128]{1,0:T(8,128)S(1)} %maximum_maximum_fusion.more_times_ref, f32[1,896]{1,0:T(1,128)S(1)} %get-tuple-element.18.energy_ref, bf16[96,1024]{1,0:T(8,128)(2,1)S(1)} %join.1.refs_0_, ...), custom_call_target="tpu_custom_call" | custom-call | flops 1000000000 | bytes 1000000 | tf_op jit(solution)/shard_map/own/pallas_call | solution.py:149
  16.5 1.8 %collective-permute-done.6 = f32[32,128]{1,0:T(8,128)S(1)} collective-permute-done((f32[32,128]{1,0:T(8,128)S(1)}, f32[32,128]{1,0:T(8,128)S(1)}, u32[]{:S(2)}, u32[]{:S(2)}) %collective-permute-start.6) | collective-permute-done | bytes 16416 | tf_op jit(solution)/shard_map/ppermute | solution.py:24
  18.4 0.6 %add.19 = f32[32,128]{1,0:T(8,128)} add(f32[32,128]{1,0:T(8,128)S(1)} %collective-permute-done.6, f32[32,128]{1,0:T(8,128)S(1)} %own.1) | non-fusion elementwise | flops 4096 | bytes 49152 | tf_op jit(solution)/shard_map/add | solution.py:260
  (7 shorter events, 0.1 us)
Async XLA Ops:
  1.6 4.1 %collective-permute-start.3 = (bf16[32,1024]{1,0:T(8,128)(2,1)S(1)}, bf16[32,1024]{1,0:T(8,128)(2,1)S(1)}, u32[]{:S(2)}, u32[]{:S(2)}) collective-permute-start(bf16[32,1024]{1,0:T(8,128)(2,1)S(1)} %get-tuple-element.13.refs_0_.block_ref), channel_id=1, source_target_pairs={{0,8},{8,0},{16,24},{24,16},{1,9},{9,1},{17,25},{25,17},{2,10},{10... | collective-permute-start | bytes 196616 | tf_op jit(solution)/shard_map/ppermute | solution.py:24
  2.1 6.7 %collective-permute-start.1 = (bf16[32,1024]{1,0:T(8,128)(2,1)S(1)}, bf16[32,1024]{1,0:T(8,128)(2,1)S(1)}, u32[]{:S(2)}, u32[]{:S(2)}) collective-permute-start(bf16[32,1024]{1,0:T(8,128)(2,1)S(1)} %get-tuple-element.13.refs_0_.block_ref), channel_id=1, source_target_pairs={{0,18},{1,19},{2,16},{3,17},{4,22},{5,23},{6,20},{7,21},{8,26},{9,... | collective-permute-start | bytes 196616 | tf_op jit(solution)/shard_map/ppermute | solution.py:211
  5.7 6.0 %collective-permute-start.4 = (bf16[64,1152]{1,0:T(8,128)(2,1)S(1)}, bf16[64,1152]{1,0:T(8,128)(2,1)S(1)}, u32[]{:S(2)}, u32[]{:S(2)}) collective-permute-start(bf16[64,1152]{1,0:T(8,128)(2,1)S(1)} %pad_maximum_fusion), channel_id=1, source_target_pairs={{0,2},{1,3},{2,0},{3,1},{4,6},{5,7},{6,4},{7,5},{8,25},{9,24},{10,... | collective-permute-start | bytes 442376 | tf_op jit(solution)/shard_map/ppermute | solution.py:215
  6.2 6.3 %collective-permute-start = (bf16[32,896]{1,0:T(8,128)(2,1)S(1)}, bf16[32,896]{1,0:T(8,128)(2,1)S(1)}, u32[]{:S(2)}, u32[]{:S(2)}) collective-permute-start(bf16[32,896]{1,0:T(8,128)(2,1)S(1)} %slice.27), channel_id=1, source_target_pairs={{0,4},{2,6},{4,0},{6,2},{1,5},{3,7},{5,1},{7,3},{8,12},{10,14},{12... | collective-permute-start | bytes 172040 | tf_op jit(solution)/shard_map/ppermute | solution.py:24
  8.8 3.7 %collective-permute-start.2 = (bf16[32,1024]{1,0:T(8,128)(2,1)S(1)}, bf16[32,1024]{1,0:T(8,128)(2,1)S(1)}, u32[]{:S(2)}, u32[]{:S(2)}) collective-permute-start(bf16[32,1024]{1,0:T(8,128)(2,1)S(1)} %collective-permute-done.1.refs_2_), channel_id=1, source_target_pairs={{0,8},{8,0},{16,24},{24,16},{1,9},{9,1},{17,25},{25,17},{2,10},{10... | collective-permute-start | bytes 196616 | tf_op jit(solution)/shard_map/ppermute | solution.py:24
  11.7 1.4 %collective-permute-start.5 = (bf16[64,1152]{1,0:T(8,128)(2,1)S(1)}, bf16[64,1152]{1,0:T(8,128)(2,1)S(1)}, u32[]{:S(2)}, u32[]{:S(2)}) collective-permute-start(bf16[64,1152]{1,0:T(8,128)(2,1)S(1)} %collective-permute-done.4.refs_2_), channel_id=1, source_target_pairs={{0,8},{8,0},{16,24},{24,16},{1,9},{9,1},{17,25},{25,17},{2,10},{10... | collective-permute-start | bytes 442376 | tf_op jit(solution)/shard_map/ppermute | solution.py:24
  13.7 4.7 %collective-permute-start.6 = (f32[32,128]{1,0:T(8,128)S(1)}, f32[32,128]{1,0:T(8,128)S(1)}, u32[]{:S(2)}, u32[]{:S(2)}) collective-permute-start(f32[32,128]{1,0:T(8,128)S(1)} %far.1), channel_id=1, source_target_pairs={{0,4},{2,6},{4,0},{6,2},{1,5},{3,7},{5,1},{7,3},{8,12},{10,14},{12... | collective-permute-start | bytes 49160 | tf_op jit(solution)/shard_map/ppermute | solution.py:24

commit v6 on v5

--- a/solution.py
+++ b/solution.py
@@ -78,16 +78,17 @@
     energy_ref[:, :nocc] = occ_energy_ref[...][None, :]
     energy_ref[:, nocc:] = -pb_energy_ref[...][None, :]
     ntau = tau_ref.shape[0]
-    code_ref[...] = jnp.zeros_like(code_ref)
+    row = lax.broadcasted_iota(jnp.int32, code_ref.shape, 0)
+    code = jnp.zeros(code_ref.shape, jnp.float32)
     for k in range(ntau):
         for i, ref in enumerate((tau_ref, weight_ref)):
             rest = jnp.full((1, LANES), ref[k], jnp.float32)
             times_ref[i * ntau + k : i * ntau + k + 1, :] = rest
             for j in range(3):
-                part = rest.astype(jnp.bfloat16)
-                row = (3 * i + j) * ntau + k
-                code_ref[row : row + 1, :] = part
-                rest = rest - part.astype(jnp.float32)
+                part = rest.astype(jnp.bfloat16).astype(jnp.float32)
+                code = jnp.where(row == (3 * i + j) * ntau + k, part, code)
+                rest = rest - part
+    code_ref[...] = code.astype(jnp.bfloat16)
 
 
 def times_in(times_refs, ntau):
@@ -113,9 +114,8 @@
     g_occ = lax.dot_general(scaled_ref[:, :nocc], occ, NT, preferred_element_type=jnp.float32)
     g_un = lax.dot_general(scaled_ref[:, nocc:], pb, NT, preferred_element_type=jnp.float32)
     each = [slice(k * rows, (k + 1) * rows) for k in range(len(weights))]
-    chi = jnp.concatenate([(w * g_occ[at] * g_un[at]).astype(jnp.bfloat16) for w, at in zip(weights, each)], axis=0)
-    terms = jnp.dot(chi, trial, preferred_element_type=jnp.float32)
-    return functools.reduce(jnp.add, [terms[at] for at in each])
+    chi = jnp.concatenate([(w * g_occ[at] * g_un[at]).astype(jnp.bfloat16) for w, at in zip(weights, each)], axis=1)
+    return jnp.dot(chi, jnp.concatenate([trial] * len(weights), axis=0), preferred_element_type=jnp.float32)
 
 
 def join_kernel(*refs):

time: 19.1 us -> 19.1 us (level)
  no operation moved by 1% of the time
where the time goes in v6:
time: 19.1 us; the launch traced here: 18.9 us
  starting transfers between devices  10.2 us (53%)
  waiting for transfers between devices  5.28 us (28%)
  Pallas kernels  2.56 us (13%)
  other arithmetic  0.71 us (4%)
    ppermute x5, starting transfers between devices, swap(): return lax.ppermute(block, axis, [(i, i ^ bit) for i in range(size)])  6.14 us
    ppermute x1, starting transfers between devices, local(): lax.ppermute(base, ('row', 'col', 'tau'), [(index(r, c, t), index(r ^ x_b...  3.58 us
    ppermute x5, waiting for transfers between devices, swap(): return lax.ppermute(block, axis, [(i, i ^ bit) for i in range(size)])  3.05 us
    ppermute x1, waiting for transfers between devices, local(): lax.ppermute(jnp.concatenate([jnp.concatenate([base, beside]), jnp.tile(c...  2.23 us
    pallas_call x1, Pallas kernels, local(): pl.pallas_call(pack_kernel, out_shape=(jax.ShapeDtypeStruct((rows, width)...  1.55 us
    pallas_call x4, Pallas kernels, call(): pl.pallas_call(kernel, out_shape=outs, in_specs=[VMEM] * len(args), out_s...  1.02 us
    add x1, other arithmetic, local(): return swap(far_total, 'col', ncol, far_bit) + total  0.61 us
    ppermute x1, starting transfers between devices, local(): lax.ppermute(jnp.concatenate([jnp.concatenate([base, beside]), jnp.tile(c...  0.51 us
  transfers between devices with their start and end apart: 7, of which 4 were waited for; matrix products, arithmetic and copies ran while one was open for 1% of the time, Pallas kernels for 3%

profile of v6, /device:TPU:0, one launch (start us, length us, event | category | flops | bytes accessed | tf_op | source)
XLA Modules:
  0.0 18.9 jit_solution(15200178265738151110)
XLA Ops:
  0.0 1.5 %pack.1 = (bf16[32,1024]{1,0:T(8,128)(2,1)S(1)}, f32[8,128]{1,0:T(8,128)S(1)}, bf16[32,128]{1,0:T(8,128)(2,1)S(1)}, f32[1,896]{1,0:T(1,128)S(1)}) custom-call(s32[128]{0:T(128)} %slice_hbm.1, f32[3]{0:T(128)} %tau_hbm.1, f32[3]{0:T(128)} %weight_hbm.1, f32[16,4096]{1,0:T(8,128)} %bitcast.2, bf16[32,4096]{1,0:T(8,128)(2,1)} %empty_hbm.1, ...), custom_call_target="tpu_custom_call" | custom-call | tf_op jit(solution)/shard_map/pack/pallas_call | solution.py:173
  1.6 0.5 %collective-permute-start.3 = (bf16[32,1024]{1,0:T(8,128)(2,1)S(1)}, bf16[32,1024]{1,0:T(8,128)(2,1)S(1)}, u32[]{:S(2)}, u32[]{:S(2)}) collective-permute-start(bf16[32,1024]{1,0:T(8,128)(2,1)S(1)} %get-tuple-element.13.refs_0_.block_ref), channel_id=1, source_target_pairs={{0,8},{8,0},{16,24},{24,16},{1,9},{9,1},{17,25},{25,17},{2,10},{10... | collective-permute-start | bytes 196616 | tf_op jit(solution)/shard_map/ppermute | solution.py:24
  2.1 3.6 %collective-permute-start.1 = (bf16[32,1024]{1,0:T(8,128)(2,1)S(1)}, bf16[32,1024]{1,0:T(8,128)(2,1)S(1)}, u32[]{:S(2)}, u32[]{:S(2)}) collective-permute-start(bf16[32,1024]{1,0:T(8,128)(2,1)S(1)} %get-tuple-element.13.refs_0_.block_ref), channel_id=1, source_target_pairs={{0,18},{1,19},{2,16},{3,17},{4,22},{5,23},{6,20},{7,21},{8,26},{9,... | collective-permute-start | bytes 196616 | tf_op jit(solution)/shard_map/ppermute | solution.py:211
  5.7 0.0 collective-permute-done.3.refs_1_
  5.7 0.5 %collective-permute-start.4 = (bf16[64,1152]{1,0:T(8,128)(2,1)S(1)}, bf16[64,1152]{1,0:T(8,128)(2,1)S(1)}, u32[]{:S(2)}, u32[]{:S(2)}) collective-permute-start(bf16[64,1152]{1,0:T(8,128)(2,1)S(1)} %pad_maximum_fusion), channel_id=1, source_target_pairs={{0,2},{1,3},{2,0},{3,1},{4,6},{5,7},{6,4},{7,5},{8,25},{9,24},{10,... | collective-permute-start | bytes 442376 | tf_op jit(solution)/shard_map/ppermute | solution.py:215
  6.2 2.6 %collective-permute-start = (bf16[32,896]{1,0:T(8,128)(2,1)S(1)}, bf16[32,896]{1,0:T(8,128)(2,1)S(1)}, u32[]{:S(2)}, u32[]{:S(2)}) collective-permute-start(bf16[32,896]{1,0:T(8,128)(2,1)S(1)} %slice.27), channel_id=1, source_target_pairs={{0,4},{2,6},{4,0},{6,2},{1,5},{3,7},{5,1},{7,3},{8,12},{10,14},{12... | collective-permute-start | bytes 172040 | tf_op jit(solution)/shard_map/ppermute | solution.py:24
  8.8 0.0 collective-permute-done.1.refs_2_
  8.8 0.7 %collective-permute-start.2 = (bf16[32,1024]{1,0:T(8,128)(2,1)S(1)}, bf16[32,1024]{1,0:T(8,128)(2,1)S(1)}, u32[]{:S(2)}, u32[]{:S(2)}) collective-permute-start(bf16[32,1024]{1,0:T(8,128)(2,1)S(1)} %collective-permute-done.1.refs_2_), channel_id=1, source_target_pairs={{0,8},{8,0},{16,24},{24,16},{1,9},{9,1},{17,25},{25,17},{2,10},{10... | collective-permute-start | bytes 196616 | tf_op jit(solution)/shard_map/ppermute | solution.py:24
  9.5 2.2 %collective-permute-done.4.refs_2_ = bf16[64,1152]{1,0:T(8,128)(2,1)S(1)} collective-permute-done((bf16[64,1152]{1,0:T(8,128)(2,1)S(1)}, bf16[64,1152]{1,0:T(8,128)(2,1)S(1)}, u32[]{:S(2)}, u32[]{:S(2)}) %collective-permute-start.4) | collective-permute-done | bytes 147488 | tf_op jit(solution)/shard_map/ppermute | solution.py:215
  11.7 0.0 collective-permute-start.5
  11.7 0.1 pad.2.clone
  11.8 0.7 %collective-permute-done.block_ref = bf16[32,896]{1,0:T(8,128)(2,1)S(1)} collective-permute-done((bf16[32,896]{1,0:T(8,128)(2,1)S(1)}, bf16[32,896]{1,0:T(8,128)(2,1)S(1)}, u32[]{:S(2)}, u32[]{:S(2)}) %collective-permute-start) | collective-permute-done | bytes 57376 | tf_op jit(solution)/shard_map/ppermute | solution.py:24
  12.5 0.0 collective-permute-done.2.refs_1_
  12.5 0.1 scale.1.seen_ref
  12.6 0.5 %collective-permute-done.5.refs_3_ = bf16[64,1152]{1,0:T(8,128)(2,1)S(1)} collective-permute-done((bf16[64,1152]{1,0:T(8,128)(2,1)S(1)}, bf16[64,1152]{1,0:T(8,128)(2,1)S(1)}, u32[]{:S(2)}, u32[]{:S(2)}) %collective-permute-start.5) | collective-permute-done | bytes 147488 | tf_op jit(solution)/shard_map/ppermute | solution.py:24
  13.1 0.1 maximum_maximum_fusion.more_times_ref
  13.2 0.4 %far.1 = f32[32,128]{1,0:T(8,128)S(1)} custom-call(bf16[32,896]{1,0:T(8,128)(2,1)S(1)} %collective-permute-done.block_ref, f32[8,128]{1,0:T(8,128)S(1)} %get-tuple-element.15.times_ref, f32[8,128]{1,0:T(8,128)S(1)} %maximum_maximum_fusion.more_times_ref, f32[1,896]{1,0:T(1,128)S(1)} %get-tuple-element.18.energy_ref, bf16[96,896]{1,0:T(8,128)(2,1)S(1)} %scale.1.seen_ref, ...), custom_call_target="tpu_custom_call" | custom-call | flops 1000000000 | bytes 1000000 | tf_op jit(solution)/shard_map/far/pallas_call | solution.py:149
  13.6 2.4 %collective-permute-start.6 = (f32[32,128]{1,0:T(8,128)S(1)}, f32[32,128]{1,0:T(8,128)S(1)}, u32[]{:S(2)}, u32[]{:S(2)}) collective-permute-start(f32[32,128]{1,0:T(8,128)S(1)} %far.1), channel_id=1, source_target_pairs={{0,4},{2,6},{4,0},{6,2},{1,5},{3,7},{5,1},{7,3},{8,12},{10,14},{12... | collective-permute-start | bytes 49160 | tf_op jit(solution)/shard_map/ppermute | solution.py:24
  16.0 0.5 %own.1 = f32[32,128]{1,0:T(8,128)S(1)} custom-call(bf16[32,1024]{1,0:T(8,128)(2,1)S(1)} %get-tuple-element.13.refs_0_.block_ref, f32[8,128]{1,0:T(8,128)S(1)} %get-tuple-element.15.times_ref, f32[8,128]{1,0:T(8,128)S(1)} %maximum_maximum_fusion.more_times_ref, f32[1,896]{1,0:T(1,128)S(1)} %get-tuple-element.18.energy_ref, bf16[96,1024]{1,0:T(8,128)(2,1)S(1)} %join.1.refs_0_, ...), custom_call_target="tpu_custom_call" | custom-call | flops 1000000000 | bytes 1000000 | tf_op jit(solution)/shard_map/own/pallas_call | solution.py:149
  16.4 1.9 %collective-permute-done.6 = f32[32,128]{1,0:T(8,128)S(1)} collective-permute-done((f32[32,128]{1,0:T(8,128)S(1)}, f32[32,128]{1,0:T(8,128)S(1)}, u32[]{:S(2)}, u32[]{:S(2)}) %collective-permute-start.6) | collective-permute-done | bytes 16416 | tf_op jit(solution)/shard_map/ppermute | solution.py:24
  18.3 0.6 %add.19 = f32[32,128]{1,0:T(8,128)} add(f32[32,128]{1,0:T(8,128)S(1)} %collective-permute-done.6, f32[32,128]{1,0:T(8,128)S(1)} %own.1) | non-fusion elementwise | flops 4096 | bytes 49152 | tf_op jit(solution)/shard_map/add | solution.py:260
  (7 shorter events, 0.1 us)
Async XLA Ops:
  1.6 4.1 %collective-permute-start.3 = (bf16[32,1024]{1,0:T(8,128)(2,1)S(1)}, bf16[32,1024]{1,0:T(8,128)(2,1)S(1)}, u32[]{:S(2)}, u32[]{:S(2)}) collective-permute-start(bf16[32,1024]{1,0:T(8,128)(2,1)S(1)} %get-tuple-element.13.refs_0_.block_ref), channel_id=1, source_target_pairs={{0,8},{8,0},{16,24},{24,16},{1,9},{9,1},{17,25},{25,17},{2,10},{10... | collective-permute-start | bytes 196616 | tf_op jit(solution)/shard_map/ppermute | solution.py:24
  2.1 6.7 %collective-permute-start.1 = (bf16[32,1024]{1,0:T(8,128)(2,1)S(1)}, bf16[32,1024]{1,0:T(8,128)(2,1)S(1)}, u32[]{:S(2)}, u32[]{:S(2)}) collective-permute-start(bf16[32,1024]{1,0:T(8,128)(2,1)S(1)} %get-tuple-element.13.refs_0_.block_ref), channel_id=1, source_target_pairs={{0,18},{1,19},{2,16},{3,17},{4,22},{5,23},{6,20},{7,21},{8,26},{9,... | collective-permute-start | bytes 196616 | tf_op jit(solution)/shard_map/ppermute | solution.py:211
  5.7 6.0 %collective-permute-start.4 = (bf16[64,1152]{1,0:T(8,128)(2,1)S(1)}, bf16[64,1152]{1,0:T(8,128)(2,1)S(1)}, u32[]{:S(2)}, u32[]{:S(2)}) collective-permute-start(bf16[64,1152]{1,0:T(8,128)(2,1)S(1)} %pad_maximum_fusion), channel_id=1, source_target_pairs={{0,2},{1,3},{2,0},{3,1},{4,6},{5,7},{6,4},{7,5},{8,25},{9,24},{10,... | collective-permute-start | bytes 442376 | tf_op jit(solution)/shard_map/ppermute | solution.py:215
  6.2 6.3 %collective-permute-start = (bf16[32,896]{1,0:T(8,128)(2,1)S(1)}, bf16[32,896]{1,0:T(8,128)(2,1)S(1)}, u32[]{:S(2)}, u32[]{:S(2)}) collective-permute-start(bf16[32,896]{1,0:T(8,128)(2,1)S(1)} %slice.27), channel_id=1, source_target_pairs={{0,4},{2,6},{4,0},{6,2},{1,5},{3,7},{5,1},{7,3},{8,12},{10,14},{12... | collective-permute-start | bytes 172040 | tf_op jit(solution)/shard_map/ppermute | solution.py:24
  8.8 3.7 %collective-permute-start.2 = (bf16[32,1024]{1,0:T(8,128)(2,1)S(1)}, bf16[32,1024]{1,0:T(8,128)(2,1)S(1)}, u32[]{:S(2)}, u32[]{:S(2)}) collective-permute-start(bf16[32,1024]{1,0:T(8,128)(2,1)S(1)} %collective-permute-done.1.refs_2_), channel_id=1, source_target_pairs={{0,8},{8,0},{16,24},{24,16},{1,9},{9,1},{17,25},{25,17},{2,10},{10... | collective-permute-start | bytes 196616 | tf_op jit(solution)/shard_map/ppermute | solution.py:24
  11.7 1.4 %collective-permute-start.5 = (bf16[64,1152]{1,0:T(8,128)(2,1)S(1)}, bf16[64,1152]{1,0:T(8,128)(2,1)S(1)}, u32[]{:S(2)}, u32[]{:S(2)}) collective-permute-start(bf16[64,1152]{1,0:T(8,128)(2,1)S(1)} %collective-permute-done.4.refs_2_), channel_id=1, source_target_pairs={{0,8},{8,0},{16,24},{24,16},{1,9},{9,1},{17,25},{25,17},{2,10},{10... | collective-permute-start | bytes 442376 | tf_op jit(solution)/shard_map/ppermute | solution.py:24
  13.6 4.7 %collective-permute-start.6 = (f32[32,128]{1,0:T(8,128)S(1)}, f32[32,128]{1,0:T(8,128)S(1)}, u32[]{:S(2)}, u32[]{:S(2)}) collective-permute-start(f32[32,128]{1,0:T(8,128)S(1)} %far.1), channel_id=1, source_target_pairs={{0,4},{2,6},{4,0},{6,2},{1,5},{3,7},{5,1},{7,3},{8,12},{10,14},{12... | collective-permute-start | bytes 49160 | tf_op jit(solution)/shard_map/ppermute | solution.py:24

commit v7 on v6

--- a/solution.py
+++ b/solution.py
@@ -9,7 +9,7 @@
 
 LANES = 128
 KERNEL_COST = 10**9
-SCALE_COST = 10**9
+SCALE_COST = 2 * 10**9
 JOIN_COST = 10**9
 VMEM = pl.BlockSpec(memory_space=pltpu.VMEM)
 PARAMS = pltpu.CompilerParams(vmem_limit_bytes=48 * 1024 * 1024)
@@ -30,7 +30,7 @@
 
 def pack_kernel(
     slice_hbm, tau_hbm, weight_hbm, mix_hbm, empty_hbm, occ_hbm, trial_hbm, occ_energy_hbm, pb_energy_hbm,
-    packed_ref, times_ref, code_ref, energy_ref,
+    packed_ref, times_ref, energy_ref,
     slice_ref, tau_ref, weight_ref, mix_ref, empty_ref, occ_energy_ref, pb_energy_ref, sems, *partial_refs,
 ):
     nocc = occ_hbm.shape[1]
@@ -78,17 +78,9 @@
     energy_ref[:, :nocc] = occ_energy_ref[...][None, :]
     energy_ref[:, nocc:] = -pb_energy_ref[...][None, :]
     ntau = tau_ref.shape[0]
-    row = lax.broadcasted_iota(jnp.int32, code_ref.shape, 0)
-    code = jnp.zeros(code_ref.shape, jnp.float32)
     for k in range(ntau):
-        for i, ref in enumerate((tau_ref, weight_ref)):
-            rest = jnp.full((1, LANES), ref[k], jnp.float32)
-            times_ref[i * ntau + k : i * ntau + k + 1, :] = rest
-            for j in range(3):
-                part = rest.astype(jnp.bfloat16).astype(jnp.float32)
-                code = jnp.where(row == (3 * i + j) * ntau + k, part, code)
-                rest = rest - part
-    code_ref[...] = code.astype(jnp.bfloat16)
+        times_ref[k : k + 1, :] = jnp.full((1, LANES), tau_ref[k], jnp.float32)
+        times_ref[ntau + k : ntau + k + 1, :] = jnp.full((1, LANES), weight_ref[k], jnp.float32)
 
 
 def times_in(times_refs, ntau):
@@ -104,12 +96,12 @@
         scaled_ref[k * rows : (k + 1) * rows, :] = (states * jnp.exp(energy * point)).astype(jnp.bfloat16)
 
 
-def respond(scaled_ref, weights, nocc, nv, cols_refs):
+def respond(scaled_ref, weights, nocc, cols_refs):
     nstates = scaled_ref.shape[1]
     rows = scaled_ref.shape[0] // len(weights)
     occ, pb, trial = (
         jnp.concatenate([ref[:, at] for ref in cols_refs], axis=0)
-        for at in (slice(nocc), slice(nocc, nstates), slice(nstates, nstates + nv))
+        for at in (slice(nocc), slice(nocc, nstates), slice(nstates, None))
     )
     g_occ = lax.dot_general(scaled_ref[:, :nocc], occ, NT, preferred_element_type=jnp.float32)
     g_un = lax.dot_general(scaled_ref[:, nocc:], pb, NT, preferred_element_type=jnp.float32)
@@ -126,23 +118,20 @@
         at += ref.shape[0]
 
 
-def scale_kernel(ntau, block_ref, times_ref, energy_ref, scaled_ref):
-    scale(block_ref, times_in([times_ref], ntau)[0], energy_ref, scaled_ref)
-
-
-def far_kernel(ntau, nocc, nv, block_ref, times_ref, more_times_ref, energy_ref, seen_ref, *refs):
-    cols_refs, (total_ref, scaled_ref) = refs[:-2], refs[-2:]
-    nseen = seen_ref.shape[0]
-    scaled_ref[:nseen, :] = seen_ref[...]
-    scale(block_ref, times_in([more_times_ref], ntau)[0], energy_ref, scaled_ref.at[nseen:])
-    total_ref[...] = respond(scaled_ref, times_in([times_ref, more_times_ref], ntau)[1], nocc, nv, cols_refs)
-
-
-def own_kernel(ntau, nocc, nv, block_ref, times_ref, more_times_ref, energy_ref, *refs):
+def scale_kernel(ntau, block_ref, times_ref, more_times_ref, energy_ref, scaled_ref):
+    scale(block_ref, times_in([times_ref, more_times_ref], ntau)[0], energy_ref, scaled_ref)
+
+
+def respond_kernel(ntau, nocc, times_ref, more_times_ref, scaled_ref, *refs):
+    cols_refs, total_ref = refs[:-1], refs[-1]
+    total_ref[...] = respond(scaled_ref, times_in([times_ref, more_times_ref], ntau)[1], nocc, cols_refs)
+
+
+def whole_kernel(ntau, nocc, block_ref, times_ref, more_times_ref, energy_ref, *refs):
     cols_refs, (total_ref, scaled_ref) = refs[:-2], refs[-2:]
     points, weights = times_in([times_ref, more_times_ref], ntau)
     scale(block_ref, points, energy_ref, scaled_ref)
-    total_ref[...] = respond(scaled_ref, weights, nocc, nv, cols_refs)
+    total_ref[...] = respond(scaled_ref, weights, nocc, cols_refs)
 
 
 def call(kernel, outs, args, name, cost, scratch=()):
@@ -165,21 +154,19 @@
     ntau = tau_points.shape[0]
     plane_rows = plane_rows_of(ntau)
     width = nocc + npb + nv
-    assert 6 * ntau <= rows
 
     nblocks, (nempty, per_slice) = slice_of_block.shape[0], mix_weights.shape
     operands = (slice_of_block, tau_points, tau_weights, mix_weights.T, empty_states, occ_states, trial)
     operands += (occ_energy, pb_energy)
-    own, times, code, energy = pl.pallas_call(
+    own, times, energy = pl.pallas_call(
         pack_kernel,
         out_shape=(
             jax.ShapeDtypeStruct((rows, width), jnp.bfloat16),
             jax.ShapeDtypeStruct((plane_rows, LANES), jnp.float32),
-            jax.ShapeDtypeStruct((rows, LANES), jnp.bfloat16),
             jax.ShapeDtypeStruct((1, nocc + npb), jnp.float32),
         ),
         in_specs=[pl.BlockSpec(memory_space=pl.ANY)] * len(operands),
-        out_specs=(VMEM,) * 4,
+        out_specs=(VMEM,) * 3,
         scratch_shapes=[
             pltpu.SMEM((nblocks,), jnp.int32),
             pltpu.SMEM((ntau,), jnp.float32),
@@ -204,58 +191,42 @@
         base = jnp.concatenate([base, swap(base, "row", nrow, bit)])
     nbase = base.shape[0]
 
-    far = swap(own[:, : nocc + npb], "col", ncol, far_bit)
+    far = swap(own, "col", ncol, far_bit)
     beside = swap(base, "row", nrow, core_bit)
-    index = lambda r, c, t: (r * ncol + c) * nplanes + t
-    places = [(r, c, t) for r in range(nrow) for c in range(ncol) for t in range(nplanes)]
-    across = lax.ppermute(
-        base, ("row", "col", "tau"), [(index(r, c, t), index(r ^ x_bit, c ^ col_bit, t)) for r, c, t in places]
-    )
+    index = lambda r, c: r * ncol + c
+    places = [(r, c) for r in range(nrow) for c in range(ncol)]
+    across = lax.ppermute(base, ("row", "col"), [(index(r, c), index(r ^ x_bit, c ^ col_bit)) for r, c in places])
     across_beside = swap(across, "row", nrow, core_bit)
     mixed = lax.ppermute(
-        jnp.concatenate([jnp.concatenate([base, beside]), jnp.tile(code, (2 * base.shape[0] // rows, 1))], axis=1),
-        ("row", "col", "tau"),
-        [
-            (index(r, c, t), index(r ^ x_bit, c, t ^ 1) if r & core_bit else index(r, c ^ col_bit, t))
-            for r, c, t in places
-        ],
-    )
+        jnp.concatenate([base, beside]),
+        ("row", "col"),
+        [(index(r, c), index(r ^ x_bit, c) if (r // core_bit + 1) % 2 else index(r, c ^ col_bit)) for r, c in places],
+    )
+    others = []
+    for bit in bits_of(nplanes):
+        others.append(swap(jnp.concatenate([times, *others]), "tau", nplanes, bit))
+    more_times = jnp.concatenate(others)
+
+    scaled_of = jax.ShapeDtypeStruct((nplanes * ntau * rows, nocc + npb), jnp.bfloat16)
+    total_of = jax.ShapeDtypeStruct((rows, nv), jnp.float32)
     early = (base, beside, across)
     joined = jax.ShapeDtypeStruct((sum(part.shape[0] for part in early), width), jnp.bfloat16)
     early = call(join_kernel, joined, early, "join", JOIN_COST)
     early, mixed = lax.optimization_barrier((early, mixed))
-    far, across_beside = lax.optimization_barrier((far, across_beside))
-    traded = swap(mixed, "row", nrow, core_bit)
-    cols = (early, across_beside, mixed, traded)
-
-    parts = jnp.where(
-        lax.axis_index("row") & core_bit == 0, traded[: 6 * ntau, width:], mixed[: 6 * ntau, width:]
-    ).astype(jnp.float32)
-    parts = [parts[j * ntau : (j + 1) * ntau] for j in range(6)]
-    padding = jnp.zeros((plane_rows - 2 * ntau, LANES), jnp.float32)
-    more_times = jnp.concatenate([parts[0] + parts[1] + parts[2], parts[3] + parts[4] + parts[5], padding])
-    for bit in bits_of(nplanes)[1:]:
-        more_times = jnp.concatenate([more_times, swap(jnp.concatenate([times, more_times]), "tau", nplanes, bit)])
-
-    scaled_of = lambda planes: jax.ShapeDtypeStruct((planes * ntau * rows, nocc + npb), jnp.bfloat16)
-    total_of = jax.ShapeDtypeStruct((rows, nv), jnp.float32)
-    scratch = [pltpu.VMEM(scaled_of(nplanes).shape, jnp.bfloat16)]
-    scaled = call(functools.partial(scale_kernel, ntau), scaled_of(1), (far, times, energy), "scale", SCALE_COST)
+    cols = (early, across_beside, mixed, swap(mixed, "row", nrow, core_bit))
+    scaled = call(
+        functools.partial(scale_kernel, ntau), scaled_of, (far, times, more_times, energy), "scale", SCALE_COST
+    )
     far_total = call(
-        functools.partial(far_kernel, ntau, nocc, nv),
-        total_of,
-        (far, times, more_times, energy, scaled, *cols),
-        "far",
-        KERNEL_COST,
-        scratch,
+        functools.partial(respond_kernel, ntau, nocc), total_of, (times, more_times, scaled, *cols), "far", KERNEL_COST
     )
     total = call(
-        functools.partial(own_kernel, ntau, nocc, nv),
+        functools.partial(whole_kernel, ntau, nocc),
         total_of,
         (own, times, more_times, energy, *cols),
         "own",
         KERNEL_COST,
-        scratch,
+        [pltpu.VMEM(scaled_of.shape, jnp.bfloat16)],
     )
     return swap(far_total, "col", ncol, far_bit) + total
 

time: 19.1 us -> 18.5 us (0.969)
  waiting for transfers between devices: 5.28 us -> 3.94 us
  starting transfers between devices: 10.2 us -> 11.2 us
    ppermute x2, waiting for transfers between devices: 2.24 us -> 0.3 us  [the longest x1 0.3 us: local(): lax.ppermute(jnp.concatenate([base, beside]), ('row', 'col'), [(index(r,...]
    ppermute x5 -> x6, starting transfers between devices: 6.14 us -> 7 us  [swap(): return lax.ppermute(block, axis, [(i, i ^ bit) for i in range(size)])]
    ppermute x5 -> x6, waiting for transfers between devices: 3.05 us -> 3.64 us  [swap(): return lax.ppermute(block, axis, [(i, i ^ bit) for i in range(size)])]
  transfers between devices with their start and end apart: 7 -> 8, of which waited for: 4 -> 3; matrix products, arithmetic and copies ran while one was open for 1% -> 0% of each run, Pallas kernels for 3% -> 3%
where the time goes in v7:
time: 18.5 us; the launch traced here: 18.4 us
  starting transfers between devices  11.2 us (61%)
  waiting for transfers between devices  3.94 us (21%)
  Pallas kernels  2.58 us (14%)
  other arithmetic  0.62 us (3%)
    ppermute x6, starting transfers between devices, swap(): return lax.ppermute(block, axis, [(i, i ^ bit) for i in range(size)])  7 us
    ppermute x6, waiting for transfers between devices, swap(): return lax.ppermute(block, axis, [(i, i ^ bit) for i in range(size)])  3.64 us
    ppermute x1, starting transfers between devices, local(): lax.ppermute(base, ('row', 'col'), [(index(r, c), index(r ^ x_bit, c ^ co...  3.58 us
    pallas_call x1, Pallas kernels, local(): pl.pallas_call(pack_kernel, out_shape=(jax.ShapeDtypeStruct((rows, width)...  1.53 us
    pallas_call x4, Pallas kernels, call(): pl.pallas_call(kernel, out_shape=outs, in_specs=[VMEM] * len(args), out_s...  1.04 us
    add x1, other arithmetic, local(): return swap(far_total, 'col', ncol, far_bit) + total  0.61 us
    ppermute x1, starting transfers between devices, local(): lax.ppermute(jnp.concatenate([base, beside]), ('row', 'col'), [(index(r,...  0.6 us
  transfers between devices with their start and end apart: 8, of which 3 were waited for; matrix products, arithmetic and copies ran while one was open for 0% of the time, Pallas kernels for 3%

profile of v7, /device:TPU:0, one launch (start us, length us, event | category | flops | bytes accessed | tf_op | source)
XLA Modules:
  0.0 18.4 jit_solution(5355217491802037107)
XLA Ops:
  0.0 1.5 %pack.1 = (bf16[32,1024]{1,0:T(8,128)(2,1)S(1)}, f32[8,128]{1,0:T(8,128)S(1)}, f32[1,896]{1,0:T(1,128)S(1)}) custom-call(s32[128]{0:T(128)} %slice_hbm.1, f32[3]{0:T(128)} %tau_hbm.1, f32[3]{0:T(128)} %weight_hbm.1, f32[16,4096]{1,0:T(8,128)} %bitcast.1, bf16[32,4096]{1,0:T(8,128)(2,1)} %empty_hbm.1, bf16[32,512]{1,0:T(8,128)(2,1)} %occ_hbm.1, ...), custom_call_target="tpu_custom_call" | custom-call | tf_op jit(solution)/shard_map/pack/pallas_call | solution.py:161
  1.5 0.5 %collective-permute-start.2 = (bf16[32,1024]{1,0:T(8,128)(2,1)S(1)}, bf16[32,1024]{1,0:T(8,128)(2,1)S(1)}, u32[]{:S(2)}, u32[]{:S(2)}) collective-permute-start(bf16[32,1024]{1,0:T(8,128)(2,1)S(1)} %get-tuple-element.11.refs_0_.block_ref), channel_id=1, source_target_pairs={{0,8},{8,0},{16,24},{24,16},{1,9},{9,1},{17,25},{25,17},{2,10},{10... | collective-permute-start | bytes 196616 | tf_op jit(solution)/shard_map/ppermute | solution.py:24
  2.1 3.6 %collective-permute-start.3 = (bf16[32,1024]{1,0:T(8,128)(2,1)S(1)}, bf16[32,1024]{1,0:T(8,128)(2,1)S(1)}, u32[]{:S(2)}, u32[]{:S(2)}) collective-permute-start(bf16[32,1024]{1,0:T(8,128)(2,1)S(1)} %get-tuple-element.11.refs_0_.block_ref), channel_id=1, source_target_pairs={{0,18},{2,16},{4,22},{6,20},{8,26},{10,24},{12,30},{14,28},{16,2},... | collective-permute-start | bytes 196616 | tf_op jit(solution)/shard_map/ppermute | solution.py:198
  5.6 0.0 collective-permute-done.2.refs_1_
  5.7 0.6 %collective-permute-start.4 = (bf16[64,1024]{1,0:T(8,128)(2,1)S(1)}, bf16[64,1024]{1,0:T(8,128)(2,1)S(1)}, u32[]{:S(2)}, u32[]{:S(2)}) collective-permute-start(bf16[64,1024]{1,0:T(8,128)(2,1)S(1)} %pad_maximum_fusion), channel_id=1, source_target_pairs={{0,16},{2,18},{4,20},{6,22},{8,10},{10,8},{12,14},{14,12},{16,0},{... | collective-permute-start | bytes 393224 | tf_op jit(solution)/shard_map/ppermute | solution.py:200
  6.3 2.6 %collective-permute-start.1 = (bf16[32,1024]{1,0:T(8,128)(2,1)S(1)}, bf16[32,1024]{1,0:T(8,128)(2,1)S(1)}, u32[]{:S(2)}, u32[]{:S(2)}) collective-permute-start(bf16[32,1024]{1,0:T(8,128)(2,1)S(1)} %get-tuple-element.11.refs_0_.block_ref), channel_id=1, source_target_pairs={{0,4},{2,6},{4,0},{6,2},{1,5},{3,7},{5,1},{7,3},{8,12},{10,14},{12... | collective-permute-start | bytes 196616 | tf_op jit(solution)/shard_map/ppermute | solution.py:24
  8.8 1.5 %collective-permute-start = (f32[8,128]{1,0:T(8,128)S(1)}, f32[8,128]{1,0:T(8,128)S(1)}, u32[]{:S(2)}, u32[]{:S(2)}) collective-permute-start(f32[8,128]{1,0:T(8,128)S(1)} %get-tuple-element.10.times_ref), channel_id=1, source_target_pairs={{0,1},{1,0},{2,3},{3,2},{4,5},{5,4},{6,7},{7,6},{8,9},{9,8},{10,11... | collective-permute-start | bytes 12296 | tf_op jit(solution)/shard_map/ppermute | solution.py:24
  10.4 0.0 collective-permute-done.3.refs_2_
  10.4 0.0 collective-permute-start.5
  10.4 0.3 %collective-permute-done.4.refs_2_ = bf16[64,1024]{1,0:T(8,128)(2,1)S(1)} collective-permute-done((bf16[64,1024]{1,0:T(8,128)(2,1)S(1)}, bf16[64,1024]{1,0:T(8,128)(2,1)S(1)}, u32[]{:S(2)}, u32[]{:S(2)}) %collective-permute-start.4) | collective-permute-done | bytes 131104 | tf_op jit(solution)/shard_map/ppermute | solution.py:200
  10.7 0.3 %collective-permute-start.6 = (bf16[64,1024]{1,0:T(8,128)(2,1)S(1)}, bf16[64,1024]{1,0:T(8,128)(2,1)S(1)}, u32[]{:S(2)}, u32[]{:S(2)}) collective-permute-start(bf16[64,1024]{1,0:T(8,128)(2,1)S(1)} %collective-permute-done.4.refs_2_), channel_id=1, source_target_pairs={{0,8},{8,0},{16,24},{24,16},{1,9},{9,1},{17,25},{25,17},{2,10},{10... | collective-permute-start | bytes 393224 | tf_op jit(solution)/shard_map/ppermute | solution.py:24
  11.0 1.5 %collective-permute-done.more_times_ref = f32[8,128]{1,0:T(8,128)S(1)} collective-permute-done((f32[8,128]{1,0:T(8,128)S(1)}, f32[8,128]{1,0:T(8,128)S(1)}, u32[]{:S(2)}, u32[]{:S(2)}) %collective-permute-start) | collective-permute-done | bytes 4128 | tf_op jit(solution)/shard_map/ppermute | solution.py:24
  12.5 0.0 collective-permute-done.1.block_ref
  12.5 0.1 scale.1.scaled_ref
  12.6 0.0 collective-permute-done.5.refs_1_
  12.6 0.0 collective-permute-done.6.refs_3_
  12.6 0.4 %far.1 = f32[32,128]{1,0:T(8,128)S(1)} custom-call(f32[8,128]{1,0:T(8,128)S(1)} %get-tuple-element.10.times_ref, f32[8,128]{1,0:T(8,128)S(1)} %collective-permute-done.more_times_ref, bf16[192,896]{1,0:T(8,128)(2,1)S(1)} %scale.1.scaled_ref, bf16[96,1024]{1,0:T(8,128)(2,1)S(1)} %join.1.refs_0_, bf16[32,1024]{1,0:T(8,128)(2,1)S(1)} %collective-permute-done.5.refs_1_, ...), custom_call_target="tpu_custom_call" | custom-call | flops 1000000000 | bytes 1000000 | tf_op jit(solution)/shard_map/far/pallas_call | solution.py:138
  13.1 2.1 %collective-permute-start.7 = (f32[32,128]{1,0:T(8,128)S(1)}, f32[32,128]{1,0:T(8,128)S(1)}, u32[]{:S(2)}, u32[]{:S(2)}) collective-permute-start(f32[32,128]{1,0:T(8,128)S(1)} %far.1), channel_id=1, source_target_pairs={{0,4},{2,6},{4,0},{6,2},{1,5},{3,7},{5,1},{7,3},{8,12},{10,14},{12... | collective-permute-start | bytes 49160 | tf_op jit(solution)/shard_map/ppermute | solution.py:24
  15.1 0.5 %own.1 = f32[32,128]{1,0:T(8,128)S(1)} custom-call(bf16[32,1024]{1,0:T(8,128)(2,1)S(1)} %get-tuple-element.11.refs_0_.block_ref, f32[8,128]{1,0:T(8,128)S(1)} %get-tuple-element.10.times_ref, f32[8,128]{1,0:T(8,128)S(1)} %collective-permute-done.more_times_ref, f32[1,896]{1,0:T(1,128)S(1)} %get-tuple-element.12.energy_ref, ...), custom_call_target="tpu_custom_call" | custom-call | flops 1000000000 | bytes 1000000 | tf_op jit(solution)/shard_map/own/pallas_call | solution.py:138
  15.6 2.2 %collective-permute-done.7 = f32[32,128]{1,0:T(8,128)S(1)} collective-permute-done((f32[32,128]{1,0:T(8,128)S(1)}, f32[32,128]{1,0:T(8,128)S(1)}, u32[]{:S(2)}, u32[]{:S(2)}) %collective-permute-start.7) | collective-permute-done | bytes 16416 | tf_op jit(solution)/shard_map/ppermute | solution.py:24
  17.8 0.6 %add.3 = f32[32,128]{1,0:T(8,128)} add(f32[32,128]{1,0:T(8,128)S(1)} %collective-permute-done.7, f32[32,128]{1,0:T(8,128)S(1)} %own.1) | non-fusion elementwise | flops 4096 | bytes 49152 | tf_op jit(solution)/shard_map/add | solution.py:231
  (2 shorter events, 0.0 us)
Async XLA Ops:
  1.5 4.1 %collective-permute-start.2 = (bf16[32,1024]{1,0:T(8,128)(2,1)S(1)}, bf16[32,1024]{1,0:T(8,128)(2,1)S(1)}, u32[]{:S(2)}, u32[]{:S(2)}) collective-permute-start(bf16[32,1024]{1,0:T(8,128)(2,1)S(1)} %get-tuple-element.11.refs_0_.block_ref), channel_id=1, source_target_pairs={{0,8},{8,0},{16,24},{24,16},{1,9},{9,1},{17,25},{25,17},{2,10},{10... | collective-permute-start | bytes 196616 | tf_op jit(solution)/shard_map/ppermute | solution.py:24
  2.1 8.3 %collective-permute-start.3 = (bf16[32,1024]{1,0:T(8,128)(2,1)S(1)}, bf16[32,1024]{1,0:T(8,128)(2,1)S(1)}, u32[]{:S(2)}, u32[]{:S(2)}) collective-permute-start(bf16[32,1024]{1,0:T(8,128)(2,1)S(1)} %get-tuple-element.11.refs_0_.block_ref), channel_id=1, source_target_pairs={{0,18},{2,16},{4,22},{6,20},{8,26},{10,24},{12,30},{14,28},{16,2},... | collective-permute-start | bytes 196616 | tf_op jit(solution)/shard_map/ppermute | solution.py:198
  5.7 5.0 %collective-permute-start.4 = (bf16[64,1024]{1,0:T(8,128)(2,1)S(1)}, bf16[64,1024]{1,0:T(8,128)(2,1)S(1)}, u32[]{:S(2)}, u32[]{:S(2)}) collective-permute-start(bf16[64,1024]{1,0:T(8,128)(2,1)S(1)} %pad_maximum_fusion), channel_id=1, source_target_pairs={{0,16},{2,18},{4,20},{6,22},{8,10},{10,8},{12,14},{14,12},{16,0},{... | collective-permute-start | bytes 393224 | tf_op jit(solution)/shard_map/ppermute | solution.py:200
  6.3 6.2 %collective-permute-start.1 = (bf16[32,1024]{1,0:T(8,128)(2,1)S(1)}, bf16[32,1024]{1,0:T(8,128)(2,1)S(1)}, u32[]{:S(2)}, u32[]{:S(2)}) collective-permute-start(bf16[32,1024]{1,0:T(8,128)(2,1)S(1)} %get-tuple-element.11.refs_0_.block_ref), channel_id=1, source_target_pairs={{0,4},{2,6},{4,0},{6,2},{1,5},{3,7},{5,1},{7,3},{8,12},{10,14},{12... | collective-permute-start | bytes 196616 | tf_op jit(solution)/shard_map/ppermute | solution.py:24
  8.8 3.6 %collective-permute-start = (f32[8,128]{1,0:T(8,128)S(1)}, f32[8,128]{1,0:T(8,128)S(1)}, u32[]{:S(2)}, u32[]{:S(2)}) collective-permute-start(f32[8,128]{1,0:T(8,128)S(1)} %get-tuple-element.10.times_ref), channel_id=1, source_target_pairs={{0,1},{1,0},{2,3},{3,2},{4,5},{5,4},{6,7},{7,6},{8,9},{9,8},{10,11... | collective-permute-start | bytes 12296 | tf_op jit(solution)/shard_map/ppermute | solution.py:24
  10.4 2.2 %collective-permute-start.5 = (bf16[32,1024]{1,0:T(8,128)(2,1)S(1)}, bf16[32,1024]{1,0:T(8,128)(2,1)S(1)}, u32[]{:S(2)}, u32[]{:S(2)}) collective-permute-start(bf16[32,1024]{1,0:T(8,128)(2,1)S(1)} %collective-permute-done.3.refs_2_), channel_id=1, source_target_pairs={{0,8},{8,0},{16,24},{24,16},{1,9},{9,1},{17,25},{25,17},{2,10},{10... | collective-permute-start | bytes 196616 | tf_op jit(solution)/shard_map/ppermute | solution.py:24
  10.7 1.9 %collective-permute-start.6 = (bf16[64,1024]{1,0:T(8,128)(2,1)S(1)}, bf16[64,1024]{1,0:T(8,128)(2,1)S(1)}, u32[]{:S(2)}, u32[]{:S(2)}) collective-permute-start(bf16[64,1024]{1,0:T(8,128)(2,1)S(1)} %collective-permute-done.4.refs_2_), channel_id=1, source_target_pairs={{0,8},{8,0},{16,24},{24,16},{1,9},{9,1},{17,25},{25,17},{2,10},{10... | collective-permute-start | bytes 393224 | tf_op jit(solution)/shard_map/ppermute | solution.py:24
  13.1 4.7 %collective-permute-start.7 = (f32[32,128]{1,0:T(8,128)S(1)}, f32[32,128]{1,0:T(8,128)S(1)}, u32[]{:S(2)}, u32[]{:S(2)}) collective-permute-start(f32[32,128]{1,0:T(8,128)S(1)} %far.1), channel_id=1, source_target_pairs={{0,4},{2,6},{4,0},{6,2},{1,5},{3,7},{5,1},{7,3},{8,12},{10,14},{12... | collective-permute-start | bytes 49160 | tf_op jit(solution)/shard_map/ppermute | solution.py:24

commit v8 on v7

--- a/solution.py
+++ b/solution.py
@@ -200,7 +200,7 @@
     mixed = lax.ppermute(
         jnp.concatenate([base, beside]),
         ("row", "col"),
-        [(index(r, c), index(r ^ x_bit, c) if (r // core_bit + 1) % 2 else index(r, c ^ col_bit)) for r, c in places],
+        [(index(r, c), index(r ^ x_bit, c) if (r // core_bit + c // far_bit + 1) % 2 else index(r, c ^ col_bit)) for r, c in places],
     )
     others = []
     for bit in bits_of(nplanes):

time: 18.5 us -> 18.4 us (level)
  no operation moved by 1% of the time
where the time goes in v8:
time: 18.4 us; the launch traced here: 18.3 us
  starting transfers between devices  11.1 us (60%)
  waiting for transfers between devices  3.95 us (21%)
  Pallas kernels  2.58 us (14%)
  other arithmetic  0.62 us (3%)
    ppermute x6, starting transfers between devices, swap(): return lax.ppermute(block, axis, [(i, i ^ bit) for i in range(size)])  6.9 us
    ppermute x1, starting transfers between devices, local(): lax.ppermute(base, ('row', 'col'), [(index(r, c), index(r ^ x_bit, c ^ co...  3.58 us
    ppermute x6, waiting for transfers between devices, swap(): return lax.ppermute(block, axis, [(i, i ^ bit) for i in range(size)])  3.56 us
    pallas_call x1, Pallas kernels, local(): pl.pallas_call(pack_kernel, out_shape=(jax.ShapeDtypeStruct((rows, width)...  1.53 us
    pallas_call x4, Pallas kernels, call(): pl.pallas_call(kernel, out_shape=outs, in_specs=[VMEM] * len(args), out_s...  1.04 us
    add x1, other arithmetic, local(): return swap(far_total, 'col', ncol, far_bit) + total  0.61 us
    ppermute x1, starting transfers between devices, local(): lax.ppermute(jnp.concatenate([base, beside]), ('row', 'col'), [(index(r,...  0.6 us
    ppermute x1, waiting for transfers between devices, local(): lax.ppermute(jnp.concatenate([base, beside]), ('row', 'col'), [(index(r,...  0.38 us
  transfers between devices with their start and end apart: 8, of which 3 were waited for; matrix products, arithmetic and copies ran while one was open for 0% of the time, Pallas kernels for 3%

profile of v8, /device:TPU:0, one launch (start us, length us, event | category | flops | bytes accessed | tf_op | source)
XLA Modules:
  0.0 18.3 jit_solution(5301577834270734497)
XLA Ops:
  0.0 1.5 %pack.1 = (bf16[32,1024]{1,0:T(8,128)(2,1)S(1)}, f32[8,128]{1,0:T(8,128)S(1)}, f32[1,896]{1,0:T(1,128)S(1)}) custom-call(s32[128]{0:T(128)} %slice_hbm.1, f32[3]{0:T(128)} %tau_hbm.1, f32[3]{0:T(128)} %weight_hbm.1, f32[16,4096]{1,0:T(8,128)} %bitcast.1, bf16[32,4096]{1,0:T(8,128)(2,1)} %empty_hbm.1, bf16[32,512]{1,0:T(8,128)(2,1)} %occ_hbm.1, ...), custom_call_target="tpu_custom_call" | custom-call | tf_op jit(solution)/shard_map/pack/pallas_call | solution.py:161
  1.5 0.5 %collective-permute-start.2 = (bf16[32,1024]{1,0:T(8,128)(2,1)S(1)}, bf16[32,1024]{1,0:T(8,128)(2,1)S(1)}, u32[]{:S(2)}, u32[]{:S(2)}) collective-permute-start(bf16[32,1024]{1,0:T(8,128)(2,1)S(1)} %get-tuple-element.11.refs_0_.block_ref), channel_id=1, source_target_pairs={{0,8},{8,0},{16,24},{24,16},{1,9},{9,1},{17,25},{25,17},{2,10},{10... | collective-permute-start | bytes 196616 | tf_op jit(solution)/shard_map/ppermute | solution.py:24
  2.1 3.6 %collective-permute-start.3 = (bf16[32,1024]{1,0:T(8,128)(2,1)S(1)}, bf16[32,1024]{1,0:T(8,128)(2,1)S(1)}, u32[]{:S(2)}, u32[]{:S(2)}) collective-permute-start(bf16[32,1024]{1,0:T(8,128)(2,1)S(1)} %get-tuple-element.11.refs_0_.block_ref), channel_id=1, source_target_pairs={{0,18},{2,16},{4,22},{6,20},{8,26},{10,24},{12,30},{14,28},{16,2},... | collective-permute-start | bytes 196616 | tf_op jit(solution)/shard_map/ppermute | solution.py:198
  5.6 0.0 collective-permute-done.2.refs_1_
  5.7 0.6 %collective-permute-start.4 = (bf16[64,1024]{1,0:T(8,128)(2,1)S(1)}, bf16[64,1024]{1,0:T(8,128)(2,1)S(1)}, u32[]{:S(2)}, u32[]{:S(2)}) collective-permute-start(bf16[64,1024]{1,0:T(8,128)(2,1)S(1)} %pad_maximum_fusion), channel_id=1, source_target_pairs={{0,16},{2,18},{4,6},{6,4},{8,10},{10,8},{12,28},{14,30},{16,0},{18... | collective-permute-start | bytes 393224 | tf_op jit(solution)/shard_map/ppermute | solution.py:200
  6.3 2.5 %collective-permute-start.1 = (bf16[32,1024]{1,0:T(8,128)(2,1)S(1)}, bf16[32,1024]{1,0:T(8,128)(2,1)S(1)}, u32[]{:S(2)}, u32[]{:S(2)}) collective-permute-start(bf16[32,1024]{1,0:T(8,128)(2,1)S(1)} %get-tuple-element.11.refs_0_.block_ref), channel_id=1, source_target_pairs={{0,4},{2,6},{4,0},{6,2},{1,5},{3,7},{5,1},{7,3},{8,12},{10,14},{12... | collective-permute-start | bytes 196616 | tf_op jit(solution)/shard_map/ppermute | solution.py:24
  8.8 1.5 %collective-permute-start = (f32[8,128]{1,0:T(8,128)S(1)}, f32[8,128]{1,0:T(8,128)S(1)}, u32[]{:S(2)}, u32[]{:S(2)}) collective-permute-start(f32[8,128]{1,0:T(8,128)S(1)} %get-tuple-element.10.times_ref), channel_id=1, source_target_pairs={{0,1},{1,0},{2,3},{3,2},{4,5},{5,4},{6,7},{7,6},{8,9},{9,8},{10,11... | collective-permute-start | bytes 12296 | tf_op jit(solution)/shard_map/ppermute | solution.py:24
  10.3 0.0 collective-permute-done.3.refs_2_
  10.3 0.0 collective-permute-start.5
  10.3 0.4 %collective-permute-done.4.refs_2_ = bf16[64,1024]{1,0:T(8,128)(2,1)S(1)} collective-permute-done((bf16[64,1024]{1,0:T(8,128)(2,1)S(1)}, bf16[64,1024]{1,0:T(8,128)(2,1)S(1)}, u32[]{:S(2)}, u32[]{:S(2)}) %collective-permute-start.4) | collective-permute-done | bytes 131104 | tf_op jit(solution)/shard_map/ppermute | solution.py:200
  10.7 0.2 %collective-permute-start.6 = (bf16[64,1024]{1,0:T(8,128)(2,1)S(1)}, bf16[64,1024]{1,0:T(8,128)(2,1)S(1)}, u32[]{:S(2)}, u32[]{:S(2)}) collective-permute-start(bf16[64,1024]{1,0:T(8,128)(2,1)S(1)} %collective-permute-done.4.refs_2_), channel_id=1, source_target_pairs={{0,8},{8,0},{16,24},{24,16},{1,9},{9,1},{17,25},{25,17},{2,10},{10... | collective-permute-start | bytes 393224 | tf_op jit(solution)/shard_map/ppermute | solution.py:24
  10.9 1.5 %collective-permute-done.more_times_ref = f32[8,128]{1,0:T(8,128)S(1)} collective-permute-done((f32[8,128]{1,0:T(8,128)S(1)}, f32[8,128]{1,0:T(8,128)S(1)}, u32[]{:S(2)}, u32[]{:S(2)}) %collective-permute-start) | collective-permute-done | bytes 4128 | tf_op jit(solution)/shard_map/ppermute | solution.py:24
  12.4 0.0 collective-permute-done.1.block_ref
  12.4 0.1 scale.1.scaled_ref
  12.5 0.0 collective-permute-done.5.refs_1_
  12.5 0.0 collective-permute-done.6.refs_3_
  12.5 0.4 %far.1 = f32[32,128]{1,0:T(8,128)S(1)} custom-call(f32[8,128]{1,0:T(8,128)S(1)} %get-tuple-element.10.times_ref, f32[8,128]{1,0:T(8,128)S(1)} %collective-permute-done.more_times_ref, bf16[192,896]{1,0:T(8,128)(2,1)S(1)} %scale.1.scaled_ref, bf16[96,1024]{1,0:T(8,128)(2,1)S(1)} %join.1.refs_0_, bf16[32,1024]{1,0:T(8,128)(2,1)S(1)} %collective-permute-done.5.refs_1_, ...), custom_call_target="tpu_custom_call" | custom-call | flops 1000000000 | bytes 1000000 | tf_op jit(solution)/shard_map/far/pallas_call | solution.py:138
  13.0 2.2 %collective-permute-start.7 = (f32[32,128]{1,0:T(8,128)S(1)}, f32[32,128]{1,0:T(8,128)S(1)}, u32[]{:S(2)}, u32[]{:S(2)}) collective-permute-start(f32[32,128]{1,0:T(8,128)S(1)} %far.1), channel_id=1, source_target_pairs={{0,4},{2,6},{4,0},{6,2},{1,5},{3,7},{5,1},{7,3},{8,12},{10,14},{12... | collective-permute-start | bytes 49160 | tf_op jit(solution)/shard_map/ppermute | solution.py:24
  15.1 0.5 %own.1 = f32[32,128]{1,0:T(8,128)S(1)} custom-call(bf16[32,1024]{1,0:T(8,128)(2,1)S(1)} %get-tuple-element.11.refs_0_.block_ref, f32[8,128]{1,0:T(8,128)S(1)} %get-tuple-element.10.times_ref, f32[8,128]{1,0:T(8,128)S(1)} %collective-permute-done.more_times_ref, f32[1,896]{1,0:T(1,128)S(1)} %get-tuple-element.12.energy_ref, ...), custom_call_target="tpu_custom_call" | custom-call | flops 1000000000 | bytes 1000000 | tf_op jit(solution)/shard_map/own/pallas_call | solution.py:138
  15.6 2.1 %collective-permute-done.7 = f32[32,128]{1,0:T(8,128)S(1)} collective-permute-done((f32[32,128]{1,0:T(8,128)S(1)}, f32[32,128]{1,0:T(8,128)S(1)}, u32[]{:S(2)}, u32[]{:S(2)}) %collective-permute-start.7) | collective-permute-done | bytes 16416 | tf_op jit(solution)/shard_map/ppermute | solution.py:24
  17.7 0.6 %add.3 = f32[32,128]{1,0:T(8,128)} add(f32[32,128]{1,0:T(8,128)S(1)} %collective-permute-done.7, f32[32,128]{1,0:T(8,128)S(1)} %own.1) | non-fusion elementwise | flops 4096 | bytes 49152 | tf_op jit(solution)/shard_map/add | solution.py:231
  (2 shorter events, 0.0 us)
Async XLA Ops:
  1.5 4.1 %collective-permute-start.2 = (bf16[32,1024]{1,0:T(8,128)(2,1)S(1)}, bf16[32,1024]{1,0:T(8,128)(2,1)S(1)}, u32[]{:S(2)}, u32[]{:S(2)}) collective-permute-start(bf16[32,1024]{1,0:T(8,128)(2,1)S(1)} %get-tuple-element.11.refs_0_.block_ref), channel_id=1, source_target_pairs={{0,8},{8,0},{16,24},{24,16},{1,9},{9,1},{17,25},{25,17},{2,10},{10... | collective-permute-start | bytes 196616 | tf_op jit(solution)/shard_map/ppermute | solution.py:24
  2.1 8.2 %collective-permute-start.3 = (bf16[32,1024]{1,0:T(8,128)(2,1)S(1)}, bf16[32,1024]{1,0:T(8,128)(2,1)S(1)}, u32[]{:S(2)}, u32[]{:S(2)}) collective-permute-start(bf16[32,1024]{1,0:T(8,128)(2,1)S(1)} %get-tuple-element.11.refs_0_.block_ref), channel_id=1, source_target_pairs={{0,18},{2,16},{4,22},{6,20},{8,26},{10,24},{12,30},{14,28},{16,2},... | collective-permute-start | bytes 196616 | tf_op jit(solution)/shard_map/ppermute | solution.py:198
  5.7 5.0 %collective-permute-start.4 = (bf16[64,1024]{1,0:T(8,128)(2,1)S(1)}, bf16[64,1024]{1,0:T(8,128)(2,1)S(1)}, u32[]{:S(2)}, u32[]{:S(2)}) collective-permute-start(bf16[64,1024]{1,0:T(8,128)(2,1)S(1)} %pad_maximum_fusion), channel_id=1, source_target_pairs={{0,16},{2,18},{4,6},{6,4},{8,10},{10,8},{12,28},{14,30},{16,0},{18... | collective-permute-start | bytes 393224 | tf_op jit(solution)/shard_map/ppermute | solution.py:200
  6.3 6.1 %collective-permute-start.1 = (bf16[32,1024]{1,0:T(8,128)(2,1)S(1)}, bf16[32,1024]{1,0:T(8,128)(2,1)S(1)}, u32[]{:S(2)}, u32[]{:S(2)}) collective-permute-start(bf16[32,1024]{1,0:T(8,128)(2,1)S(1)} %get-tuple-element.11.refs_0_.block_ref), channel_id=1, source_target_pairs={{0,4},{2,6},{4,0},{6,2},{1,5},{3,7},{5,1},{7,3},{8,12},{10,14},{12... | collective-permute-start | bytes 196616 | tf_op jit(solution)/shard_map/ppermute | solution.py:24
  8.8 3.6 %collective-permute-start = (f32[8,128]{1,0:T(8,128)S(1)}, f32[8,128]{1,0:T(8,128)S(1)}, u32[]{:S(2)}, u32[]{:S(2)}) collective-permute-start(f32[8,128]{1,0:T(8,128)S(1)} %get-tuple-element.10.times_ref), channel_id=1, source_target_pairs={{0,1},{1,0},{2,3},{3,2},{4,5},{5,4},{6,7},{7,6},{8,9},{9,8},{10,11... | collective-permute-start | bytes 12296 | tf_op jit(solution)/shard_map/ppermute | solution.py:24
  10.3 2.2 %collective-permute-start.5 = (bf16[32,1024]{1,0:T(8,128)(2,1)S(1)}, bf16[32,1024]{1,0:T(8,128)(2,1)S(1)}, u32[]{:S(2)}, u32[]{:S(2)}) collective-permute-start(bf16[32,1024]{1,0:T(8,128)(2,1)S(1)} %collective-permute-done.3.refs_2_), channel_id=1, source_target_pairs={{0,8},{8,0},{16,24},{24,16},{1,9},{9,1},{17,25},{25,17},{2,10},{10... | collective-permute-start | bytes 196616 | tf_op jit(solution)/shard_map/ppermute | solution.py:24
  10.7 1.8 %collective-permute-start.6 = (bf16[64,1024]{1,0:T(8,128)(2,1)S(1)}, bf16[64,1024]{1,0:T(8,128)(2,1)S(1)}, u32[]{:S(2)}, u32[]{:S(2)}) collective-permute-start(bf16[64,1024]{1,0:T(8,128)(2,1)S(1)} %collective-permute-done.4.refs_2_), channel_id=1, source_target_pairs={{0,8},{8,0},{16,24},{24,16},{1,9},{9,1},{17,25},{25,17},{2,10},{10... | collective-permute-start | bytes 393224 | tf_op jit(solution)/shard_map/ppermute | solution.py:24
  13.0 4.7 %collective-permute-start.7 = (f32[32,128]{1,0:T(8,128)S(1)}, f32[32,128]{1,0:T(8,128)S(1)}, u32[]{:S(2)}, u32[]{:S(2)}) collective-permute-start(f32[32,128]{1,0:T(8,128)S(1)} %far.1), channel_id=1, source_target_pairs={{0,4},{2,6},{4,0},{6,2},{1,5},{3,7},{5,1},{7,3},{8,12},{10,14},{12... | collective-permute-start | bytes 49160 | tf_op jit(solution)/shard_map/ppermute | solution.py:24

commit v9 on v8

--- a/solution.py
+++ b/solution.py
@@ -30,7 +30,7 @@
 
 def pack_kernel(
     slice_hbm, tau_hbm, weight_hbm, mix_hbm, empty_hbm, occ_hbm, trial_hbm, occ_energy_hbm, pb_energy_hbm,
-    packed_ref, times_ref, energy_ref,
+    packed_ref, states_ref, times_ref, energy_ref,
     slice_ref, tau_ref, weight_ref, mix_ref, empty_ref, occ_energy_ref, pb_energy_ref, sems, *partial_refs,
 ):
     nocc = occ_hbm.shape[1]
@@ -75,6 +75,7 @@
     packed_ref[:, nocc : nocc + nbands] = pseudo.T.astype(jnp.bfloat16)
     for copy in copies[3:]:
         copy.wait()
+    states_ref[...] = packed_ref[:, : nocc + nbands]
     energy_ref[:, :nocc] = occ_energy_ref[...][None, :]
     energy_ref[:, nocc:] = -pb_energy_ref[...][None, :]
     ntau = tau_ref.shape[0]
@@ -158,15 +159,16 @@
     nblocks, (nempty, per_slice) = slice_of_block.shape[0], mix_weights.shape
     operands = (slice_of_block, tau_points, tau_weights, mix_weights.T, empty_states, occ_states, trial)
     operands += (occ_energy, pb_energy)
-    own, times, energy = pl.pallas_call(
+    own, states, times, energy = pl.pallas_call(
         pack_kernel,
         out_shape=(
             jax.ShapeDtypeStruct((rows, width), jnp.bfloat16),
+            jax.ShapeDtypeStruct((rows, nocc + npb), jnp.bfloat16),
             jax.ShapeDtypeStruct((plane_rows, LANES), jnp.float32),
             jax.ShapeDtypeStruct((1, nocc + npb), jnp.float32),
         ),
         in_specs=[pl.BlockSpec(memory_space=pl.ANY)] * len(operands),
-        out_specs=(VMEM,) * 3,
+        out_specs=(VMEM,) * 4,
         scratch_shapes=[
             pltpu.SMEM((nblocks,), jnp.int32),
             pltpu.SMEM((ntau,), jnp.float32),
@@ -191,7 +193,7 @@
         base = jnp.concatenate([base, swap(base, "row", nrow, bit)])
     nbase = base.shape[0]
 
-    far = swap(own, "col", ncol, far_bit)
+    far = swap(states, "col", ncol, far_bit)
     beside = swap(base, "row", nrow, core_bit)
     index = lambda r, c: r * ncol + c
     places = [(r, c) for r in range(nrow) for c in range(ncol)]
@@ -202,9 +204,10 @@
         ("row", "col"),
         [(index(r, c), index(r ^ x_bit, c) if (r // core_bit + c // far_bit + 1) % 2 else index(r, c ^ col_bit)) for r, c in places],
     )
+    sent_times, across = lax.optimization_barrier((times, across))
     others = []
     for bit in bits_of(nplanes):
-        others.append(swap(jnp.concatenate([times, *others]), "tau", nplanes, bit))
+        others.append(swap(jnp.concatenate([sent_times, *others]), "tau", nplanes, bit))
     more_times = jnp.concatenate(others)
 
     scaled_of = jax.ShapeDtypeStruct((nplanes * ntau * rows, nocc + npb), jnp.bfloat16)

time: 18.4 us -> 18.5 us (level)
  starting transfers between devices: 11.1 us -> 11.3 us
    ppermute x6, starting transfers between devices: 6.9 us -> 7.11 us  [swap(): return lax.ppermute(block, axis, [(i, i ^ bit) for i in range(size)])]
  transfers between devices with their start and end apart: 8 -> 8, of which waited for: 3 -> 4; matrix products, arithmetic and copies ran while one was open for 0% -> 0% of each run, Pallas kernels for 3% -> 3%
where the time goes in v9:
time: 18.5 us; the launch traced here: 18.3 us
  starting transfers between devices  11.3 us (61%)
  waiting for transfers between devices  3.79 us (20%)
  Pallas kernels  2.59 us (14%)
  other arithmetic  0.62 us (3%)
    ppermute x6, starting transfers between devices, swap(): return lax.ppermute(block, axis, [(i, i ^ bit) for i in range(size)])  7.11 us
    ppermute x1, starting transfers between devices, local(): lax.ppermute(base, ('row', 'col'), [(index(r, c), index(r ^ x_bit, c ^ co...  3.58 us
    ppermute x6, waiting for transfers between devices, swap(): return lax.ppermute(block, axis, [(i, i ^ bit) for i in range(size)])  3.41 us
    pallas_call x1, Pallas kernels, local(): pl.pallas_call(pack_kernel, out_shape=(jax.ShapeDtypeStruct((rows, width)...  1.54 us
    pallas_call x4, Pallas kernels, call(): pl.pallas_call(kernel, out_shape=outs, in_specs=[VMEM] * len(args), out_s...  1.05 us
    add x1, other arithmetic, local(): return swap(far_total, 'col', ncol, far_bit) + total  0.61 us
    ppermute x1, starting transfers between devices, local(): lax.ppermute(jnp.concatenate([base, beside]), ('row', 'col'), [(index(r,...  0.6 us
    ppermute x1, waiting for transfers between devices, local(): lax.ppermute(jnp.concatenate([base, beside]), ('row', 'col'), [(index(r,...  0.38 us
  transfers between devices with their start and end apart: 8, of which 4 were waited for; matrix products, arithmetic and copies ran while one was open for 0% of the time, Pallas kernels for 3%

profile of v9, /device:TPU:0, one launch (start us, length us, event | category | flops | bytes accessed | tf_op | source)
XLA Modules:
  0.0 18.3 jit_solution(15878338754858867272)
XLA Ops:
  0.0 1.5 %pack.1 = (bf16[32,1024]{1,0:T(8,128)(2,1)S(1)}, bf16[32,896]{1,0:T(8,128)(2,1)S(1)}, f32[8,128]{1,0:T(8,128)S(1)}, f32[1,896]{1,0:T(1,128)S(1)}) custom-call(s32[128]{0:T(128)} %slice_hbm.1, f32[3]{0:T(128)} %tau_hbm.1, f32[3]{0:T(128)} %weight_hbm.1, f32[16,4096]{1,0:T(8,128)} %bitcast.1, bf16[32,4096]{1,0:T(8,128)(2,1)} %empty_hbm.1, ...), custom_call_target="tpu_custom_call" | custom-call | tf_op jit(solution)/shard_map/pack/pallas_call | solution.py:162
  1.5 0.5 %collective-permute-start.3 = (bf16[32,1024]{1,0:T(8,128)(2,1)S(1)}, bf16[32,1024]{1,0:T(8,128)(2,1)S(1)}, u32[]{:S(2)}, u32[]{:S(2)}) collective-permute-start(bf16[32,1024]{1,0:T(8,128)(2,1)S(1)} %get-tuple-element.14.refs_0_.block_ref), channel_id=1, source_target_pairs={{0,8},{8,0},{16,24},{24,16},{1,9},{9,1},{17,25},{25,17},{2,10},{10... | collective-permute-start | bytes 196616 | tf_op jit(solution)/shard_map/ppermute | solution.py:24
  2.1 3.6 %collective-permute-start = (bf16[32,1024]{1,0:T(8,128)(2,1)S(1)}, bf16[32,1024]{1,0:T(8,128)(2,1)S(1)}, u32[]{:S(2)}, u32[]{:S(2)}) collective-permute-start(bf16[32,1024]{1,0:T(8,128)(2,1)S(1)} %get-tuple-element.14.refs_0_.block_ref), channel_id=1, source_target_pairs={{0,18},{2,16},{4,22},{6,20},{8,26},{10,24},{12,30},{14,28},{16,2},... | collective-permute-start | bytes 196616 | tf_op jit(solution)/shard_map/ppermute | solution.py:200
  5.6 0.0 collective-permute-done.3.refs_1_
  5.7 0.6 %collective-permute-start.4 = (bf16[64,1024]{1,0:T(8,128)(2,1)S(1)}, bf16[64,1024]{1,0:T(8,128)(2,1)S(1)}, u32[]{:S(2)}, u32[]{:S(2)}) collective-permute-start(bf16[64,1024]{1,0:T(8,128)(2,1)S(1)} %pad_maximum_fusion), channel_id=1, source_target_pairs={{0,16},{2,18},{4,6},{6,4},{8,10},{10,8},{12,28},{14,30},{16,0},{18... | collective-permute-start | bytes 393224 | tf_op jit(solution)/shard_map/ppermute | solution.py:202
  6.3 2.5 %collective-permute-start.2 = (bf16[32,896]{1,0:T(8,128)(2,1)S(1)}, bf16[32,896]{1,0:T(8,128)(2,1)S(1)}, u32[]{:S(2)}, u32[]{:S(2)}) collective-permute-start(bf16[32,896]{1,0:T(8,128)(2,1)S(1)} %get-tuple-element.16), channel_id=1, source_target_pairs={{0,4},{2,6},{4,0},{6,2},{1,5},{3,7},{5,1},{7,3},{8,12},{10,14},{12... | collective-permute-start | bytes 172040 | tf_op jit(solution)/shard_map/ppermute | solution.py:24
  8.8 0.0 collective-permute-done.refs_2_
  8.8 1.5 %collective-permute-start.1 = (f32[8,128]{1,0:T(8,128)S(1)}, f32[8,128]{1,0:T(8,128)S(1)}, u32[]{:S(2)}, u32[]{:S(2)}) collective-permute-start(f32[8,128]{1,0:T(8,128)S(1)} %get-tuple-element.15.times_ref), channel_id=1, source_target_pairs={{0,1},{1,0},{2,3},{3,2},{4,5},{5,4},{6,7},{7,6},{8,9},{9,8},{10,11... | collective-permute-start | bytes 12296 | tf_op jit(solution)/shard_map/ppermute | solution.py:24
  10.3 0.0 collective-permute-start.5
  10.3 0.4 %collective-permute-done.4.refs_2_ = bf16[64,1024]{1,0:T(8,128)(2,1)S(1)} collective-permute-done((bf16[64,1024]{1,0:T(8,128)(2,1)S(1)}, bf16[64,1024]{1,0:T(8,128)(2,1)S(1)}, u32[]{:S(2)}, u32[]{:S(2)}) %collective-permute-start.4) | collective-permute-done | bytes 131104 | tf_op jit(solution)/shard_map/ppermute | solution.py:202
  10.7 0.2 %collective-permute-start.6 = (bf16[64,1024]{1,0:T(8,128)(2,1)S(1)}, bf16[64,1024]{1,0:T(8,128)(2,1)S(1)}, u32[]{:S(2)}, u32[]{:S(2)}) collective-permute-start(bf16[64,1024]{1,0:T(8,128)(2,1)S(1)} %collective-permute-done.4.refs_2_), channel_id=1, source_target_pairs={{0,8},{8,0},{16,24},{24,16},{1,9},{9,1},{17,25},{25,17},{2,10},{10... | collective-permute-start | bytes 393224 | tf_op jit(solution)/shard_map/ppermute | solution.py:24
  10.9 0.9 %collective-permute-done.2.block_ref = bf16[32,896]{1,0:T(8,128)(2,1)S(1)} collective-permute-done((bf16[32,896]{1,0:T(8,128)(2,1)S(1)}, bf16[32,896]{1,0:T(8,128)(2,1)S(1)}, u32[]{:S(2)}, u32[]{:S(2)}) %collective-permute-start.2) | collective-permute-done | bytes 57376 | tf_op jit(solution)/shard_map/ppermute | solution.py:24
  11.8 0.6 %collective-permute-done.1.more_times_ref = f32[8,128]{1,0:T(8,128)S(1)} collective-permute-done((f32[8,128]{1,0:T(8,128)S(1)}, f32[8,128]{1,0:T(8,128)S(1)}, u32[]{:S(2)}, u32[]{:S(2)}) %collective-permute-start.1) | collective-permute-done | bytes 4128 | tf_op jit(solution)/shard_map/ppermute | solution.py:24
  12.4 0.1 scale.1.scaled_ref
  12.5 0.0 collective-permute-done.5.refs_1_
  12.5 0.0 collective-permute-done.6.refs_3_
  12.5 0.5 %far.1 = f32[32,128]{1,0:T(8,128)S(1)} custom-call(f32[8,128]{1,0:T(8,128)S(1)} %get-tuple-element.15.times_ref, f32[8,128]{1,0:T(8,128)S(1)} %collective-permute-done.1.more_times_ref, bf16[192,896]{1,0:T(8,128)(2,1)S(1)} %scale.1.scaled_ref, bf16[96,1024]{1,0:T(8,128)(2,1)S(1)} %join.1.refs_0_, bf16[32,1024]{1,0:T(8,128)(2,1)S(1)} %collective-permute-done.5.refs_1_, ...), custom_call_target="tpu_custom_call" | custom-call | flops 1000000000 | bytes 1000000 | tf_op jit(solution)/shard_map/far/pallas_call | solution.py:139
  13.0 2.4 %collective-permute-start.7 = (f32[32,128]{1,0:T(8,128)S(1)}, f32[32,128]{1,0:T(8,128)S(1)}, u32[]{:S(2)}, u32[]{:S(2)}) collective-permute-start(f32[32,128]{1,0:T(8,128)S(1)} %far.1), channel_id=1, source_target_pairs={{0,4},{2,6},{4,0},{6,2},{1,5},{3,7},{5,1},{7,3},{8,12},{10,14},{12... | collective-permute-start | bytes 49160 | tf_op jit(solution)/shard_map/ppermute | solution.py:24
  15.4 0.5 %own.1 = f32[32,128]{1,0:T(8,128)S(1)} custom-call(bf16[32,1024]{1,0:T(8,128)(2,1)S(1)} %get-tuple-element.14.refs_0_.block_ref, f32[8,128]{1,0:T(8,128)S(1)} %get-tuple-element.15.times_ref, f32[8,128]{1,0:T(8,128)S(1)} %collective-permute-done.1.more_times_ref, f32[1,896]{1,0:T(1,128)S(1)} %get-tuple-element.17.energy_ref, ...), custom_call_target="tpu_custom_call" | custom-call | flops 1000000000 | bytes 1000000 | tf_op jit(solution)/shard_map/own/pallas_call | solution.py:139
  15.8 1.9 %collective-permute-done.7 = f32[32,128]{1,0:T(8,128)S(1)} collective-permute-done((f32[32,128]{1,0:T(8,128)S(1)}, f32[32,128]{1,0:T(8,128)S(1)}, u32[]{:S(2)}, u32[]{:S(2)}) %collective-permute-start.7) | collective-permute-done | bytes 16416 | tf_op jit(solution)/shard_map/ppermute | solution.py:24
  17.7 0.6 %add.3 = f32[32,128]{1,0:T(8,128)} add(f32[32,128]{1,0:T(8,128)S(1)} %collective-permute-done.7, f32[32,128]{1,0:T(8,128)S(1)} %own.1) | non-fusion elementwise | flops 4096 | bytes 49152 | tf_op jit(solution)/shard_map/add | solution.py:234
  (2 shorter events, 0.0 us)
Async XLA Ops:
  1.5 4.1 %collective-permute-start.3 = (bf16[32,1024]{1,0:T(8,128)(2,1)S(1)}, bf16[32,1024]{1,0:T(8,128)(2,1)S(1)}, u32[]{:S(2)}, u32[]{:S(2)}) collective-permute-start(bf16[32,1024]{1,0:T(8,128)(2,1)S(1)} %get-tuple-element.14.refs_0_.block_ref), channel_id=1, source_target_pairs={{0,8},{8,0},{16,24},{24,16},{1,9},{9,1},{17,25},{25,17},{2,10},{10... | collective-permute-start | bytes 196616 | tf_op jit(solution)/shard_map/ppermute | solution.py:24
  2.1 6.7 %collective-permute-start = (bf16[32,1024]{1,0:T(8,128)(2,1)S(1)}, bf16[32,1024]{1,0:T(8,128)(2,1)S(1)}, u32[]{:S(2)}, u32[]{:S(2)}) collective-permute-start(bf16[32,1024]{1,0:T(8,128)(2,1)S(1)} %get-tuple-element.14.refs_0_.block_ref), channel_id=1, source_target_pairs={{0,18},{2,16},{4,22},{6,20},{8,26},{10,24},{12,30},{14,28},{16,2},... | collective-permute-start | bytes 196616 | tf_op jit(solution)/shard_map/ppermute | solution.py:200
  5.7 5.0 %collective-permute-start.4 = (bf16[64,1024]{1,0:T(8,128)(2,1)S(1)}, bf16[64,1024]{1,0:T(8,128)(2,1)S(1)}, u32[]{:S(2)}, u32[]{:S(2)}) collective-permute-start(bf16[64,1024]{1,0:T(8,128)(2,1)S(1)} %pad_maximum_fusion), channel_id=1, source_target_pairs={{0,16},{2,18},{4,6},{6,4},{8,10},{10,8},{12,28},{14,30},{16,0},{18... | collective-permute-start | bytes 393224 | tf_op jit(solution)/shard_map/ppermute | solution.py:202
  6.3 5.5 %collective-permute-start.2 = (bf16[32,896]{1,0:T(8,128)(2,1)S(1)}, bf16[32,896]{1,0:T(8,128)(2,1)S(1)}, u32[]{:S(2)}, u32[]{:S(2)}) collective-permute-start(bf16[32,896]{1,0:T(8,128)(2,1)S(1)} %get-tuple-element.16), channel_id=1, source_target_pairs={{0,4},{2,6},{4,0},{6,2},{1,5},{3,7},{5,1},{7,3},{8,12},{10,14},{12... | collective-permute-start | bytes 172040 | tf_op jit(solution)/shard_map/ppermute | solution.py:24
  8.8 3.6 %collective-permute-start.1 = (f32[8,128]{1,0:T(8,128)S(1)}, f32[8,128]{1,0:T(8,128)S(1)}, u32[]{:S(2)}, u32[]{:S(2)}) collective-permute-start(f32[8,128]{1,0:T(8,128)S(1)} %get-tuple-element.15.times_ref), channel_id=1, source_target_pairs={{0,1},{1,0},{2,3},{3,2},{4,5},{5,4},{6,7},{7,6},{8,9},{9,8},{10,11... | collective-permute-start | bytes 12296 | tf_op jit(solution)/shard_map/ppermute | solution.py:24
  10.3 2.2 %collective-permute-start.5 = (bf16[32,1024]{1,0:T(8,128)(2,1)S(1)}, bf16[32,1024]{1,0:T(8,128)(2,1)S(1)}, u32[]{:S(2)}, u32[]{:S(2)}) collective-permute-start(bf16[32,1024]{1,0:T(8,128)(2,1)S(1)} %collective-permute-done.refs_2_), channel_id=1, source_target_pairs={{0,8},{8,0},{16,24},{24,16},{1,9},{9,1},{17,25},{25,17},{2,10},{10... | collective-permute-start | bytes 196616 | tf_op jit(solution)/shard_map/ppermute | solution.py:24
  10.7 1.8 %collective-permute-start.6 = (bf16[64,1024]{1,0:T(8,128)(2,1)S(1)}, bf16[64,1024]{1,0:T(8,128)(2,1)S(1)}, u32[]{:S(2)}, u32[]{:S(2)}) collective-permute-start(bf16[64,1024]{1,0:T(8,128)(2,1)S(1)} %collective-permute-done.4.refs_2_), channel_id=1, source_target_pairs={{0,8},{8,0},{16,24},{24,16},{1,9},{9,1},{17,25},{25,17},{2,10},{10... | collective-permute-start | bytes 393224 | tf_op jit(solution)/shard_map/ppermute | solution.py:24
  13.0 4.8 %collective-permute-start.7 = (f32[32,128]{1,0:T(8,128)S(1)}, f32[32,128]{1,0:T(8,128)S(1)}, u32[]{:S(2)}, u32[]{:S(2)}) collective-permute-start(f32[32,128]{1,0:T(8,128)S(1)} %far.1), channel_id=1, source_target_pairs={{0,4},{2,6},{4,0},{6,2},{1,5},{3,7},{5,1},{7,3},{8,12},{10,14},{12... | collective-permute-start | bytes 49160 | tf_op jit(solution)/shard_map/ppermute | solution.py:24

commit v10 on v7

--- a/solution.py
+++ b/solution.py
@@ -41,9 +41,9 @@
     copies = [
         pltpu.make_async_copy(source, target, sems.at[i])
         for i, (source, target) in enumerate((
+            (empty_hbm, empty_ref),
+            (mix_hbm, mix_ref),
             (slice_hbm, slice_ref),
-            (mix_hbm, mix_ref),
-            (empty_hbm, empty_ref),
             (tau_hbm, tau_ref),
             (weight_hbm, weight_ref),
             (occ_hbm, packed_ref.at[:, :nocc]),

time: 18.5 us -> 18.5 us (level)
  no operation moved by 1% of the time
where the time goes in v10:
time: 18.5 us; the launch traced here: 18.4 us
  starting transfers between devices  11.2 us (61%)
  waiting for transfers between devices  3.94 us (21%)
  Pallas kernels  2.59 us (14%)
  other arithmetic  0.62 us (3%)
    ppermute x6, starting transfers between devices, swap(): return lax.ppermute(block, axis, [(i, i ^ bit) for i in range(size)])  7 us
    ppermute x6, waiting for transfers between devices, swap(): return lax.ppermute(block, axis, [(i, i ^ bit) for i in range(size)])  3.64 us
    ppermute x1, starting transfers between devices, local(): lax.ppermute(base, ('row', 'col'), [(index(r, c), index(r ^ x_bit, c ^ co...  3.58 us
    pallas_call x1, Pallas kernels, local(): pl.pallas_call(pack_kernel, out_shape=(jax.ShapeDtypeStruct((rows, width)...  1.55 us
    pallas_call x4, Pallas kernels, call(): pl.pallas_call(kernel, out_shape=outs, in_specs=[VMEM] * len(args), out_s...  1.04 us
    add x1, other arithmetic, local(): return swap(far_total, 'col', ncol, far_bit) + total  0.61 us
    ppermute x1, starting transfers between devices, local(): lax.ppermute(jnp.concatenate([base, beside]), ('row', 'col'), [(index(r,...  0.6 us
  transfers between devices with their start and end apart: 8, of which 3 were waited for; matrix products, arithmetic and copies ran while one was open for 0% of the time, Pallas kernels for 3%

profile of v10, /device:TPU:0, one launch (start us, length us, event | category | flops | bytes accessed | tf_op | source)
XLA Modules:
  0.0 18.4 jit_solution(16269560506934674609)
XLA Ops:
  0.0 1.5 %pack.1 = (bf16[32,1024]{1,0:T(8,128)(2,1)S(1)}, f32[8,128]{1,0:T(8,128)S(1)}, f32[1,896]{1,0:T(1,128)S(1)}) custom-call(s32[128]{0:T(128)} %slice_hbm.1, f32[3]{0:T(128)} %tau_hbm.1, f32[3]{0:T(128)} %weight_hbm.1, f32[16,4096]{1,0:T(8,128)} %bitcast.1, bf16[32,4096]{1,0:T(8,128)(2,1)} %empty_hbm.1, bf16[32,512]{1,0:T(8,128)(2,1)} %occ_hbm.1, ...), custom_call_target="tpu_custom_call" | custom-call | tf_op jit(solution)/shard_map/pack/pallas_call | solution.py:161
  1.6 0.5 %collective-permute-start.2 = (bf16[32,1024]{1,0:T(8,128)(2,1)S(1)}, bf16[32,1024]{1,0:T(8,128)(2,1)S(1)}, u32[]{:S(2)}, u32[]{:S(2)}) collective-permute-start(bf16[32,1024]{1,0:T(8,128)(2,1)S(1)} %get-tuple-element.11.refs_0_.block_ref), channel_id=1, source_target_pairs={{0,8},{8,0},{16,24},{24,16},{1,9},{9,1},{17,25},{25,17},{2,10},{10... | collective-permute-start | bytes 196616 | tf_op jit(solution)/shard_map/ppermute | solution.py:24
  2.1 3.6 %collective-permute-start.3 = (bf16[32,1024]{1,0:T(8,128)(2,1)S(1)}, bf16[32,1024]{1,0:T(8,128)(2,1)S(1)}, u32[]{:S(2)}, u32[]{:S(2)}) collective-permute-start(bf16[32,1024]{1,0:T(8,128)(2,1)S(1)} %get-tuple-element.11.refs_0_.block_ref), channel_id=1, source_target_pairs={{0,18},{2,16},{4,22},{6,20},{8,26},{10,24},{12,30},{14,28},{16,2},... | collective-permute-start | bytes 196616 | tf_op jit(solution)/shard_map/ppermute | solution.py:198
  5.7 0.0 collective-permute-done.2.refs_1_
  5.7 0.6 %collective-permute-start.4 = (bf16[64,1024]{1,0:T(8,128)(2,1)S(1)}, bf16[64,1024]{1,0:T(8,128)(2,1)S(1)}, u32[]{:S(2)}, u32[]{:S(2)}) collective-permute-start(bf16[64,1024]{1,0:T(8,128)(2,1)S(1)} %pad_maximum_fusion), channel_id=1, source_target_pairs={{0,16},{2,18},{4,20},{6,22},{8,10},{10,8},{12,14},{14,12},{16,0},{... | collective-permute-start | bytes 393224 | tf_op jit(solution)/shard_map/ppermute | solution.py:200
  6.3 2.6 %collective-permute-start.1 = (bf16[32,1024]{1,0:T(8,128)(2,1)S(1)}, bf16[32,1024]{1,0:T(8,128)(2,1)S(1)}, u32[]{:S(2)}, u32[]{:S(2)}) collective-permute-start(bf16[32,1024]{1,0:T(8,128)(2,1)S(1)} %get-tuple-element.11.refs_0_.block_ref), channel_id=1, source_target_pairs={{0,4},{2,6},{4,0},{6,2},{1,5},{3,7},{5,1},{7,3},{8,12},{10,14},{12... | collective-permute-start | bytes 196616 | tf_op jit(solution)/shard_map/ppermute | solution.py:24
  8.9 1.5 %collective-permute-start = (f32[8,128]{1,0:T(8,128)S(1)}, f32[8,128]{1,0:T(8,128)S(1)}, u32[]{:S(2)}, u32[]{:S(2)}) collective-permute-start(f32[8,128]{1,0:T(8,128)S(1)} %get-tuple-element.10.times_ref), channel_id=1, source_target_pairs={{0,1},{1,0},{2,3},{3,2},{4,5},{5,4},{6,7},{7,6},{8,9},{9,8},{10,11... | collective-permute-start | bytes 12296 | tf_op jit(solution)/shard_map/ppermute | solution.py:24
  10.4 0.0 collective-permute-done.3.refs_2_
  10.4 0.0 collective-permute-start.5
  10.4 0.3 %collective-permute-done.4.refs_2_ = bf16[64,1024]{1,0:T(8,128)(2,1)S(1)} collective-permute-done((bf16[64,1024]{1,0:T(8,128)(2,1)S(1)}, bf16[64,1024]{1,0:T(8,128)(2,1)S(1)}, u32[]{:S(2)}, u32[]{:S(2)}) %collective-permute-start.4) | collective-permute-done | bytes 131104 | tf_op jit(solution)/shard_map/ppermute | solution.py:200
  10.7 0.3 %collective-permute-start.6 = (bf16[64,1024]{1,0:T(8,128)(2,1)S(1)}, bf16[64,1024]{1,0:T(8,128)(2,1)S(1)}, u32[]{:S(2)}, u32[]{:S(2)}) collective-permute-start(bf16[64,1024]{1,0:T(8,128)(2,1)S(1)} %collective-permute-done.4.refs_2_), channel_id=1, source_target_pairs={{0,8},{8,0},{16,24},{24,16},{1,9},{9,1},{17,25},{25,17},{2,10},{10... | collective-permute-start | bytes 393224 | tf_op jit(solution)/shard_map/ppermute | solution.py:24
  11.0 1.5 %collective-permute-done.more_times_ref = f32[8,128]{1,0:T(8,128)S(1)} collective-permute-done((f32[8,128]{1,0:T(8,128)S(1)}, f32[8,128]{1,0:T(8,128)S(1)}, u32[]{:S(2)}, u32[]{:S(2)}) %collective-permute-start) | collective-permute-done | bytes 4128 | tf_op jit(solution)/shard_map/ppermute | solution.py:24
  12.5 0.0 collective-permute-done.1.block_ref
  12.5 0.1 scale.1.scaled_ref
  12.6 0.0 collective-permute-done.5.refs_1_
  12.6 0.0 collective-permute-done.6.refs_3_
  12.6 0.4 %far.1 = f32[32,128]{1,0:T(8,128)S(1)} custom-call(f32[8,128]{1,0:T(8,128)S(1)} %get-tuple-element.10.times_ref, f32[8,128]{1,0:T(8,128)S(1)} %collective-permute-done.more_times_ref, bf16[192,896]{1,0:T(8,128)(2,1)S(1)} %scale.1.scaled_ref, bf16[96,1024]{1,0:T(8,128)(2,1)S(1)} %join.1.refs_0_, bf16[32,1024]{1,0:T(8,128)(2,1)S(1)} %collective-permute-done.5.refs_1_, ...), custom_call_target="tpu_custom_call" | custom-call | flops 1000000000 | bytes 1000000 | tf_op jit(solution)/shard_map/far/pallas_call | solution.py:138
  13.1 2.1 %collective-permute-start.7 = (f32[32,128]{1,0:T(8,128)S(1)}, f32[32,128]{1,0:T(8,128)S(1)}, u32[]{:S(2)}, u32[]{:S(2)}) collective-permute-start(f32[32,128]{1,0:T(8,128)S(1)} %far.1), channel_id=1, source_target_pairs={{0,4},{2,6},{4,0},{6,2},{1,5},{3,7},{5,1},{7,3},{8,12},{10,14},{12... | collective-permute-start | bytes 49160 | tf_op jit(solution)/shard_map/ppermute | solution.py:24
  15.2 0.5 %own.1 = f32[32,128]{1,0:T(8,128)S(1)} custom-call(bf16[32,1024]{1,0:T(8,128)(2,1)S(1)} %get-tuple-element.11.refs_0_.block_ref, f32[8,128]{1,0:T(8,128)S(1)} %get-tuple-element.10.times_ref, f32[8,128]{1,0:T(8,128)S(1)} %collective-permute-done.more_times_ref, f32[1,896]{1,0:T(1,128)S(1)} %get-tuple-element.12.energy_ref, ...), custom_call_target="tpu_custom_call" | custom-call | flops 1000000000 | bytes 1000000 | tf_op jit(solution)/shard_map/own/pallas_call | solution.py:138
  15.6 2.2 %collective-permute-done.7 = f32[32,128]{1,0:T(8,128)S(1)} collective-permute-done((f32[32,128]{1,0:T(8,128)S(1)}, f32[32,128]{1,0:T(8,128)S(1)}, u32[]{:S(2)}, u32[]{:S(2)}) %collective-permute-start.7) | collective-permute-done | bytes 16416 | tf_op jit(solution)/shard_map/ppermute | solution.py:24
  17.8 0.6 %add.3 = f32[32,128]{1,0:T(8,128)} add(f32[32,128]{1,0:T(8,128)S(1)} %collective-permute-done.7, f32[32,128]{1,0:T(8,128)S(1)} %own.1) | non-fusion elementwise | flops 4096 | bytes 49152 | tf_op jit(solution)/shard_map/add | solution.py:231
  (2 shorter events, 0.0 us)
Async XLA Ops:
  1.6 4.1 %collective-permute-start.2 = (bf16[32,1024]{1,0:T(8,128)(2,1)S(1)}, bf16[32,1024]{1,0:T(8,128)(2,1)S(1)}, u32[]{:S(2)}, u32[]{:S(2)}) collective-permute-start(bf16[32,1024]{1,0:T(8,128)(2,1)S(1)} %get-tuple-element.11.refs_0_.block_ref), channel_id=1, source_target_pairs={{0,8},{8,0},{16,24},{24,16},{1,9},{9,1},{17,25},{25,17},{2,10},{10... | collective-permute-start | bytes 196616 | tf_op jit(solution)/shard_map/ppermute | solution.py:24
  2.1 8.3 %collective-permute-start.3 = (bf16[32,1024]{1,0:T(8,128)(2,1)S(1)}, bf16[32,1024]{1,0:T(8,128)(2,1)S(1)}, u32[]{:S(2)}, u32[]{:S(2)}) collective-permute-start(bf16[32,1024]{1,0:T(8,128)(2,1)S(1)} %get-tuple-element.11.refs_0_.block_ref), channel_id=1, source_target_pairs={{0,18},{2,16},{4,22},{6,20},{8,26},{10,24},{12,30},{14,28},{16,2},... | collective-permute-start | bytes 196616 | tf_op jit(solution)/shard_map/ppermute | solution.py:198
  5.7 5.0 %collective-permute-start.4 = (bf16[64,1024]{1,0:T(8,128)(2,1)S(1)}, bf16[64,1024]{1,0:T(8,128)(2,1)S(1)}, u32[]{:S(2)}, u32[]{:S(2)}) collective-permute-start(bf16[64,1024]{1,0:T(8,128)(2,1)S(1)} %pad_maximum_fusion), channel_id=1, source_target_pairs={{0,16},{2,18},{4,20},{6,22},{8,10},{10,8},{12,14},{14,12},{16,0},{... | collective-permute-start | bytes 393224 | tf_op jit(solution)/shard_map/ppermute | solution.py:200
  6.3 6.2 %collective-permute-start.1 = (bf16[32,1024]{1,0:T(8,128)(2,1)S(1)}, bf16[32,1024]{1,0:T(8,128)(2,1)S(1)}, u32[]{:S(2)}, u32[]{:S(2)}) collective-permute-start(bf16[32,1024]{1,0:T(8,128)(2,1)S(1)} %get-tuple-element.11.refs_0_.block_ref), channel_id=1, source_target_pairs={{0,4},{2,6},{4,0},{6,2},{1,5},{3,7},{5,1},{7,3},{8,12},{10,14},{12... | collective-permute-start | bytes 196616 | tf_op jit(solution)/shard_map/ppermute | solution.py:24
  8.9 3.6 %collective-permute-start = (f32[8,128]{1,0:T(8,128)S(1)}, f32[8,128]{1,0:T(8,128)S(1)}, u32[]{:S(2)}, u32[]{:S(2)}) collective-permute-start(f32[8,128]{1,0:T(8,128)S(1)} %get-tuple-element.10.times_ref), channel_id=1, source_target_pairs={{0,1},{1,0},{2,3},{3,2},{4,5},{5,4},{6,7},{7,6},{8,9},{9,8},{10,11... | collective-permute-start | bytes 12296 | tf_op jit(solution)/shard_map/ppermute | solution.py:24
  10.4 2.2 %collective-permute-start.5 = (bf16[32,1024]{1,0:T(8,128)(2,1)S(1)}, bf16[32,1024]{1,0:T(8,128)(2,1)S(1)}, u32[]{:S(2)}, u32[]{:S(2)}) collective-permute-start(bf16[32,1024]{1,0:T(8,128)(2,1)S(1)} %collective-permute-done.3.refs_2_), channel_id=1, source_target_pairs={{0,8},{8,0},{16,24},{24,16},{1,9},{9,1},{17,25},{25,17},{2,10},{10... | collective-permute-start | bytes 196616 | tf_op jit(solution)/shard_map/ppermute | solution.py:24
  10.7 1.9 %collective-permute-start.6 = (bf16[64,1024]{1,0:T(8,128)(2,1)S(1)}, bf16[64,1024]{1,0:T(8,128)(2,1)S(1)}, u32[]{:S(2)}, u32[]{:S(2)}) collective-permute-start(bf16[64,1024]{1,0:T(8,128)(2,1)S(1)} %collective-permute-done.4.refs_2_), channel_id=1, source_target_pairs={{0,8},{8,0},{16,24},{24,16},{1,9},{9,1},{17,25},{25,17},{2,10},{10... | collective-permute-start | bytes 393224 | tf_op jit(solution)/shard_map/ppermute | solution.py:24
  13.1 4.7 %collective-permute-start.7 = (f32[32,128]{1,0:T(8,128)S(1)}, f32[32,128]{1,0:T(8,128)S(1)}, u32[]{:S(2)}, u32[]{:S(2)}) collective-permute-start(f32[32,128]{1,0:T(8,128)S(1)} %far.1), channel_id=1, source_target_pairs={{0,4},{2,6},{4,0},{6,2},{1,5},{3,7},{5,1},{7,3},{8,12},{10,14},{12... | collective-permute-start | bytes 49160 | tf_op jit(solution)/shard_map/ppermute | solution.py:24

commit v11 on v10

--- a/solution.py
+++ b/solution.py
@@ -200,7 +200,7 @@
     mixed = lax.ppermute(
         jnp.concatenate([base, beside]),
         ("row", "col"),
-        [(index(r, c), index(r ^ x_bit, c) if (r // core_bit + 1) % 2 else index(r, c ^ col_bit)) for r, c in places],
+        [(index(r, c), index(r ^ x_bit, c) if (r // core_bit + c // far_bit + 1) % 2 else index(r, c ^ col_bit)) for r, c in places],
     )
     others = []
     for bit in bits_of(nplanes):

time: 18.5 us -> 18.4 us (level)
  no operation moved by 1% of the time
where the time goes in v11:
time: 18.4 us; the launch traced here: 18.3 us
  starting transfers between devices  11.1 us (60%)
  waiting for transfers between devices  3.95 us (21%)
  Pallas kernels  2.59 us (14%)
  other arithmetic  0.62 us (3%)
    ppermute x6, starting transfers between devices, swap(): return lax.ppermute(block, axis, [(i, i ^ bit) for i in range(size)])  6.91 us
    ppermute x1, starting transfers between devices, local(): lax.ppermute(base, ('row', 'col'), [(index(r, c), index(r ^ x_bit, c ^ co...  3.58 us
    ppermute x6, waiting for transfers between devices, swap(): return lax.ppermute(block, axis, [(i, i ^ bit) for i in range(size)])  3.56 us
    pallas_call x1, Pallas kernels, local(): pl.pallas_call(pack_kernel, out_shape=(jax.ShapeDtypeStruct((rows, width)...  1.54 us
    pallas_call x4, Pallas kernels, call(): pl.pallas_call(kernel, out_shape=outs, in_specs=[VMEM] * len(args), out_s...  1.05 us
    add x1, other arithmetic, local(): return swap(far_total, 'col', ncol, far_bit) + total  0.61 us
    ppermute x1, starting transfers between devices, local(): lax.ppermute(jnp.concatenate([base, beside]), ('row', 'col'), [(index(r,...  0.6 us
    ppermute x1, waiting for transfers between devices, local(): lax.ppermute(jnp.concatenate([base, beside]), ('row', 'col'), [(index(r,...  0.38 us
  transfers between devices with their start and end apart: 8, of which 3 were waited for; matrix products, arithmetic and copies ran while one was open for 0% of the time, Pallas kernels for 3%

profile of v11, /device:TPU:0, one launch (start us, length us, event | category | flops | bytes accessed | tf_op | source)
XLA Modules:
  0.0 18.3 jit_solution(6706651855485949547)
XLA Ops:
  0.0 1.5 %pack.1 = (bf16[32,1024]{1,0:T(8,128)(2,1)S(1)}, f32[8,128]{1,0:T(8,128)S(1)}, f32[1,896]{1,0:T(1,128)S(1)}) custom-call(s32[128]{0:T(128)} %slice_hbm.1, f32[3]{0:T(128)} %tau_hbm.1, f32[3]{0:T(128)} %weight_hbm.1, f32[16,4096]{1,0:T(8,128)} %bitcast.1, bf16[32,4096]{1,0:T(8,128)(2,1)} %empty_hbm.1, bf16[32,512]{1,0:T(8,128)(2,1)} %occ_hbm.1, ...), custom_call_target="tpu_custom_call" | custom-call | tf_op jit(solution)/shard_map/pack/pallas_call | solution.py:161
  1.6 0.5 %collective-permute-start.2 = (bf16[32,1024]{1,0:T(8,128)(2,1)S(1)}, bf16[32,1024]{1,0:T(8,128)(2,1)S(1)}, u32[]{:S(2)}, u32[]{:S(2)}) collective-permute-start(bf16[32,1024]{1,0:T(8,128)(2,1)S(1)} %get-tuple-element.11.refs_0_.block_ref), channel_id=1, source_target_pairs={{0,8},{8,0},{16,24},{24,16},{1,9},{9,1},{17,25},{25,17},{2,10},{10... | collective-permute-start | bytes 196616 | tf_op jit(solution)/shard_map/ppermute | solution.py:24
  2.1 3.6 %collective-permute-start.3 = (bf16[32,1024]{1,0:T(8,128)(2,1)S(1)}, bf16[32,1024]{1,0:T(8,128)(2,1)S(1)}, u32[]{:S(2)}, u32[]{:S(2)}) collective-permute-start(bf16[32,1024]{1,0:T(8,128)(2,1)S(1)} %get-tuple-element.11.refs_0_.block_ref), channel_id=1, source_target_pairs={{0,18},{2,16},{4,22},{6,20},{8,26},{10,24},{12,30},{14,28},{16,2},... | collective-permute-start | bytes 196616 | tf_op jit(solution)/shard_map/ppermute | solution.py:198
  5.6 0.0 collective-permute-done.2.refs_1_
  5.7 0.6 %collective-permute-start.4 = (bf16[64,1024]{1,0:T(8,128)(2,1)S(1)}, bf16[64,1024]{1,0:T(8,128)(2,1)S(1)}, u32[]{:S(2)}, u32[]{:S(2)}) collective-permute-start(bf16[64,1024]{1,0:T(8,128)(2,1)S(1)} %pad_maximum_fusion), channel_id=1, source_target_pairs={{0,16},{2,18},{4,6},{6,4},{8,10},{10,8},{12,28},{14,30},{16,0},{18... | collective-permute-start | bytes 393224 | tf_op jit(solution)/shard_map/ppermute | solution.py:200
  6.3 2.5 %collective-permute-start.1 = (bf16[32,1024]{1,0:T(8,128)(2,1)S(1)}, bf16[32,1024]{1,0:T(8,128)(2,1)S(1)}, u32[]{:S(2)}, u32[]{:S(2)}) collective-permute-start(bf16[32,1024]{1,0:T(8,128)(2,1)S(1)} %get-tuple-element.11.refs_0_.block_ref), channel_id=1, source_target_pairs={{0,4},{2,6},{4,0},{6,2},{1,5},{3,7},{5,1},{7,3},{8,12},{10,14},{12... | collective-permute-start | bytes 196616 | tf_op jit(solution)/shard_map/ppermute | solution.py:24
  8.8 1.5 %collective-permute-start = (f32[8,128]{1,0:T(8,128)S(1)}, f32[8,128]{1,0:T(8,128)S(1)}, u32[]{:S(2)}, u32[]{:S(2)}) collective-permute-start(f32[8,128]{1,0:T(8,128)S(1)} %get-tuple-element.10.times_ref), channel_id=1, source_target_pairs={{0,1},{1,0},{2,3},{3,2},{4,5},{5,4},{6,7},{7,6},{8,9},{9,8},{10,11... | collective-permute-start | bytes 12296 | tf_op jit(solution)/shard_map/ppermute | solution.py:24
  10.3 0.0 collective-permute-done.3.refs_2_
  10.3 0.0 collective-permute-start.5
  10.3 0.4 %collective-permute-done.4.refs_2_ = bf16[64,1024]{1,0:T(8,128)(2,1)S(1)} collective-permute-done((bf16[64,1024]{1,0:T(8,128)(2,1)S(1)}, bf16[64,1024]{1,0:T(8,128)(2,1)S(1)}, u32[]{:S(2)}, u32[]{:S(2)}) %collective-permute-start.4) | collective-permute-done | bytes 131104 | tf_op jit(solution)/shard_map/ppermute | solution.py:200
  10.7 0.2 %collective-permute-start.6 = (bf16[64,1024]{1,0:T(8,128)(2,1)S(1)}, bf16[64,1024]{1,0:T(8,128)(2,1)S(1)}, u32[]{:S(2)}, u32[]{:S(2)}) collective-permute-start(bf16[64,1024]{1,0:T(8,128)(2,1)S(1)} %collective-permute-done.4.refs_2_), channel_id=1, source_target_pairs={{0,8},{8,0},{16,24},{24,16},{1,9},{9,1},{17,25},{25,17},{2,10},{10... | collective-permute-start | bytes 393224 | tf_op jit(solution)/shard_map/ppermute | solution.py:24
  10.9 1.5 %collective-permute-done.more_times_ref = f32[8,128]{1,0:T(8,128)S(1)} collective-permute-done((f32[8,128]{1,0:T(8,128)S(1)}, f32[8,128]{1,0:T(8,128)S(1)}, u32[]{:S(2)}, u32[]{:S(2)}) %collective-permute-start) | collective-permute-done | bytes 4128 | tf_op jit(solution)/shard_map/ppermute | solution.py:24
  12.4 0.0 collective-permute-done.1.block_ref
  12.4 0.1 scale.1.scaled_ref
  12.5 0.0 collective-permute-done.5.refs_1_
  12.5 0.0 collective-permute-done.6.refs_3_
  12.5 0.5 %far.1 = f32[32,128]{1,0:T(8,128)S(1)} custom-call(f32[8,128]{1,0:T(8,128)S(1)} %get-tuple-element.10.times_ref, f32[8,128]{1,0:T(8,128)S(1)} %collective-permute-done.more_times_ref, bf16[192,896]{1,0:T(8,128)(2,1)S(1)} %scale.1.scaled_ref, bf16[96,1024]{1,0:T(8,128)(2,1)S(1)} %join.1.refs_0_, bf16[32,1024]{1,0:T(8,128)(2,1)S(1)} %collective-permute-done.5.refs_1_, ...), custom_call_target="tpu_custom_call" | custom-call | flops 1000000000 | bytes 1000000 | tf_op jit(solution)/shard_map/far/pallas_call | solution.py:138
  13.0 2.2 %collective-permute-start.7 = (f32[32,128]{1,0:T(8,128)S(1)}, f32[32,128]{1,0:T(8,128)S(1)}, u32[]{:S(2)}, u32[]{:S(2)}) collective-permute-start(f32[32,128]{1,0:T(8,128)S(1)} %far.1), channel_id=1, source_target_pairs={{0,4},{2,6},{4,0},{6,2},{1,5},{3,7},{5,1},{7,3},{8,12},{10,14},{12... | collective-permute-start | bytes 49160 | tf_op jit(solution)/shard_map/ppermute | solution.py:24
  15.2 0.5 %own.1 = f32[32,128]{1,0:T(8,128)S(1)} custom-call(bf16[32,1024]{1,0:T(8,128)(2,1)S(1)} %get-tuple-element.11.refs_0_.block_ref, f32[8,128]{1,0:T(8,128)S(1)} %get-tuple-element.10.times_ref, f32[8,128]{1,0:T(8,128)S(1)} %collective-permute-done.more_times_ref, f32[1,896]{1,0:T(1,128)S(1)} %get-tuple-element.12.energy_ref, ...), custom_call_target="tpu_custom_call" | custom-call | flops 1000000000 | bytes 1000000 | tf_op jit(solution)/shard_map/own/pallas_call | solution.py:138
  15.6 2.1 %collective-permute-done.7 = f32[32,128]{1,0:T(8,128)S(1)} collective-permute-done((f32[32,128]{1,0:T(8,128)S(1)}, f32[32,128]{1,0:T(8,128)S(1)}, u32[]{:S(2)}, u32[]{:S(2)}) %collective-permute-start.7) | collective-permute-done | bytes 16416 | tf_op jit(solution)/shard_map/ppermute | solution.py:24
  17.7 0.6 %add.3 = f32[32,128]{1,0:T(8,128)} add(f32[32,128]{1,0:T(8,128)S(1)} %collective-permute-done.7, f32[32,128]{1,0:T(8,128)S(1)} %own.1) | non-fusion elementwise | flops 4096 | bytes 49152 | tf_op jit(solution)/shard_map/add | solution.py:231
  (2 shorter events, 0.0 us)
Async XLA Ops:
  1.6 4.1 %collective-permute-start.2 = (bf16[32,1024]{1,0:T(8,128)(2,1)S(1)}, bf16[32,1024]{1,0:T(8,128)(2,1)S(1)}, u32[]{:S(2)}, u32[]{:S(2)}) collective-permute-start(bf16[32,1024]{1,0:T(8,128)(2,1)S(1)} %get-tuple-element.11.refs_0_.block_ref), channel_id=1, source_target_pairs={{0,8},{8,0},{16,24},{24,16},{1,9},{9,1},{17,25},{25,17},{2,10},{10... | collective-permute-start | bytes 196616 | tf_op jit(solution)/shard_map/ppermute | solution.py:24
  2.1 8.2 %collective-permute-start.3 = (bf16[32,1024]{1,0:T(8,128)(2,1)S(1)}, bf16[32,1024]{1,0:T(8,128)(2,1)S(1)}, u32[]{:S(2)}, u32[]{:S(2)}) collective-permute-start(bf16[32,1024]{1,0:T(8,128)(2,1)S(1)} %get-tuple-element.11.refs_0_.block_ref), channel_id=1, source_target_pairs={{0,18},{2,16},{4,22},{6,20},{8,26},{10,24},{12,30},{14,28},{16,2},... | collective-permute-start | bytes 196616 | tf_op jit(solution)/shard_map/ppermute | solution.py:198
  5.7 5.0 %collective-permute-start.4 = (bf16[64,1024]{1,0:T(8,128)(2,1)S(1)}, bf16[64,1024]{1,0:T(8,128)(2,1)S(1)}, u32[]{:S(2)}, u32[]{:S(2)}) collective-permute-start(bf16[64,1024]{1,0:T(8,128)(2,1)S(1)} %pad_maximum_fusion), channel_id=1, source_target_pairs={{0,16},{2,18},{4,6},{6,4},{8,10},{10,8},{12,28},{14,30},{16,0},{18... | collective-permute-start | bytes 393224 | tf_op jit(solution)/shard_map/ppermute | solution.py:200
  6.3 6.1 %collective-permute-start.1 = (bf16[32,1024]{1,0:T(8,128)(2,1)S(1)}, bf16[32,1024]{1,0:T(8,128)(2,1)S(1)}, u32[]{:S(2)}, u32[]{:S(2)}) collective-permute-start(bf16[32,1024]{1,0:T(8,128)(2,1)S(1)} %get-tuple-element.11.refs_0_.block_ref), channel_id=1, source_target_pairs={{0,4},{2,6},{4,0},{6,2},{1,5},{3,7},{5,1},{7,3},{8,12},{10,14},{12... | collective-permute-start | bytes 196616 | tf_op jit(solution)/shard_map/ppermute | solution.py:24
  8.8 3.6 %collective-permute-start = (f32[8,128]{1,0:T(8,128)S(1)}, f32[8,128]{1,0:T(8,128)S(1)}, u32[]{:S(2)}, u32[]{:S(2)}) collective-permute-start(f32[8,128]{1,0:T(8,128)S(1)} %get-tuple-element.10.times_ref), channel_id=1, source_target_pairs={{0,1},{1,0},{2,3},{3,2},{4,5},{5,4},{6,7},{7,6},{8,9},{9,8},{10,11... | collective-permute-start | bytes 12296 | tf_op jit(solution)/shard_map/ppermute | solution.py:24
  10.3 2.2 %collective-permute-start.5 = (bf16[32,1024]{1,0:T(8,128)(2,1)S(1)}, bf16[32,1024]{1,0:T(8,128)(2,1)S(1)}, u32[]{:S(2)}, u32[]{:S(2)}) collective-permute-start(bf16[32,1024]{1,0:T(8,128)(2,1)S(1)} %collective-permute-done.3.refs_2_), channel_id=1, source_target_pairs={{0,8},{8,0},{16,24},{24,16},{1,9},{9,1},{17,25},{25,17},{2,10},{10... | collective-permute-start | bytes 196616 | tf_op jit(solution)/shard_map/ppermute | solution.py:24
  10.7 1.8 %collective-permute-start.6 = (bf16[64,1024]{1,0:T(8,128)(2,1)S(1)}, bf16[64,1024]{1,0:T(8,128)(2,1)S(1)}, u32[]{:S(2)}, u32[]{:S(2)}) collective-permute-start(bf16[64,1024]{1,0:T(8,128)(2,1)S(1)} %collective-permute-done.4.refs_2_), channel_id=1, source_target_pairs={{0,8},{8,0},{16,24},{24,16},{1,9},{9,1},{17,25},{25,17},{2,10},{10... | collective-permute-start | bytes 393224 | tf_op jit(solution)/shard_map/ppermute | solution.py:24
  13.0 4.7 %collective-permute-start.7 = (f32[32,128]{1,0:T(8,128)S(1)}, f32[32,128]{1,0:T(8,128)S(1)}, u32[]{:S(2)}, u32[]{:S(2)}) collective-permute-start(f32[32,128]{1,0:T(8,128)S(1)} %far.1), channel_id=1, source_target_pairs={{0,4},{2,6},{4,0},{6,2},{1,5},{3,7},{5,1},{7,3},{8,12},{10,14},{12... | collective-permute-start | bytes 49160 | tf_op jit(solution)/shard_map/ppermute | solution.py:24
